TPU v7x, 32 devices: a whole 2x2x4 slice. The times are simulated.
32 devices in a mesh: groups: 2 (over y), ep: 4 (over z), hd: 4 (over x, core).
Axes of the slice: x: 2, y: 2, z: 4, core: 2. Of those that a mesh axis runs over, the one named last changes fastest.
Arguments:
- residual: bfloat16 [64, 4096], P(('groups', 'ep'), 'hd'), parts along dimension 0, may hold values from -13 to 13
- queries: bfloat16 [64, 8192], P(('groups', 'ep'), 'hd'), parts along dimension 0, may hold values from -90 to 90
- key_value_cache: bfloat16 [64, 256, 2, 512], P(('groups', 'ep'), None, None, 'hd'), parts along dimension 0, may hold values from -4.5 to 4.5
- lengths: int32 [64], P(('groups', 'ep')), parts along dimension 0, may hold values from 2 to 256, as said below
- slot_of: int32 [64], P('groups'), parts along dimension 0, may hold values from 0 to 31, each once
- out_weight: bfloat16 [8192, 4096], P('hd', 'ep'), may hold values from -0.5 to 0.5
- expert_ids: int32 [64, 8], P(('groups', 'ep')), parts along dimension 0, may hold values from 0 to 63, all different within a row; in each aligned block of 8 rows (0 to 7, 8 to 15, ...) at most 2 rows name the same one
- route_weight: float32 [64, 8], P(('groups', 'ep')), parts along dimension 0, may hold values from 0.05 to 0.3
- in_weight: bfloat16 [64, 4096, 768], P('ep', None, 'hd'), may hold values from -0.09375 to 0.09375
- down_weight: bfloat16 [64, 768, 4096], P('ep', 'hd'), may hold values from -0.21875 to 0.21875
Outputs:
- layer_out: bfloat16 [64, 4096], P(('groups', 'ep'), 'hd'), parts along dimension 0
There are 2 independent parts, one for each index of `groups`. A program takes and returns all parts, laid end to end along the dimension named above; an argument that names none is the same for every part. Nothing has to cross between parts.
Inputs may be any that keep to these rules, and one draw needn't show every extreme that they name: `expert_ids`: among the rows of one device, at most 2 name the same expert; some expert is named by exactly 2 of them. A permutation: request r's cache sits in slot slot_of[r]. Slot s's cache is filled in its first lengths[s] positions; some slot is full.
All inputs are finite; a program needn't handle non-finite values.
Results may differ from a plain program's by a relative error of at most 0.0043.
The roundings to bfloat16 on the way count: a program that leaves them out, or rounds other values in their place, can miss the bound.
Values may be sent and summed in bfloat16 or wider, within the bound.
No kernel may reach another device: no remote copies, remote signals or barrier semaphores. Data moves between devices by JAX's collectives and lax.ppermute only.
A program may use at most 128 MiB of HBM per device.

v0:
```python
import math

import jax
import jax.numpy as jnp
from jax import lax
from jax.sharding import PartitionSpec as P

D = 4096
QUERY_HEADS = 64
KEY_VALUE_HEADS = 4
HEAD_SIZE = 128
EXPERTS = 64
TOPK = 8
CAP = 2
CACHE_LENGTH = 256


def expert_pass(block, in_weight, down_weight):
    local_count = in_weight.shape[0]
    senders = block.shape[0] // local_count
    slots = block.shape[1]
    width = block.shape[2]
    grouped = block.reshape(senders, local_count, slots, width)
    hidden = jnp.einsum("secd,edf->secf", grouped, in_weight, preferred_element_type=jnp.float32)
    hidden = jax.nn.silu(hidden).astype(jnp.bfloat16)
    output = jnp.einsum("secf,efd->secd", hidden, down_weight, preferred_element_type=jnp.float32)
    return output.reshape(senders * local_count, slots, width)


def body(
    residual,
    queries,
    key_value_cache,
    lengths,
    slot_of,
    out_weight,
    expert_ids,
    route_weight,
    in_weight,
    down_weight,
):
    rows_here = queries.shape[0]
    local_groups = key_value_cache.shape[3] // HEAD_SIZE
    heads_per_group = QUERY_HEADS // KEY_VALUE_HEADS
    query_head_rows = queries.reshape(rows_here, local_groups, heads_per_group, HEAD_SIZE)
    cached_key_rows = key_value_cache[:, :, 0].reshape(
        rows_here, CACHE_LENGTH, local_groups, HEAD_SIZE
    )
    cached_value_rows = key_value_cache[:, :, 1].reshape(
        rows_here, CACHE_LENGTH, local_groups, HEAD_SIZE
    )
    scores = jnp.einsum(
        "sagd,slad->sagl", query_head_rows, cached_key_rows, preferred_element_type=jnp.float32
    )
    scores = scores * (1.0 / math.sqrt(HEAD_SIZE))
    visible = (jnp.arange(CACHE_LENGTH)[None, :] < lengths[:, None])[:, None, None, :]
    scores = jnp.where(visible, scores, -1e30)
    highest = jnp.max(scores, axis=3, keepdims=True)
    raised = jnp.where(visible, jnp.exp(scores - highest), 0.0)
    weights = (raised / jnp.sum(raised, axis=3, keepdims=True)).astype(jnp.bfloat16)
    attended = jnp.einsum(
        "sagl,slad->sagd", weights, cached_value_rows, preferred_element_type=jnp.float32
    )
    attended = attended.astype(jnp.bfloat16).reshape(
        rows_here, local_groups * heads_per_group * HEAD_SIZE
    )
    partial_value = jnp.dot(
        lax.all_gather(attended, "ep", axis=0, tiled=True),
        out_weight,
        preferred_element_type=jnp.float32,
    )
    ordered = jnp.take(partial_value, slot_of, axis=0)
    moved = lax.all_to_all(ordered, "ep", split_axis=0, concat_axis=1, tiled=True)
    summed = lax.psum_scatter(moved, "hd", scatter_dimension=1, tiled=True)
    stream = residual.astype(jnp.float32) + summed
    squares = lax.psum(jnp.sum(stream * stream, axis=1), "hd")
    normed = (stream * lax.rsqrt(squares / D + 1e-06)[:, None]).astype(jnp.bfloat16)
    picked = expert_ids.reshape(-1)
    member = (picked[:, None] == jnp.arange(EXPERTS)[None, :]).astype(jnp.int32)
    earlier = jnp.cumsum(member, axis=0) - member
    position = jnp.sum(earlier * member, axis=1)
    target = picked * CAP + position
    placed = (target[:, None] == jnp.arange(EXPERTS * CAP)[None, :]).astype(jnp.float32)
    owner = (jnp.arange(picked.shape[0])[:, None] // TOPK == jnp.arange(rows_here)[None, :]).astype(
        jnp.float32
    )
    select_matrix = jnp.dot(placed.T, owner, precision=lax.Precision.HIGHEST).astype(jnp.bfloat16)
    mixing = jnp.dot(
        owner.T, placed * route_weight.reshape(-1)[:, None], precision=lax.Precision.HIGHEST
    )
    full_rows = lax.all_gather(normed, "hd", axis=1, tiled=True)
    outgoing = jnp.dot(select_matrix, full_rows, preferred_element_type=jnp.float32).astype(
        jnp.bfloat16
    )
    outgoing = outgoing.reshape(EXPERTS, CAP, full_rows.shape[1])
    results = expert_pass(
        lax.all_to_all(outgoing, "ep", split_axis=0, concat_axis=0, tiled=True),
        in_weight,
        down_weight,
    )
    share_width = residual.shape[1]
    shares = lax.psum_scatter(results.astype(jnp.bfloat16), "hd", scatter_dimension=2, tiled=True)
    returned = lax.all_to_all(shares, "ep", split_axis=0, concat_axis=0, tiled=True)
    flat_back = returned.reshape(EXPERTS * CAP, share_width).astype(jnp.float32)
    mixture = jnp.dot(mixing, flat_back, precision=lax.Precision.HIGHEST)
    return (stream + mixture).astype(jnp.bfloat16)


def solution(mesh):
    in_specs = (
        P(("groups", "ep"), "hd"),
        P(("groups", "ep"), "hd"),
        P(("groups", "ep"), None, None, "hd"),
        P(("groups", "ep")),
        P("groups"),
        P("hd", "ep"),
        P(("groups", "ep"), None),
        P(("groups", "ep"), None),
        P("ep", None, "hd"),
        P("ep", "hd", None),
    )
    out_specs = P(("groups", "ep"), "hd")
    return jax.shard_map(body, mesh=mesh, in_specs=in_specs, out_specs=out_specs, check_vma=False)
```

profile of v0, /device:TPU:0, one launch (start us, length us, event | category | flops | bytes accessed | tf_op | source)
XLA Modules:
  0.0 175.8 jit_solution(16582425023631153865)
XLA Ops:
  6.5 0.7 compare_select_fusion
  7.2 0.7 compare_and_fusion
  7.9 3.3 %fusion.48 = (bf16[8,256,1,128]{3,2,1,0:T(2,128)(2,1)S(1)}, bf16[8,256,1,128]{3,2,1,0:T(2,128)(2,1)S(1)}) fusion(bf16[8,256,2,128]{3,2,1,0:T(2,128)(2,1)} %param.12), kind=kLoop, calls=%fused_computation.59 | loop fusion | bytes 2097152 | tf_op jit(solution)/shard_map/slice | solution.py:46
  11.2 0.7 iota_compare_fusion.7
  11.9 1.2 fusion.49
  13.1 0.3 fusion.18
  13.3 15.1 %all_gather.6 = bf16[32,2048]{1,0:T(8,128)(2,1)S(1)} all-gather(bf16[8,2048]{1,0:T(8,128)(2,1)S(1)} %bitcast.62), channel_id=1, replica_groups=mesh['groups'=2,'ep'=4,'hd'=4] {'ep'}, dimensions={0}, use_global_device_ids=true | all-gather | bytes 163840 | tf_op jit(solution)/shard_map/all_gather | solution.py:68
  28.4 0.1 broadcast_in_dim.43
  28.5 3.0 %fusion.52 = f32[32,1024]{1,0:T(8,128)S(1)} fusion(bf16[32,2048]{1,0:T(8,128)(2,1)S(1)} %all_gather.6, bf16[2048,1024]{1,0:T(8,128)(2,1)} %param.15), kind=kOutput, calls=%fused_computation.61 | convolution fusion | flops 134217728 | bytes 4456448 | tf_op jit(solution)/shard_map/dot_general | solution.py:67
  31.5 0.6 gather_fusion
  32.1 0.7 bitcast_select_fusion
  32.9 5.0 %all-to-all-start = ((f32[4,8,1024]{2,1,0:T(8,128)}), f32[4,8,1024]{2,1,0:T(8,128)S(1)}, u32[]{:S(2)}, u32[]{:S(2)}) async-start(f32[4,8,1024]{2,1,0:T(8,128)} %bitcast_select_fusion), calls=%async_computation | async-start | bytes 262144 | tf_op jit(solution)/shard_map/all_to_all | solution.py:73
  37.8 0.0 reduce-scatter.3.cloned.1.call-start
  37.8 0.8 reshape.136
  38.6 0.1 fusion.39
  38.7 0.1 reduce_window_sum.11
  38.8 5.0 %all-to-all-done = f32[4,8,1024]{2,1,0:T(8,128)S(1)} async-done(((f32[4,8,1024]{2,1,0:T(8,128)}), f32[4,8,1024]{2,1,0:T(8,128)S(1)}, u32[]{:S(2)}, u32[]{:S(2)}) %all-to-all-start) | async-done | bytes 131104 | tf_op jit(solution)/shard_map/all_to_all | solution.py:73
  43.7 0.0 copy-start
  43.7 0.6 copy-done
  44.4 0.0 reduce-scatter.3.cloned.1.call-update
  44.4 0.0 reduce-scatter.5.cloned.1.call-start
  44.5 0.2 select_reduce_fusion
  44.6 18.6 %reduce-scatter.3.cloned.1.call-done = f32[8,1024]{1,0:T(8,128)} async-done(((f32[8,4096]{1,0:T(8,128)}), f32[8,1024]{1,0:T(8,128)}) %reduce-scatter.3.cloned.1.call-update) | async-done | bytes 32784 | tf_op jit(solution)/shard_map/reduce_scatter | solution.py:74
  63.2 0.9 multiply_reduce_fusion
  64.1 0.3 convolution_convert_fusion.2
  64.3 5.7 %psum.7 = f32[8]{0:T(128)S(1)} all-reduce(f32[8]{0:T(128)S(1)} %multiply_reduce_fusion), channel_id=1, replica_groups=mesh['groups'=2,'ep'=4,'hd'=4] {'hd'}, use_global_device_ids=true, to_apply=%region_6.7 | all-reduce | flops 8 | bytes 64 | tf_op jit(solution)/shard_map/psum | solution.py:76
  70.1 0.8 multiply_convert_fusion
  70.9 5.2 %all_gather.7 = bf16[8,4096]{1,0:T(8,128)(2,1)S(1)} all-gather(bf16[8,1024]{1,0:T(8,128)(2,1)S(1)} %multiply_convert_fusion), channel_id=1, replica_groups=mesh['groups'=2,'ep'=4,'hd'=4] {'hd'}, dimensions={1}, use_global_device_ids=true | all-gather | bytes 81920 | tf_op jit(solution)/shard_map/all_gather | solution.py:91
  76.1 0.5 convolution_convert_fusion
  76.6 0.7 reshape.137
  77.3 30.8 %all_to_all.26 = bf16[64,2,4096]{2,1,0:T(2,128)(2,1)S(1)} all-to-all(bf16[64,2,4096]{2,1,0:T(2,128)(2,1)S(1)} %reshape.137), channel_id=1, replica_groups=mesh['groups'=2,'ep'=4,'hd'=4] {'ep'}, dimensions={0} | all-to-all | bytes 2097152 | tf_op jit(solution)/shard_map/all_to_all | solution.py:97
  108.2 0.0 copy-start.3
  108.2 0.0 copy-start.1
  108.2 0.0 copy-start.2
  108.2 19.5 %fusion.8 = bf16[4,16,2,4096]{3,0,2,1:T(4,128)(2,1)S(1)} fusion(bf16[16,192,4096]{2,1,0:T(8,128)(2,1)} %param.19, bf16[16,4096,192]{1,2,0:T(8,128)(2,1)} %param.18, bf16[4,16,2,4096]{3,2,1,0:T(2,128)(2,1)S(1)} %bitcast.59), kind=kOutput, calls=%fused_computation.8 | convolution fusion | flops 403300352 | bytes 52428800 | tf_op jit(solution)/shard_map/secf,efd->secd/dot_general | solution.py:26
  127.7 1.6 copy.32
  129.3 0.0 reduce-scatter.5.cloned.1.call-update
  129.3 23.3 %reduce-scatter.5.cloned.1.call-done = bf16[64,2,1024]{2,0,1:T(8,128)(2,1)} async-done(((bf16[64,2,4096]{2,0,1:T(8,128)(2,1)}), bf16[64,2,1024]{2,0,1:T(8,128)(2,1)}) %reduce-scatter.5.cloned.1.call-update) | async-done | bytes 262160 | tf_op jit(solution)/shard_map/reduce_scatter | solution.py:102
  152.6 1.9 %copy.33 = bf16[64,2,1024]{2,1,0:T(2,128)(2,1)} copy(bf16[64,2,1024]{2,0,1:T(8,128)(2,1)} %reduce-scatter.5.cloned.1.call-done) | data formatting | bytes 524288 | tf_op jit(solution)/shard_map/reduce_scatter | solution.py:102
  154.5 4.6 %all-to-all-start.2 = ((bf16[64,2,1024]{2,1,0:T(2,128)(2,1)}), bf16[64,2,1024]{2,1,0:T(2,128)(2,1)S(1)}, u32[]{:S(2)}, u32[]{:S(2)}) async-start(bf16[64,2,1024]{2,1,0:T(2,128)(2,1)} %copy.33), calls=%async_computation.4 | async-start | bytes 524288 | tf_op jit(solution)/shard_map/all_to_all | solution.py:103
  159.1 0.0 copy-done.3
  159.1 0.1 mul.50
  159.2 0.3 fusion.37
  159.4 8.6 %all-to-all-done.2 = bf16[64,2,1024]{2,1,0:T(2,128)(2,1)S(1)} async-done(((bf16[64,2,1024]{2,1,0:T(2,128)(2,1)}), bf16[64,2,1024]{2,1,0:T(2,128)(2,1)S(1)}, u32[]{:S(2)}, u32[]{:S(2)}) %all-to-all-start.2) | async-done | bytes 262176 | tf_op jit(solution)/shard_map/all_to_all | solution.py:103
  168.0 0.1 reshape.139
  168.1 0.0 copy-done.1
  168.1 0.0 copy-done.2
  168.1 0.8 fusion.19
  (4 shorter events, 0.0 us)
Async XLA Ops:
  32.9 10.9 %all-to-all-start = ((f32[4,8,1024]{2,1,0:T(8,128)}), f32[4,8,1024]{2,1,0:T(8,128)S(1)}, u32[]{:S(2)}, u32[]{:S(2)}) async-start(f32[4,8,1024]{2,1,0:T(8,128)} %bitcast_select_fusion), calls=%async_computation | async-start | bytes 262144 | tf_op jit(solution)/shard_map/all_to_all | solution.py:73
  37.8 25.4 %reduce-scatter.3.cloned.1.call-start = ((), (), s32[]{:S(2)}) async-start(), calls=%async_computation.5 | async-start | bytes 163840 | tf_op jit(solution)/shard_map/reduce_scatter | solution.py:74
  43.7 0.6 copy-start
  44.4 108.1 %reduce-scatter.5.cloned.1.call-start = ((), (), s32[]{:S(2)}) async-start(), calls=%async_computation.6 | async-start | bytes 1310720 | tf_op jit(solution)/shard_map/reduce_scatter | solution.py:102
  108.2 50.9 %copy-start.3 = (f32[8,8]{1,0:T(8,128)S(1)}, f32[8,8]{1,0:T(8,128)}, u32[]{:S(2)}) copy-start(f32[8,8]{1,0:T(8,128)} %param.17) | copy-start | bytes 772
  108.2 60.0 %copy-start.1 = (f32[8,1024]{1,0:T(8,128)S(1)}, f32[8,1024]{1,0:T(8,128)}, u32[]{:S(2)}) copy-start(f32[8,1024]{1,0:T(8,128)} %reduce-scatter.3.cloned.1.call-done) | copy-start | bytes 98308
  108.2 60.0 %copy-start.2 = (bf16[8,1024]{1,0:T(8,128)(2,1)S(1)}, bf16[8,1024]{1,0:T(8,128)(2,1)}, u32[]{:S(2)}) copy-start(bf16[8,1024]{1,0:T(8,128)(2,1)} %param.10) | copy-start | bytes 49156
  154.5 13.5 %all-to-all-start.2 = ((bf16[64,2,1024]{2,1,0:T(2,128)(2,1)}), bf16[64,2,1024]{2,1,0:T(2,128)(2,1)S(1)}, u32[]{:S(2)}, u32[]{:S(2)}) async-start(bf16[64,2,1024]{2,1,0:T(2,128)(2,1)} %copy.33), calls=%async_computation.4 | async-start | bytes 524288 | tf_op jit(solution)/shard_map/all_to_all | solution.py:103
Sparse Core Ops, SparseCore 0:
  44.5 18.6 reduce-scatter.2
  129.4 23.1 reduce-scatter.4
where the time goes:
time: 177 us; the launch traced here: 176 us
  blocking collectives  56.9 us (32%)
  waiting for transfers between devices  55.4 us (31%)
  matrix products  25.8 us (15%)
  between operations  13.5 us (8%)
  local copies, waits for them, and re-layouts  9.82 us (6%)
  starting transfers between devices  9.62 us (5%)
  other arithmetic  4.85 us (3%)
    all_to_all x1, blocking collectives, body(): lax.all_to_all(outgoing, 'ep', split_axis=0, concat_axis=0, tiled=True)  30.8 us
    reduce_scatter x1, waiting for transfers between devices, body(): lax.psum_scatter(results.astype(jnp.bfloat16), 'hd', scatter_dimension=2,...  23.3 us
    dot_general x1, matrix products, expert_pass(): jnp.einsum('secf,efd->secd', hidden, down_weight, preferred_element_type=...  19.5 us
    reduce_scatter x1, waiting for transfers between devices, body(): summed = lax.psum_scatter(moved, 'hd', scatter_dimension=1, tiled=True)  18.6 us
    all_gather x1, blocking collectives, body(): lax.all_gather(attended, 'ep', axis=0, tiled=True)  15.1 us
    all_to_all x1, waiting for transfers between devices, body(): lax.all_to_all(shares, 'ep', split_axis=0, concat_axis=0, tiled=True)  8.59 us
    psum x1, blocking collectives, body(): squares = lax.psum(jnp.sum(stream * stream, axis=1), 'hd')  5.73 us
    all_gather x1, blocking collectives, body(): full_rows = lax.all_gather(normed, 'hd', axis=1, tiled=True)  5.23 us
  transfers between devices with their start and end apart: 4, of which 4 were waited for; matrix products, arithmetic and copies ran while one was open for 1% of the time, Pallas kernels for 0%

commit v1 on v0

--- a/solution.py
+++ b/solution.py
@@ -1,8 +1,11 @@
+import functools
 import math
 
 import jax
 import jax.numpy as jnp
 from jax import lax
+from jax.experimental import pallas as pl
+from jax.experimental.pallas import tpu as pltpu
 from jax.sharding import PartitionSpec as P
 
 D = 4096
@@ -13,6 +16,262 @@
 TOPK = 8
 CAP = 2
 CACHE_LENGTH = 256
+BF16 = jnp.bfloat16
+F32 = jnp.float32
+MIB = 1 << 20
+VMEM_SPEC = pl.BlockSpec(memory_space=pltpu.VMEM)
+SMEM_SPEC = pl.BlockSpec(memory_space=pltpu.SMEM)
+
+
+def swap(block, axis, k, n):
+    return lax.ppermute(block, axis, [(i, i ^ k) for i in range(n)])
+
+
+def attention_kernel(lengths, queries, cache, ids, route, out, staged, gathered):
+    rows = queries.shape[0]
+    heads = queries.shape[1] // HEAD_SIZE
+    for h in range(heads):
+        lanes = slice(h * HEAD_SIZE, (h + 1) * HEAD_SIZE)
+        staged[h * rows : (h + 1) * rows, :] = queries[:, lanes].astype(F32)
+    place = lax.broadcasted_iota(jnp.int32, (heads, 2 * CACHE_LENGTH), 1)
+    for s in range(rows):
+        mine = staged[pl.ds(s, heads, stride=rows), :].astype(BF16)
+        both = cache[s]
+        scores = lax.dot_general(
+            mine, both, (((1,), (1,)), ((), ())), preferred_element_type=F32
+        ) * (1.0 / math.sqrt(HEAD_SIZE))
+        visible = jnp.logical_and(place % 2 == 0, place < 2 * lengths[s])
+        scores = jnp.where(visible, scores, -1e30)
+        raised = jnp.where(visible, jnp.exp(scores - jnp.max(scores, axis=1, keepdims=True)), 0.0)
+        weights = raised / jnp.sum(raised, axis=1, keepdims=True)
+        moved = pltpu.roll(weights, 1, 1).astype(BF16)
+        gathered[pl.ds(s, heads, stride=rows), :] = jnp.dot(
+            moved, both, preferred_element_type=F32
+        )
+    for h in range(heads):
+        lanes = slice(h * HEAD_SIZE, (h + 1) * HEAD_SIZE)
+        out[:, lanes] = gathered[h * rows : (h + 1) * rows, :].astype(BF16)
+    weight = route[...]
+    high = weight.astype(BF16)
+    rest = weight - high.astype(F32)
+    middle = rest.astype(BF16)
+    low = (rest - middle.astype(F32)).astype(BF16)
+    row = lax.broadcasted_iota(jnp.int32, (TOPK, 128), 0)
+    lane = lax.broadcasted_iota(jnp.int32, (TOPK, 128), 1)
+    total = jnp.zeros((rows, 128), F32)
+    for j, part in enumerate((ids[...].astype(F32).astype(BF16), high, middle, low)):
+        spread = (lane == row + j * TOPK).astype(F32).astype(BF16)
+        total = total + jnp.dot(part, spread, preferred_element_type=F32)
+    out[:, heads * HEAD_SIZE :] = total.astype(BF16)
+
+
+def attention(lengths, queries, cache, ids, route):
+    rows, width = queries.shape
+    return pl.pallas_call(
+        attention_kernel,
+        out_shape=jax.ShapeDtypeStruct((rows, width + 128), BF16),
+        in_specs=[SMEM_SPEC] + [VMEM_SPEC] * 4,
+        out_specs=VMEM_SPEC,
+        scratch_shapes=[
+            pltpu.VMEM((rows * width // HEAD_SIZE, HEAD_SIZE), F32),
+            pltpu.VMEM((rows * width // HEAD_SIZE, HEAD_SIZE), F32),
+        ],
+        compiler_params=pltpu.CompilerParams(vmem_limit_bytes=6 * MIB),
+        cost_estimate=pl.CostEstimate(
+            flops=10_000_000, bytes_accessed=1_200_000, transcendentals=65536
+        ),
+        name="attention",
+    )(lengths, queries, cache, ids, route)
+
+
+def projection_kernel(n, slot_of, b0, b1, b2, b3, weight, out, routing):
+    blocks = (b0, b1, b2, b3)
+    rows = b0.shape[0]
+    width = b0.shape[1] - 128
+    everyone = n * rows
+    me = lax.axis_index("ep")
+    held = jnp.concatenate([b[:, :width].astype(F32) for b in blocks], axis=0).astype(BF16)
+    row = lax.broadcasted_iota(jnp.int32, (everyone, everyone), 0)
+    column = lax.broadcasted_iota(jnp.int32, (everyone, everyone), 1)
+    wanted = jnp.zeros((everyone, everyone), jnp.int32)
+    for r in range(everyone):
+        slot = slot_of[r]
+        wanted = jnp.where(row == r, ((slot // rows) ^ me) * rows + slot % rows, wanted)
+    order = (wanted == column).astype(F32).astype(BF16)
+    ordered = jnp.dot(order, held, preferred_element_type=F32).astype(BF16)
+    answer = jnp.dot(ordered, weight[...], preferred_element_type=F32)
+    for i in range(n):
+        out[i] = answer[i * rows : (i + 1) * rows, :]
+    for k, block in enumerate(blocks):
+        routing[pl.ds((me ^ k) * rows, rows), :] = block[:, width:].astype(F32)
+
+
+def projection(slot_of, blocks, weight):
+    n = len(blocks)
+    rows = blocks[0].shape[0]
+    return pl.pallas_call(
+        functools.partial(projection_kernel, n),
+        out_shape=(
+            jax.ShapeDtypeStruct((n, rows, weight.shape[1]), F32),
+            jax.ShapeDtypeStruct((n * rows, 128), F32),
+        ),
+        in_specs=[SMEM_SPEC] + [VMEM_SPEC] * 5,
+        out_specs=(VMEM_SPEC, VMEM_SPEC),
+        compiler_params=pltpu.CompilerParams(vmem_limit_bytes=8 * MIB),
+        cost_estimate=pl.CostEstimate(
+            flops=140_000_000, bytes_accessed=4_500_000, transcendentals=0
+        ),
+        name="projection",
+    )(slot_of, *blocks, weight)
+
+
+def norm_kernel(b0, b1, b2, b3, out):
+    blocks = (b0, b1, b2, b3)
+    me = lax.axis_index("ep")
+    width = b0.shape[1]
+    squares = 0.0
+    for block in blocks:
+        squares = squares + jnp.sum(block[...] * block[...], axis=1, keepdims=True)
+    scale = lax.rsqrt(squares / (width * len(blocks)) + 1e-06)
+    for k, block in enumerate(blocks):
+        start = pl.multiple_of((me ^ k) * width, width)
+        out[:, pl.ds(start, width)] = (block[...] * scale).astype(BF16)
+
+
+def norm(blocks):
+    rows, width = blocks[0].shape
+    return pl.pallas_call(
+        norm_kernel,
+        out_shape=jax.ShapeDtypeStruct((rows, width * len(blocks)), BF16),
+        in_specs=[VMEM_SPEC] * 4,
+        out_specs=VMEM_SPEC,
+        compiler_params=pltpu.CompilerParams(vmem_limit_bytes=4 * MIB),
+        cost_estimate=pl.CostEstimate(flops=100_000, bytes_accessed=200_000, transcendentals=8),
+        name="norm",
+    )(*blocks)
+
+
+def experts_kernel(rows_in, routing, entry, leave, o0, o1, o2, o3, total):
+    step = pl.program_id(0)
+    number = lax.axis_index("ep") * pl.num_programs(0) + step
+    table = routing[...]
+    lane = lax.broadcasted_iota(jnp.int32, table.shape, 1)
+    weight = pltpu.roll(table, 128 - TOPK, 1) + pltpu.roll(table, 128 - 2 * TOPK, 1)
+    weight = weight + pltpu.roll(table, 128 - 3 * TOPK, 1)
+    chosen = jnp.logical_and(lane < TOPK, table == number.astype(F32))
+    share = jnp.sum(jnp.where(chosen, weight, 0.0), axis=1, keepdims=True)
+    before = lax.dot_general(
+        rows_in[...], entry[0], (((1,), (1,)), ((), ())), preferred_element_type=F32
+    )
+    hidden = (before / (1.0 + jnp.exp(-before))).astype(BF16)
+    result = jnp.dot(hidden, leave[0], preferred_element_type=F32) * share
+
+    @pl.when(step == 0)
+    def _():
+        total[...] = result
+
+    @pl.when(step > 0)
+    def _():
+        total[...] += result
+
+    @pl.when(step == pl.num_programs(0) - 1)
+    def _():
+        me = lax.axis_index("hd")
+        for k, out in enumerate((o0, o1, o2, o3)):
+            width = out.shape[1]
+            start = pl.multiple_of((me ^ k) * width, width)
+            out[...] = total[:, pl.ds(start, width)].astype(out.dtype)
+
+
+def experts(rows_in, routing, entry, leave):
+    count, hidden, width = leave.shape
+    rows = rows_in.shape[0]
+    part = (rows, width // 4)
+    whole = lambda shape: pl.BlockSpec(shape, lambda i: (0, 0))
+    return pl.pallas_call(
+        experts_kernel,
+        grid=(count,),
+        out_shape=[jax.ShapeDtypeStruct(part, F32)] + [jax.ShapeDtypeStruct(part, BF16)] * 3,
+        in_specs=[
+            whole((rows, width)),
+            whole((rows, 128)),
+            pl.BlockSpec((1, hidden, width), lambda i: (i, 0, 0)),
+            pl.BlockSpec((1, hidden, width), lambda i: (i, 0, 0)),
+        ],
+        out_specs=[whole(part)] * 4,
+        scratch_shapes=[pltpu.VMEM((rows, width), F32)],
+        compiler_params=pltpu.CompilerParams(vmem_limit_bytes=24 * MIB),
+        cost_estimate=pl.CostEstimate(
+            flops=4 * rows * count * hidden * width,
+            bytes_accessed=4 * count * hidden * width,
+            transcendentals=rows * count * hidden,
+        ),
+        name="experts",
+    )(rows_in, routing, entry, leave)
+
+
+def gather_kernel(own, r1, r2, r3, o0, o1, o2, o3):
+    total = own[...] + r1[...].astype(F32) + r2[...].astype(F32) + r3[...].astype(F32)
+    rows = o0.shape[0]
+    me = lax.axis_index("ep")
+    scratch = total.reshape(4, rows, total.shape[1])
+    for k, out in enumerate((o0, o1, o2, o3)):
+        picked = jnp.zeros(out.shape, F32)
+        for i in range(4):
+            picked = jnp.where((me ^ k) == i, scratch[i], picked)
+        out[...] = picked.astype(out.dtype)
+
+
+def combine(own, received):
+    rows, width = own.shape
+    part = (rows // 4, width)
+    return pl.pallas_call(
+        gather_kernel,
+        out_shape=[jax.ShapeDtypeStruct(part, F32)] * 4,
+        in_specs=[VMEM_SPEC] * 4,
+        out_specs=[VMEM_SPEC] * 4,
+        compiler_params=pltpu.CompilerParams(vmem_limit_bytes=4 * MIB),
+        cost_estimate=pl.CostEstimate(flops=200_000, bytes_accessed=500_000, transcendentals=0),
+        name="combine",
+    )(own, *received)
+
+
+def square_body(
+    n,
+    residual,
+    queries,
+    key_value_cache,
+    lengths,
+    slot_of,
+    out_weight,
+    expert_ids,
+    route_weight,
+    in_weight,
+    down_weight,
+):
+    rows = queries.shape[0]
+    mirror = [(e * n + h, h * n + e) for e in range(n) for h in range(n)]
+    crossed = lax.ppermute(residual, ("ep", "hd"), mirror)
+    cache = key_value_cache.reshape(rows, 2 * CACHE_LENGTH, HEAD_SIZE)
+    attended = attention(lengths, queries, cache, expert_ids, route_weight)
+    blocks = [attended] + [swap(attended, "ep", k, n) for k in range(1, n)]
+    projected, routing = projection(slot_of, blocks, out_weight)
+    mine = lax.axis_index("hd")
+    pieces = [lax.dynamic_index_in_dim(projected, mine ^ k, 0, keepdims=False) for k in range(n)]
+    summed = pieces[0]
+    for k in range(1, n):
+        summed = summed + swap(pieces[k], "hd", k, n)
+    stream = crossed.astype(F32) + summed
+    returned = lax.ppermute(stream, ("ep", "hd"), mirror)
+    normed = norm([stream] + [swap(stream, "ep", k, n) for k in range(1, n)])
+    full_rows = lax.all_gather(normed, "hd", axis=0, tiled=True)
+    own, *others = experts(full_rows, routing, jnp.swapaxes(in_weight, 1, 2), down_weight)
+    received = [swap(block, "hd", k + 1, n) for k, block in enumerate(others)]
+    own, *others = combine(own, received)
+    total = returned + own
+    for k, block in enumerate(others):
+        total = total + swap(block, "ep", k + 1, n)
+    return total.astype(BF16)
 
 
 def expert_pass(block, in_weight, down_weight):
@@ -120,4 +379,5 @@
         P("ep", "hd", None),
     )
     out_specs = P(("groups", "ep"), "hd")
-    return jax.shard_map(body, mesh=mesh, in_specs=in_specs, out_specs=out_specs, check_vma=False)
+    chosen = functools.partial(square_body, 4) if mesh.shape["ep"] == mesh.shape["hd"] == 4 else body
+    return jax.shard_map(chosen, mesh=mesh, in_specs=in_specs, out_specs=out_specs, check_vma=False)

time: 177 us -> 92.4 us (0.52)
  blocking collectives: 56.9 us -> 5.79 us
  waiting for transfers between devices: 55.4 us -> 18 us
  Pallas kernels: 0 us -> 28.8 us
  matrix products: 25.8 us -> 0 us
  starting transfers between devices: 9.62 us -> 23.3 us
  between operations: 13.5 us -> 0.09 us
  local copies, waits for them, and re-layouts: 9.82 us -> 15 us
  other arithmetic: 4.85 us -> 0.63 us
    reduce_scatter x2 -> x0, waiting for transfers between devices: 41.8 us -> none  [the longest x1 23.3 us: body(): lax.psum_scatter(results.astype(jnp.bfloat16), 'hd', scatter_dimension=2,...]
    all_to_all x1 -> x0, blocking collectives: 30.8 us -> none  [body(): lax.all_to_all(outgoing, 'ep', split_axis=0, concat_axis=0, tiled=True)]
    pallas_call x0 -> x5, Pallas kernels: none -> 28.8 us  [the longest x1 23.2 us: experts(): pl.pallas_call(experts_kernel, grid=(count,), out_shape=[jax.ShapeDtypeSt...]
    dot_general x7 -> x0, matrix products: 24.6 us -> none  [the longest x1 19.5 us: expert_pass(): jnp.einsum('secf,efd->secd', hidden, down_weight, preferred_element_type=...]
    ppermute x0 -> x17, starting transfers between devices: none -> 23.3 us  [the longest x15 21.3 us: swap(): return lax.ppermute(block, axis, [(i, i ^ k) for i in range(n)])]
    ppermute x0 -> x17, waiting for transfers between devices: none -> 18 us  [the longest x15 18 us: swap(): return lax.ppermute(block, axis, [(i, i ^ k) for i in range(n)])]
    all_gather x2 -> x1, blocking collectives: 20.3 us -> 5.79 us  [square_body(): full_rows = lax.all_gather(normed, 'hd', axis=0, tiled=True)]
    unnamed x9 -> x16, local copies, waits for them, and re-layouts: 0.66 us -> 15 us
  transfers between devices with their start and end apart: 4 -> 17, of which waited for: 4 -> 9; matrix products, arithmetic and copies ran while one was open for 1% -> 0% of each run, Pallas kernels for 0% -> 0%
where the time goes in v1:
time: 92.4 us; the launch traced here: 91.6 us
  Pallas kernels  28.8 us (31%)
  starting transfers between devices  23.3 us (25%)
  waiting for transfers between devices  18 us (19%)
  local copies, waits for them, and re-layouts  15 us (16%)
  blocking collectives  5.79 us (6%)
    pallas_call x1, Pallas kernels, experts(): pl.pallas_call(experts_kernel, grid=(count,), out_shape=[jax.ShapeDtypeSt...  23.2 us
    ppermute x15, starting transfers between devices, swap(): return lax.ppermute(block, axis, [(i, i ^ k) for i in range(n)])  21.3 us
    ppermute x15, waiting for transfers between devices, swap(): return lax.ppermute(block, axis, [(i, i ^ k) for i in range(n)])  18 us
    unnamed x16, local copies, waits for them, and re-layouts  15 us
    all_gather x1, blocking collectives, square_body(): full_rows = lax.all_gather(normed, 'hd', axis=0, tiled=True)  5.79 us
    pallas_call x1, Pallas kernels, attention(): pl.pallas_call(attention_kernel, out_shape=jax.ShapeDtypeStruct((rows, wi...  3.84 us
  transfers between devices with their start and end apart: 17, of which 9 were waited for; matrix products, arithmetic and copies ran while one was open for 0% of the time, Pallas kernels for 0%

profile of v1, /device:TPU:0, one launch (start us, length us, event | category | flops | bytes accessed | tf_op | source)
XLA Modules:
  0.0 91.6 jit_solution(13124615082842465716)
XLA Ops:
  0.0 1.2 %copy-done.2 = bf16[8,256,2,128]{3,2,1,0:T(2,128)(2,1)S(1)} copy-done((bf16[8,256,2,128]{3,2,1,0:T(2,128)(2,1)S(1)}, bf16[8,256,2,128]{3,2,1,0:T(2,128)(2,1)}, u32[]{:S(2)}) %copy-start.2) | copy-done | bytes 1048600
  1.2 0.8 copy-done.3
  2.0 0.7 copy-done.4
  2.7 0.7 copy-done.5
  3.4 0.7 copy-done.6
  4.0 3.8 %attention.1.b0 = bf16[8,2176]{1,0:T(8,128)(2,1)S(1)} custom-call(s32[8]{0:T(128)S(1)} %copy-done.6, bf16[8,2048]{1,0:T(8,128)(2,1)S(1)} %copy-done.3, bf16[8,512,128]{2,1,0:T(8,128)(2,1)S(1)} %bitcast.17, s32[8,8]{1,0:T(8,128)S(1)} %copy-done.4, f32[8,8]{1,0:T(8,128)S(1)} %copy-done.5), custom_call_target="tpu_custom_call" | custom-call | flops 10000000 | bytes 1200000 | tf_op jit(solution)/shard_map/attention/pallas_call | solution.py:70
  7.9 5.1 %collective-permute-start.3 = (bf16[8,2176]{1,0:T(8,128)(2,1)S(1)}, bf16[8,2176]{1,0:T(8,128)(2,1)S(1)}, u32[]{:S(2)}, u32[]{:S(2)}) collective-permute-start(bf16[8,2176]{1,0:T(8,128)(2,1)S(1)} %attention.1.b0), channel_id=1, source_target_pairs={{0,12},{4,8},{8,4},{12,0},{1,13},{5,9},{9,5},{13,1},{2,14},{6,10},... | collective-permute-start | bytes 104456 | tf_op jit(solution)/shard_map/ppermute | solution.py:27
  13.0 0.0 collective-permute-start.2
  13.0 0.6 collective-permute-start.1
  13.6 1.3 %collective-permute-done.3.b3 = bf16[8,2176]{1,0:T(8,128)(2,1)S(1)} collective-permute-done((bf16[8,2176]{1,0:T(8,128)(2,1)S(1)}, bf16[8,2176]{1,0:T(8,128)(2,1)S(1)}, u32[]{:S(2)}, u32[]{:S(2)}) %collective-permute-start.3) | collective-permute-done | bytes 34848 | tf_op jit(solution)/shard_map/ppermute | solution.py:27
  14.9 2.9 %collective-permute-done.2.b2 = bf16[8,2176]{1,0:T(8,128)(2,1)S(1)} collective-permute-done((bf16[8,2176]{1,0:T(8,128)(2,1)S(1)}, bf16[8,2176]{1,0:T(8,128)(2,1)S(1)}, u32[]{:S(2)}, u32[]{:S(2)}) %collective-permute-start.2) | collective-permute-done | bytes 34848 | tf_op jit(solution)/shard_map/ppermute | solution.py:27
  17.8 0.0 collective-permute-done.1.b1
  17.8 2.2 %copy-done.1 = bf16[2048,1024]{1,0:T(8,128)(2,1)S(1)} copy-done((bf16[2048,1024]{1,0:T(8,128)(2,1)S(1)}, bf16[2048,1024]{1,0:T(8,128)(2,1)}, u32[]{:S(2)}) %copy-start.1) | copy-done | bytes 4194328
  20.0 0.7 copy-done.7
  20.7 1.6 %projection.1 = (f32[4,8,1024]{2,1,0:T(8,128)S(1)}, f32[32,128]{1,0:T(8,128)S(1)}) custom-call(s32[32]{0:T(128)S(1)} %copy-done.7, bf16[8,2176]{1,0:T(8,128)(2,1)S(1)} %attention.1.b0, bf16[8,2176]{1,0:T(8,128)(2,1)S(1)} %collective-permute-done.1.b1, bf16[8,2176]{1,0:T(8,128)(2,1)S(1)} %collective-permute-done.2.b2, ...), custom_call_target="tpu_custom_call" | custom-call | flops 140000000 | bytes 4500000 | tf_op jit(solution)/shard_map/projection/pallas_call | solution.py:112
  22.3 0.1 collective-permute-start.4
  22.4 1.6 %collective-permute-start.6 = (f32[8,1024]{1,0:T(8,128)S(1)}, f32[8,1024]{1,0:T(8,128)S(1)}, u32[]{:S(2)}, u32[]{:S(2)}) collective-permute-start(f32[8,1024]{1,0:T(8,128)S(1)} %get-tuple-element.26), channel_id=1, source_target_pairs={{0,3},{1,2},{2,1},{3,0},{4,7},{5,6},{6,5},{7,4},{8,11},{9,10},{10,... | collective-permute-start | bytes 98312 | tf_op jit(solution)/shard_map/ppermute | solution.py:27
  24.0 0.5 collective-permute-start.5
  24.5 1.4 %collective-permute-start = (bf16[8,1024]{1,0:T(8,128)(2,1)}, bf16[8,1024]{1,0:T(8,128)(2,1)S(1)}, u32[]{:S(2)}, u32[]{:S(2)}) collective-permute-start(bf16[8,1024]{1,0:T(8,128)(2,1)} %param.10), channel_id=1, source_target_pairs={{0,0},{1,4},{2,8},{3,12},{4,1},{5,5},{6,9},{7,13},{8,2},{9,6},{10,... | collective-permute-start | bytes 49160 | tf_op jit(solution)/shard_map/ppermute | solution.py:254
  25.9 0.0 collective-permute-done
  25.9 0.0 collective-permute-done.4
  25.9 0.0 collective-permute-done.6
  25.9 2.0 %collective-permute-done.5 = f32[8,1024]{1,0:T(8,128)S(1)} collective-permute-done((f32[8,1024]{1,0:T(8,128)S(1)}, f32[8,1024]{1,0:T(8,128)S(1)}, u32[]{:S(2)}, u32[]{:S(2)}) %collective-permute-start.5) | collective-permute-done | bytes 32800 | tf_op jit(solution)/shard_map/ppermute | solution.py:27
  27.9 6.1 %collective-permute-start.10 = (f32[8,1024]{1,0:T(8,128)S(1)}, f32[8,1024]{1,0:T(8,128)S(1)}, u32[]{:S(2)}, u32[]{:S(2)}) collective-permute-start(f32[8,1024]{1,0:T(8,128)S(1)} %fusion.2.b0), channel_id=1, source_target_pairs={{0,12},{4,8},{8,4},{12,0},{1,13},{5,9},{9,5},{13,1},{2,14},{6,10},... | collective-permute-start | bytes 98312 | tf_op jit(solution)/shard_map/ppermute | solution.py:27
  34.0 0.3 collective-permute-start.9
  34.4 0.5 collective-permute-start.8
  34.8 1.3 %collective-permute-done.10.b3 = f32[8,1024]{1,0:T(8,128)S(1)} collective-permute-done((f32[8,1024]{1,0:T(8,128)S(1)}, f32[8,1024]{1,0:T(8,128)S(1)}, u32[]{:S(2)}, u32[]{:S(2)}) %collective-permute-start.10) | collective-permute-done | bytes 32800 | tf_op jit(solution)/shard_map/ppermute | solution.py:27
  36.2 3.0 %collective-permute-done.9.b2 = f32[8,1024]{1,0:T(8,128)S(1)} collective-permute-done((f32[8,1024]{1,0:T(8,128)S(1)}, f32[8,1024]{1,0:T(8,128)S(1)}, u32[]{:S(2)}, u32[]{:S(2)}) %collective-permute-start.9) | collective-permute-done | bytes 32800 | tf_op jit(solution)/shard_map/ppermute | solution.py:27
  39.2 0.0 collective-permute-done.8.b1
  39.2 0.1 norm.1
  39.3 5.8 %all_gather.3.rows_in = bf16[32,4096]{1,0:T(8,128)(2,1)S(1)} all-gather(bf16[8,4096]{1,0:T(8,128)(2,1)S(1)} %norm.1), channel_id=1, replica_groups=mesh['groups'=2,'ep'=4,'hd'=4] {'hd'}, dimensions={0}, use_global_device_ids=true | all-gather | bytes 327680 | tf_op jit(solution)/shard_map/all_gather | solution.py:267
  45.1 8.2 %copy-done = bf16[16,4096,192]{1,2,0:T(8,128)(2,1)S(1)} copy-done((bf16[16,4096,192]{1,2,0:T(8,128)(2,1)S(1)}, bf16[16,4096,192]{1,2,0:T(8,128)(2,1)}, u32[]{:S(2)}) %copy-start) | copy-done | bytes 25165848
  53.3 23.2 %experts.1 = (f32[32,1024]{1,0:T(8,128)S(1)}, bf16[32,1024]{1,0:T(8,128)(2,1)S(1)}, bf16[32,1024]{1,0:T(8,128)(2,1)S(1)}, bf16[32,1024]{1,0:T(8,128)(2,1)S(1)}) custom-call(bf16[32,4096]{1,0:T(8,128)(2,1)S(1)} %all_gather.3.rows_in, f32[32,128]{1,0:T(8,128)S(1)} %get-tuple-element.16.routing, bf16[16,192,4096]{2,1,0:T(8,128)(2,1)S(1)} %bitcast.16, ...), custom_call_target="tpu_custom_call" | custom-call | flops 1610612736 | bytes 50331648 | tf_op jit(solution)/shard_map/experts/pallas_call | solution.py:191
  76.4 0.4 collective-permute-start.11
  76.8 0.8 collective-permute-start.12
  77.7 0.7 collective-permute-start.13
  78.4 0.7 collective-permute-start.7
  79.0 2.5 %collective-permute-done.12.r2 = bf16[32,1024]{1,0:T(8,128)(2,1)S(1)} collective-permute-done((bf16[32,1024]{1,0:T(8,128)(2,1)S(1)}, bf16[32,1024]{1,0:T(8,128)(2,1)S(1)}, u32[]{:S(2)}, u32[]{:S(2)}) %collective-permute-start.12) | collective-permute-done | bytes 65568 | tf_op jit(solution)/shard_map/ppermute | solution.py:27
  81.6 0.5 collective-permute-done.13.r3
  82.1 0.1 combine.1
  82.1 2.1 %collective-permute-start.14 = (f32[8,1024]{1,0:T(8,128)S(1)}, f32[8,1024]{1,0:T(8,128)S(1)}, u32[]{:S(2)}, u32[]{:S(2)}) collective-permute-start(f32[8,1024]{1,0:T(8,128)S(1)} %get-tuple-element.22), channel_id=1, source_target_pairs={{0,4},{4,0},{8,12},{12,8},{1,5},{5,1},{9,13},{13,9},{2,6},{6,2},{1... | collective-permute-start | bytes 98312 | tf_op jit(solution)/shard_map/ppermute | solution.py:27
  84.2 1.1 %collective-permute-start.15 = (f32[8,1024]{1,0:T(8,128)S(1)}, f32[8,1024]{1,0:T(8,128)S(1)}, u32[]{:S(2)}, u32[]{:S(2)}) collective-permute-start(f32[8,1024]{1,0:T(8,128)S(1)} %get-tuple-element.23), channel_id=1, source_target_pairs={{0,8},{4,12},{8,0},{12,4},{1,9},{5,13},{9,1},{13,5},{2,10},{6,14},... | collective-permute-start | bytes 98312 | tf_op jit(solution)/shard_map/ppermute | solution.py:27
  85.3 1.3 %collective-permute-start.16 = (f32[8,1024]{1,0:T(8,128)S(1)}, f32[8,1024]{1,0:T(8,128)S(1)}, u32[]{:S(2)}, u32[]{:S(2)}) collective-permute-start(f32[8,1024]{1,0:T(8,128)S(1)} %get-tuple-element.24), channel_id=1, source_target_pairs={{0,12},{4,8},{8,4},{12,0},{1,13},{5,9},{9,5},{13,1},{2,14},{6,10},... | collective-permute-start | bytes 98312 | tf_op jit(solution)/shard_map/ppermute | solution.py:27
  86.6 0.0 collective-permute-done.7
  86.6 0.0 collective-permute-done.14
  86.6 2.6 %collective-permute-done.15 = f32[8,1024]{1,0:T(8,128)S(1)} collective-permute-done((f32[8,1024]{1,0:T(8,128)S(1)}, f32[8,1024]{1,0:T(8,128)S(1)}, u32[]{:S(2)}, u32[]{:S(2)}) %collective-permute-start.15) | collective-permute-done | bytes 32800 | tf_op jit(solution)/shard_map/ppermute | solution.py:27
  89.2 1.8 %collective-permute-done.16 = f32[8,1024]{1,0:T(8,128)S(1)} collective-permute-done((f32[8,1024]{1,0:T(8,128)S(1)}, f32[8,1024]{1,0:T(8,128)S(1)}, u32[]{:S(2)}, u32[]{:S(2)}) %collective-permute-start.16) | collective-permute-done | bytes 32800 | tf_op jit(solution)/shard_map/ppermute | solution.py:27
  91.0 0.6 add_convert_fusion
  (11 shorter events, 0.0 us)
Async XLA Ops:
  0.0 1.2 %copy-start.2 = (bf16[8,256,2,128]{3,2,1,0:T(2,128)(2,1)S(1)}, bf16[8,256,2,128]{3,2,1,0:T(2,128)(2,1)}, u32[]{:S(2)}) copy-start(bf16[8,256,2,128]{3,2,1,0:T(2,128)(2,1)} %param.12) | copy-start | bytes 3145732
  1.2 0.8 copy-start.3
  2.0 0.7 copy-start.4
  2.7 0.7 copy-start.5
  3.4 0.7 copy-start.6
  7.9 7.0 %collective-permute-start.3 = (bf16[8,2176]{1,0:T(8,128)(2,1)S(1)}, bf16[8,2176]{1,0:T(8,128)(2,1)S(1)}, u32[]{:S(2)}, u32[]{:S(2)}) collective-permute-start(bf16[8,2176]{1,0:T(8,128)(2,1)S(1)} %attention.1.b0), channel_id=1, source_target_pairs={{0,12},{4,8},{8,4},{12,0},{1,13},{5,9},{9,5},{13,1},{2,14},{6,10},... | collective-permute-start | bytes 104456 | tf_op jit(solution)/shard_map/ppermute | solution.py:27
  13.0 4.8 %collective-permute-start.2 = (bf16[8,2176]{1,0:T(8,128)(2,1)S(1)}, bf16[8,2176]{1,0:T(8,128)(2,1)S(1)}, u32[]{:S(2)}, u32[]{:S(2)}) collective-permute-start(bf16[8,2176]{1,0:T(8,128)(2,1)S(1)} %attention.1.b0), channel_id=1, source_target_pairs={{0,8},{4,12},{8,0},{12,4},{1,9},{5,13},{9,1},{13,5},{2,10},{6,14},... | collective-permute-start | bytes 104456 | tf_op jit(solution)/shard_map/ppermute | solution.py:27
  13.0 4.8 %collective-permute-start.1 = (bf16[8,2176]{1,0:T(8,128)(2,1)S(1)}, bf16[8,2176]{1,0:T(8,128)(2,1)S(1)}, u32[]{:S(2)}, u32[]{:S(2)}) collective-permute-start(bf16[8,2176]{1,0:T(8,128)(2,1)S(1)} %attention.1.b0), channel_id=1, source_target_pairs={{0,4},{4,0},{8,12},{12,8},{1,5},{5,1},{9,13},{13,9},{2,6},{6,2},{1... | collective-permute-start | bytes 104456 | tf_op jit(solution)/shard_map/ppermute | solution.py:27
  17.8 2.2 %copy-start.1 = (bf16[2048,1024]{1,0:T(8,128)(2,1)S(1)}, bf16[2048,1024]{1,0:T(8,128)(2,1)}, u32[]{:S(2)}) copy-start(bf16[2048,1024]{1,0:T(8,128)(2,1)} %weight.1) | copy-start | bytes 12582916
  20.0 0.7 copy-start.7
  22.3 3.6 %collective-permute-start.4 = (f32[8,1024]{1,0:T(8,128)S(1)}, f32[8,1024]{1,0:T(8,128)S(1)}, u32[]{:S(2)}, u32[]{:S(2)}) collective-permute-start(f32[8,1024]{1,0:T(8,128)S(1)} %get-tuple-element.25), channel_id=1, source_target_pairs={{0,1},{1,0},{2,3},{3,2},{4,5},{5,4},{6,7},{7,6},{8,9},{9,8},{10,11... | collective-permute-start | bytes 98312 | tf_op jit(solution)/shard_map/ppermute | solution.py:27
  22.4 3.5 %collective-permute-start.6 = (f32[8,1024]{1,0:T(8,128)S(1)}, f32[8,1024]{1,0:T(8,128)S(1)}, u32[]{:S(2)}, u32[]{:S(2)}) collective-permute-start(f32[8,1024]{1,0:T(8,128)S(1)} %get-tuple-element.26), channel_id=1, source_target_pairs={{0,3},{1,2},{2,1},{3,0},{4,7},{5,6},{6,5},{7,4},{8,11},{9,10},{10,... | collective-permute-start | bytes 98312 | tf_op jit(solution)/shard_map/ppermute | solution.py:27
  24.0 3.9 %collective-permute-start.5 = (f32[8,1024]{1,0:T(8,128)S(1)}, f32[8,1024]{1,0:T(8,128)S(1)}, u32[]{:S(2)}, u32[]{:S(2)}) collective-permute-start(f32[8,1024]{1,0:T(8,128)S(1)} %get-tuple-element.27), channel_id=1, source_target_pairs={{0,2},{1,3},{2,0},{3,1},{4,6},{5,7},{6,4},{7,5},{8,10},{9,11},{10,... | collective-permute-start | bytes 98312 | tf_op jit(solution)/shard_map/ppermute | solution.py:27
  24.5 1.4 %collective-permute-start = (bf16[8,1024]{1,0:T(8,128)(2,1)}, bf16[8,1024]{1,0:T(8,128)(2,1)S(1)}, u32[]{:S(2)}, u32[]{:S(2)}) collective-permute-start(bf16[8,1024]{1,0:T(8,128)(2,1)} %param.10), channel_id=1, source_target_pairs={{0,0},{1,4},{2,8},{3,12},{4,1},{5,5},{6,9},{7,13},{8,2},{9,6},{10,... | collective-permute-start | bytes 49160 | tf_op jit(solution)/shard_map/ppermute | solution.py:254
  27.9 8.2 %collective-permute-start.10 = (f32[8,1024]{1,0:T(8,128)S(1)}, f32[8,1024]{1,0:T(8,128)S(1)}, u32[]{:S(2)}, u32[]{:S(2)}) collective-permute-start(f32[8,1024]{1,0:T(8,128)S(1)} %fusion.2.b0), channel_id=1, source_target_pairs={{0,12},{4,8},{8,4},{12,0},{1,13},{5,9},{9,5},{13,1},{2,14},{6,10},... | collective-permute-start | bytes 98312 | tf_op jit(solution)/shard_map/ppermute | solution.py:27
  34.0 5.2 %collective-permute-start.9 = (f32[8,1024]{1,0:T(8,128)S(1)}, f32[8,1024]{1,0:T(8,128)S(1)}, u32[]{:S(2)}, u32[]{:S(2)}) collective-permute-start(f32[8,1024]{1,0:T(8,128)S(1)} %fusion.2.b0), channel_id=1, source_target_pairs={{0,8},{4,12},{8,0},{12,4},{1,9},{5,13},{9,1},{13,5},{2,10},{6,14},... | collective-permute-start | bytes 98312 | tf_op jit(solution)/shard_map/ppermute | solution.py:27
  34.4 4.9 %collective-permute-start.8 = (f32[8,1024]{1,0:T(8,128)S(1)}, f32[8,1024]{1,0:T(8,128)S(1)}, u32[]{:S(2)}, u32[]{:S(2)}) collective-permute-start(f32[8,1024]{1,0:T(8,128)S(1)} %fusion.2.b0), channel_id=1, source_target_pairs={{0,4},{4,0},{8,12},{12,8},{1,5},{5,1},{9,13},{13,9},{2,6},{6,2},{1... | collective-permute-start | bytes 98312 | tf_op jit(solution)/shard_map/ppermute | solution.py:27
  45.1 8.2 %copy-start = (bf16[16,4096,192]{1,2,0:T(8,128)(2,1)S(1)}, bf16[16,4096,192]{1,2,0:T(8,128)(2,1)}, u32[]{:S(2)}) copy-start(bf16[16,4096,192]{1,2,0:T(8,128)(2,1)} %param.18) | copy-start | bytes 75497472
  76.4 2.6 %collective-permute-start.11 = (bf16[32,1024]{1,0:T(8,128)(2,1)S(1)}, bf16[32,1024]{1,0:T(8,128)(2,1)S(1)}, u32[]{:S(2)}, u32[]{:S(2)}) collective-permute-start(bf16[32,1024]{1,0:T(8,128)(2,1)S(1)} %get-tuple-element.18), channel_id=1, source_target_pairs={{0,1},{1,0},{2,3},{3,2},{4,5},{5,4},{6,7},{7,6},{8,9},{9,8},{10,11... | collective-permute-start | bytes 196616 | tf_op jit(solution)/shard_map/ppermute | solution.py:27
  76.8 4.7 %collective-permute-start.12 = (bf16[32,1024]{1,0:T(8,128)(2,1)S(1)}, bf16[32,1024]{1,0:T(8,128)(2,1)S(1)}, u32[]{:S(2)}, u32[]{:S(2)}) collective-permute-start(bf16[32,1024]{1,0:T(8,128)(2,1)S(1)} %get-tuple-element.19), channel_id=1, source_target_pairs={{0,2},{1,3},{2,0},{3,1},{4,6},{5,7},{6,4},{7,5},{8,10},{9,11},{10,... | collective-permute-start | bytes 196616 | tf_op jit(solution)/shard_map/ppermute | solution.py:27
  77.7 4.4 %collective-permute-start.13 = (bf16[32,1024]{1,0:T(8,128)(2,1)S(1)}, bf16[32,1024]{1,0:T(8,128)(2,1)S(1)}, u32[]{:S(2)}, u32[]{:S(2)}) collective-permute-start(bf16[32,1024]{1,0:T(8,128)(2,1)S(1)} %get-tuple-element.20), channel_id=1, source_target_pairs={{0,3},{1,2},{2,1},{3,0},{4,7},{5,6},{6,5},{7,4},{8,11},{9,10},{10,... | collective-permute-start | bytes 196616 | tf_op jit(solution)/shard_map/ppermute | solution.py:27
  78.4 8.2 %collective-permute-start.7 = (f32[8,1024]{1,0:T(8,128)S(1)}, f32[8,1024]{1,0:T(8,128)S(1)}, u32[]{:S(2)}, u32[]{:S(2)}) collective-permute-start(f32[8,1024]{1,0:T(8,128)S(1)} %fusion.2.b0), channel_id=1, source_target_pairs={{0,0},{1,4},{2,8},{3,12},{4,1},{5,5},{6,9},{7,13},{8,2},{9,6},{10,... | collective-permute-start | bytes 98312 | tf_op jit(solution)/shard_map/ppermute | solution.py:265
  82.1 4.5 %collective-permute-start.14 = (f32[8,1024]{1,0:T(8,128)S(1)}, f32[8,1024]{1,0:T(8,128)S(1)}, u32[]{:S(2)}, u32[]{:S(2)}) collective-permute-start(f32[8,1024]{1,0:T(8,128)S(1)} %get-tuple-element.22), channel_id=1, source_target_pairs={{0,4},{4,0},{8,12},{12,8},{1,5},{5,1},{9,13},{13,9},{2,6},{6,2},{1... | collective-permute-start | bytes 98312 | tf_op jit(solution)/shard_map/ppermute | solution.py:27
  84.2 5.1 %collective-permute-start.15 = (f32[8,1024]{1,0:T(8,128)S(1)}, f32[8,1024]{1,0:T(8,128)S(1)}, u32[]{:S(2)}, u32[]{:S(2)}) collective-permute-start(f32[8,1024]{1,0:T(8,128)S(1)} %get-tuple-element.23), channel_id=1, source_target_pairs={{0,8},{4,12},{8,0},{12,4},{1,9},{5,13},{9,1},{13,5},{2,10},{6,14},... | collective-permute-start | bytes 98312 | tf_op jit(solution)/shard_map/ppermute | solution.py:27
  85.3 5.7 %collective-permute-start.16 = (f32[8,1024]{1,0:T(8,128)S(1)}, f32[8,1024]{1,0:T(8,128)S(1)}, u32[]{:S(2)}, u32[]{:S(2)}) collective-permute-start(f32[8,1024]{1,0:T(8,128)S(1)} %get-tuple-element.24), channel_id=1, source_target_pairs={{0,12},{4,8},{8,4},{12,0},{1,13},{5,9},{9,5},{13,1},{2,14},{6,10},... | collective-permute-start | bytes 98312 | tf_op jit(solution)/shard_map/ppermute | solution.py:27

commit v2 on v0

--- a/solution.py
+++ b/solution.py
@@ -1,8 +1,11 @@
+import functools
 import math
 
 import jax
 import jax.numpy as jnp
 from jax import lax
+from jax.experimental import pallas as pl
+from jax.experimental.pallas import tpu as pltpu
 from jax.sharding import PartitionSpec as P
 
 D = 4096
@@ -13,6 +16,493 @@
 TOPK = 8
 CAP = 2
 CACHE_LENGTH = 256
+SIDE = 4
+BF16 = jnp.bfloat16
+F32 = jnp.float32
+MIB = 1 << 20
+HERE = pl.BlockSpec(memory_space=pltpu.VMEM)
+SCALARS = pl.BlockSpec(memory_space=pltpu.SMEM)
+ANYWHERE = pl.BlockSpec(memory_space=pl.ANY)
+DMA = pltpu.SemaphoreType.DMA
+
+
+def swap(block, axis, k):
+    return lax.ppermute(block, axis, [(i, i ^ k) for i in range(SIDE)])
+
+
+def far(array):
+    return pltpu.with_memory_space_constraint(array, pltpu.HBM)
+
+
+def split3(value):
+    high = value.astype(BF16)
+    rest = value - high.astype(F32)
+    middle = rest.astype(BF16)
+    low = (rest - middle.astype(F32)).astype(BF16)
+    return high, middle, low
+
+
+def kernel_call(body, name, out_shape, in_specs, scratch=(), limit=4, cost=(0, 0, 0), aliases=None):
+    many = isinstance(out_shape, (tuple, list))
+    return pl.pallas_call(
+        body,
+        out_shape=out_shape,
+        in_specs=in_specs,
+        out_specs=(HERE,) * len(out_shape) if many else HERE,
+        scratch_shapes=list(scratch),
+        input_output_aliases=aliases or {},
+        compiler_params=pltpu.CompilerParams(vmem_limit_bytes=limit * MIB),
+        cost_estimate=pl.CostEstimate(
+            flops=cost[0], bytes_accessed=cost[1], transcendentals=cost[2]
+        ),
+        name=name,
+    )
+
+
+def attention_kernel(
+    lengths_far,
+    queries_far,
+    cache_far,
+    ids_far,
+    route_far,
+    residual_far,
+    weight_far,
+    entry_far,
+    out,
+    weight,
+    entry,
+    lengths,
+    queries,
+    cache,
+    ids,
+    route,
+    residual,
+    staged,
+    gathered,
+    sems,
+):
+    width = entry.shape[2]
+    own = pl.ds(pl.multiple_of(lax.axis_index("ep") * width, width), width)
+    copies = [
+        pltpu.make_async_copy(source, target, sems.at[i])
+        for i, (source, target) in enumerate(
+            (
+                (lengths_far, lengths),
+                (queries_far, queries),
+                (cache_far, cache),
+                (ids_far, ids),
+                (route_far, route),
+                (residual_far, residual),
+                (weight_far, weight),
+                (entry_far.at[:, :, own], entry),
+            )
+        )
+    ]
+    for copy in copies:
+        copy.start()
+    copies[0].wait()
+    copies[1].wait()
+    rows = queries.shape[0]
+    heads = queries.shape[1] // HEAD_SIZE
+    for h in range(heads):
+        lanes = slice(h * HEAD_SIZE, (h + 1) * HEAD_SIZE)
+        staged[h * rows : (h + 1) * rows, :] = queries[:, lanes].astype(F32)
+    copies[2].wait()
+    place = lax.broadcasted_iota(jnp.int32, (heads, 2 * CACHE_LENGTH), 1)
+    for s in range(rows):
+        mine = staged[pl.ds(s, heads, stride=rows), :].astype(BF16)
+        both = cache[s]
+        scores = lax.dot_general(
+            mine, both, (((1,), (1,)), ((), ())), preferred_element_type=F32
+        ) * (1.0 / math.sqrt(HEAD_SIZE))
+        visible = jnp.logical_and(place % 2 == 0, place < 2 * lengths[s])
+        scores = jnp.where(visible, scores, -1e30)
+        raised = jnp.where(visible, jnp.exp(scores - jnp.max(scores, axis=1, keepdims=True)), 0.0)
+        weights = raised / jnp.sum(raised, axis=1, keepdims=True)
+        moved = pltpu.roll(weights, 1, 1).astype(BF16)
+        gathered[pl.ds(s, heads, stride=rows), :] = jnp.dot(
+            moved, both, preferred_element_type=F32
+        )
+    width = heads * HEAD_SIZE
+    for h in range(heads):
+        lanes = slice(h * HEAD_SIZE, (h + 1) * HEAD_SIZE)
+        out[:, lanes] = gathered[h * rows : (h + 1) * rows, :].astype(BF16)
+    copies[3].wait()
+    copies[4].wait()
+    row = lax.broadcasted_iota(jnp.int32, (TOPK, 128), 0)
+    lane = lax.broadcasted_iota(jnp.int32, (TOPK, 128), 1)
+    total = jnp.zeros((rows, 128), F32)
+    for j, part in enumerate((ids[...].astype(F32).astype(BF16), *split3(route[...]))):
+        spread = (lane == row + j * TOPK).astype(F32).astype(BF16)
+        total = total + jnp.dot(part, spread, preferred_element_type=F32)
+    out[:, width : width + 128] = total.astype(BF16)
+    copies[5].wait()
+    out[:, width + 128 :] = residual[...]
+    copies[6].wait()
+    copies[7].wait()
+
+
+def attention(lengths, queries, cache, ids, route, residual, weight, entry):
+    rows, width = queries.shape
+    staged = pltpu.VMEM((rows * width // HEAD_SIZE, HEAD_SIZE), F32)
+    return kernel_call(
+        attention_kernel,
+        "attention",
+        (
+            jax.ShapeDtypeStruct((rows, width + 128 + residual.shape[1]), BF16),
+            pltpu.VMEM(weight.shape, BF16),
+            pltpu.VMEM((*entry.shape[:2], entry.shape[2] // SIDE), BF16),
+        ),
+        [ANYWHERE] * 8,
+        [
+            pltpu.SMEM(lengths.shape, jnp.int32),
+            pltpu.VMEM(queries.shape, BF16),
+            pltpu.VMEM(cache.shape, BF16),
+            pltpu.VMEM(ids.shape, jnp.int32),
+            pltpu.VMEM(route.shape, F32),
+            pltpu.VMEM(residual.shape, BF16),
+            staged,
+            staged,
+            DMA((8,)),
+        ],
+        cost=(10_000_000, 12_000_000, 65536),
+    )(*map(far, (lengths, queries, cache, ids, route, residual, weight, entry)))
+
+
+def fetch_entry_kernel(after, source, t1, t2, t3, sems):
+    del after
+    width = t1.shape[2]
+    copies = []
+    for k, target in enumerate((t1, t2, t3), 1):
+        start = pl.multiple_of((lax.axis_index("ep") ^ k) * width, width)
+        copies.append(
+            pltpu.make_async_copy(source.at[:, :, pl.ds(start, width)], target, sems.at[k - 1])
+        )
+    for copy in copies:
+        copy.start()
+    for copy in copies:
+        copy.wait()
+
+
+def fetch_entry(source, after):
+    shape = (*source.shape[:2], source.shape[2] // SIDE)
+    return kernel_call(
+        fetch_entry_kernel,
+        "fetch_entry",
+        (pltpu.VMEM(shape, BF16),) * 3,
+        [ANYWHERE, ANYWHERE],
+        [DMA((3,))],
+        limit=1,
+        cost=(0, 6 * math.prod(shape), 0),
+    )(after, far(source))
+
+
+def fetch_kernel(start, after, source, target, sem):
+    del after
+    copy = pltpu.make_async_copy(source.at[pl.ds(start, target.shape[0])], target, sem)
+    copy.start()
+    copy.wait()
+
+
+def fetch(name, source, start, count, after):
+    shape = (count, *source.shape[1:])
+    return kernel_call(
+        functools.partial(fetch_kernel, start),
+        name,
+        pltpu.VMEM(shape, BF16),
+        [ANYWHERE, ANYWHERE],
+        [DMA],
+        limit=1,
+        cost=(0, 2 * math.prod(shape), 0),
+    )(after, far(source))
+
+
+def projection_kernel(slot_far, b0, b1, b2, b3, weight, unused, out, routing, slot_of, kept, sem):
+    del unused
+    copy = pltpu.make_async_copy(slot_far, slot_of, sem)
+    copy.start()
+    blocks = (b0, b1, b2, b3)
+    rows = b0.shape[0]
+    width = weight.shape[0]
+    everyone = SIDE * rows
+    me = lax.axis_index("ep")
+    held = jnp.concatenate([b[:, :width].astype(F32) for b in blocks], axis=0).astype(BF16)
+    row = lax.broadcasted_iota(jnp.int32, (everyone, everyone), 0)
+    column = lax.broadcasted_iota(jnp.int32, (everyone, everyone), 1)
+    wanted = jnp.zeros((everyone, everyone), jnp.int32)
+    for k, block in enumerate(blocks):
+        span = pl.ds(pl.multiple_of((me ^ k) * rows, rows), rows)
+        routing[span, :] = block[:, width : width + 128].astype(F32)
+        kept[span, :] = block[:, width + 128 :].astype(F32)
+    copy.wait()
+    for r in range(everyone):
+        slot = slot_of[r]
+        wanted = jnp.where(row == r, ((slot // rows) ^ me) * rows + slot % rows, wanted)
+    order = (wanted == column).astype(F32).astype(BF16)
+    ordered = jnp.dot(order, held, preferred_element_type=F32).astype(BF16)
+    own = (me == lax.axis_index("hd")).astype(F32)
+    out[...] = jnp.dot(ordered, weight[...], preferred_element_type=F32) + own * kept[...]
+
+
+def projection(slot_of, blocks, weight, unused):
+    everyone = SIDE * blocks[0].shape[0]
+    wide = (everyone, weight.shape[1])
+    return kernel_call(
+        projection_kernel,
+        "projection",
+        (jax.ShapeDtypeStruct(wide, F32), jax.ShapeDtypeStruct((everyone, 128), F32)),
+        [ANYWHERE] + [HERE] * 5 + [ANYWHERE],
+        [pltpu.SMEM(slot_of.shape, jnp.int32), pltpu.VMEM(wide, F32), DMA],
+        limit=6,
+        cost=(140_000_000, 4_500_000, 0),
+    )(far(slot_of), *blocks, weight, unused)
+
+
+def add_kernel(a, b, out):
+    out[...] = a[...] + b[...]
+
+
+def add(a, b):
+    return kernel_call(
+        add_kernel, "add", jax.ShapeDtypeStruct(a.shape, F32), [HERE] * 2, cost=(a.size, a.size, 0)
+    )(a, b)
+
+
+def stream_kernel(a, b, unused, stream, packed):
+    del unused
+    total = a[...] + b[...]
+    stream[...] = total
+    width = total.shape[1]
+    packed[:, :width] = total.astype(BF16)
+    squares = jnp.sum(total * total, axis=1, keepdims=True)
+    lane = lax.broadcasted_iota(jnp.int32, (total.shape[0], 128), 1)
+    parts = [part.astype(F32) for part in split3(jnp.broadcast_to(squares, lane.shape))]
+    spread = jnp.where(lane == 0, parts[0], jnp.where(lane == 1, parts[1], parts[2]))
+    packed[:, width:] = jnp.where(lane < 3, spread, 0.0).astype(BF16)
+
+
+def streams(a, b, unused):
+    rows, width = a.shape
+    return kernel_call(
+        stream_kernel,
+        "stream",
+        (jax.ShapeDtypeStruct(a.shape, F32), jax.ShapeDtypeStruct((rows, width + 128), BF16)),
+        [HERE, HERE, ANYWHERE],
+        cost=(a.size * 4, a.size * 4, 0),
+    )(a, b, unused)
+
+
+def entry_product(packed, near, put):
+    count, hidden, width = near.shape
+    turned = packed[:, :width].astype(F32).T.astype(BF16)
+    for e in range(count):
+        part = jnp.dot(near[e], turned, preferred_element_type=F32)
+        put(e * hidden, hidden, part)
+
+
+def entry_first_kernel(start, packed, near, source, out, target, sem):
+    copy = pltpu.make_async_copy(source.at[pl.ds(start, target.shape[0])], target, sem)
+    copy.start()
+
+    def put(at, hidden, part):
+        out[at : at + hidden, :] = part
+
+    entry_product(packed, near, put)
+    copy.wait()
+
+
+def entry_next_kernel(start, packed, near, before, source, out, target, sem):
+    copy = pltpu.make_async_copy(source.at[pl.ds(start, target.shape[0])], target, sem)
+    copy.start()
+
+    def put(at, hidden, part):
+        out[at : at + hidden, :] = before[at : at + hidden, :] + part
+
+    entry_product(packed, near, put)
+    copy.wait()
+
+
+def entry_more_kernel(packed, near, before, out):
+    def put(at, hidden, part):
+        out[at : at + hidden, :] = before[at : at + hidden, :] + part
+
+    entry_product(packed, near, put)
+
+
+def entry_last_kernel(packed, near, before, routing, p0, p1, p2, out):
+    count, _, width = near.shape
+    rows = packed.shape[0]
+    squares = jnp.zeros((rows, 128), F32)
+    for block in (p0, p1, p2, packed):
+        squares = squares + block[:, width:].astype(F32)
+    mean = jnp.sum(squares.T, axis=0, keepdims=True) / (SIDE * width)
+    scale = lax.rsqrt(mean + 1e-06)
+    table = routing[...].T
+    ids = table[0:TOPK, :]
+    weight = table[TOPK : 2 * TOPK, :] + table[2 * TOPK : 3 * TOPK, :]
+    weight = weight + table[3 * TOPK : 4 * TOPK, :]
+    base = lax.axis_index("ep") * count
+
+    def put(at, hidden, part):
+        number = (base + at // hidden).astype(F32)
+        share = jnp.sum(jnp.where(ids == number, weight, 0.0), axis=0, keepdims=True)
+        total = (before[at : at + hidden, :] + part) * scale
+        active = (total / (1.0 + jnp.exp(-total))).astype(BF16).astype(F32) * share
+        high = active.astype(BF16).astype(F32)
+        out[at : at + hidden, :] = jnp.concatenate([high, active - high], axis=1).astype(BF16)
+
+    entry_product(packed, near, put)
+
+
+def entries(packs, near, routing, source, starts):
+    count, hidden, width = source.shape
+    rows = packs[0].shape[0]
+    part = jax.ShapeDtypeStruct((count * hidden, rows), F32)
+    cost = (2 * rows * count * hidden * width // SIDE, 2 * count * hidden * width // SIDE, 0)
+    bring = lambda start, end: pltpu.VMEM((end - start, hidden, width), BF16)
+    total, more = kernel_call(
+        functools.partial(entry_first_kernel, starts[0]),
+        "entry0",
+        (part, bring(*starts[:2])),
+        [HERE] * 2 + [ANYWHERE],
+        [DMA],
+        cost=cost,
+    )(packs[0], near[0], far(source))
+    total, rest = kernel_call(
+        functools.partial(entry_next_kernel, starts[1]),
+        "entry1",
+        (part, bring(starts[1], count)),
+        [HERE] * 3 + [ANYWHERE],
+        [DMA],
+        cost=cost,
+        aliases={2: 0},
+    )(packs[1], near[1], total, far(source))
+    total = kernel_call(
+        entry_more_kernel, "entry2", part, [HERE] * 3, cost=cost, aliases={2: 0}
+    )(packs[2], near[2], total)
+    scaled = kernel_call(
+        entry_last_kernel,
+        "entry3",
+        jax.ShapeDtypeStruct((count * hidden, 2 * rows), BF16),
+        [HERE] * 7,
+        cost=cost,
+    )(packs[3], near[3], total, routing, *packs[:3])
+    return scaled, more, rest
+
+
+def leave_product(start, count, step, scaled, near, out):
+    rows = out.shape[0]
+    left = scaled[...].astype(F32).T.astype(BF16)
+    for c in range(0, count, step):
+        columns = pl.ds(pl.multiple_of(start + c, step), step)
+        total = jnp.zeros((2 * rows, step), F32)
+        at = 0
+        for array in near:
+            depth = array.shape[0] * array.shape[1]
+            flat = array.reshape(depth, array.shape[2])
+            total = total + jnp.dot(
+                left[:, at : at + depth], flat[:, columns], preferred_element_type=F32
+            )
+            at += depth
+        out[:, c : c + step] = (total[:rows] + total[rows:]).astype(out.dtype)
+
+
+def leave_kernel(other, step, scaled, a, b, c, unused, out):
+    del unused
+    half = out.shape[1]
+    chip = (lax.axis_index("hd") // 2) ^ other
+    leave_product(pl.multiple_of(chip * half, half), half, step, scaled, (a, b, c), out)
+
+
+def leaves(name, other, dtype, scaled, near, unused):
+    count = sum(array.shape[0] for array in near)
+    _, hidden, width = near[0].shape
+    rows = scaled.shape[1] // 2
+    return kernel_call(
+        functools.partial(leave_kernel, other, 1024),
+        name,
+        jax.ShapeDtypeStruct((rows, width // 2), dtype),
+        [HERE] * 4 + [ANYWHERE],
+        cost=(2 * rows * count * hidden * width, count * hidden * width, 0),
+        limit=6,
+    )(scaled, *near, unused)
+
+
+def halve_kernel(mine, received, keep, send):
+    width = keep.shape[1]
+    core = lax.axis_index("hd") % 2
+    for out, which in ((send, 1 - core), (keep, core)):
+        columns = pl.ds(pl.multiple_of(which * width, width), width)
+        out[...] = mine[:, columns] + received[:, columns].astype(F32)
+
+
+def halve(mine, received):
+    rows, width = mine.shape
+    return kernel_call(
+        halve_kernel,
+        "halve",
+        (jax.ShapeDtypeStruct((rows, width // 2), F32),) * 2,
+        [HERE] * 2,
+        cost=(mine.size, mine.size * 6, 0),
+    )(mine, received)
+
+
+def share_kernel(own, received, stream, o0, o1, o2, o3):
+    rows = o0.shape[0]
+    me = lax.axis_index("ep")
+    here = (me == lax.axis_index("hd")).astype(F32)
+    for k, out in enumerate((o0, o1, o2, o3)):
+        span = pl.ds(pl.multiple_of((me ^ k) * rows, rows), rows)
+        out[...] = own[span, :] + received[span, :] + here * stream[span, :]
+
+
+def share(own, received, stream):
+    rows, width = own.shape
+    return kernel_call(
+        share_kernel,
+        "share",
+        (jax.ShapeDtypeStruct((rows // SIDE, width), F32),) * SIDE,
+        [HERE] * 3,
+        cost=(own.size * 3, own.size * 16, 0),
+    )(own, received, stream)
+
+
+def square_body(
+    residual,
+    queries,
+    key_value_cache,
+    lengths,
+    slot_of,
+    out_weight,
+    expert_ids,
+    route_weight,
+    in_weight,
+    down_weight,
+):
+    rows = queries.shape[0]
+    cache = key_value_cache.reshape(rows, 2 * CACHE_LENGTH, HEAD_SIZE)
+    entry = jnp.swapaxes(in_weight, 1, 2)
+    count = entry.shape[0]
+    starts = (count // 2, count * 3 // 4)
+    attended, weight, near0 = attention(
+        lengths, queries, cache, expert_ids, route_weight, residual, out_weight, entry
+    )
+    blocks = [attended] + [swap(attended, "ep", k) for k in (1, 2, 3)]
+    near = (near0, *fetch_entry(entry, attended))
+    partial_value, routing = projection(slot_of, blocks, weight, near[3])
+    pair = add(partial_value, swap(partial_value, "hd", 1))
+    far_pair = swap(pair, "hd", 2)
+    leave_a = fetch("fetch_leave", down_weight, 0, starts[0], pair)
+    stream, packed = streams(pair, far_pair, leave_a)
+    packs = [packed] + [swap(packed, "ep", k) for k in (1, 2, 3)]
+    scaled, *rest = entries(packs, near, routing, down_weight, starts)
+    theirs = leaves("leave_away", 1, BF16, scaled, (leave_a, *rest), scaled)
+    mine = leaves("leave_here", 0, F32, scaled, (leave_a, *rest), theirs)
+    keep, send = halve(mine, swap(theirs, "hd", 2))
+    total, *others = share(keep, swap(send, "hd", 1), stream)
+    for k, block in enumerate(others):
+        total = total + swap(block, "ep", k + 1)
+    return total.astype(BF16)
 
 
 def expert_pass(block, in_weight, down_weight):
@@ -120,4 +610,5 @@
         P("ep", "hd", None),
     )
     out_specs = P(("groups", "ep"), "hd")
-    return jax.shard_map(body, mesh=mesh, in_specs=in_specs, out_specs=out_specs, check_vma=False)
+    chosen = square_body if mesh.shape["ep"] == mesh.shape["hd"] == SIDE else body
+    return jax.shard_map(chosen, mesh=mesh, in_specs=in_specs, out_specs=out_specs, check_vma=False)

time: 177 us -> 60.5 us (0.34)
  blocking collectives: 56.9 us -> 0 us
  waiting for transfers between devices: 55.4 us -> 9.86 us
  Pallas kernels: 0 us -> 32.2 us
  matrix products: 25.8 us -> 0 us
  between operations: 13.5 us -> 0.15 us
  local copies, waits for them, and re-layouts: 9.82 us -> 0 us
  starting transfers between devices: 9.62 us -> 17.5 us
  other arithmetic: 4.85 us -> 0.62 us
    reduce_scatter x2 -> x0, waiting for transfers between devices: 41.8 us -> none  [the longest x1 23.3 us: body(): lax.psum_scatter(results.astype(jnp.bfloat16), 'hd', scatter_dimension=2,...]
    pallas_call x0 -> x14, Pallas kernels: none -> 32.2 us  [the longest x1 6.45 us: fetch_entry(): kernel_call(fetch_entry_kernel, 'fetch_entry', (pltpu.VMEM(shape, BF16),)...]
    all_to_all x1 -> x0, blocking collectives: 30.8 us -> none  [body(): lax.all_to_all(outgoing, 'ep', split_axis=0, concat_axis=0, tiled=True)]
    dot_general x7 -> x0, matrix products: 24.6 us -> none  [the longest x1 19.5 us: expert_pass(): jnp.einsum('secf,efd->secd', hidden, down_weight, preferred_element_type=...]
    all_gather x2 -> x0, blocking collectives: 20.3 us -> none  [the longest x1 15.1 us: body(): lax.all_gather(attended, 'ep', axis=0, tiled=True)]
    ppermute x0 -> x13, starting transfers between devices: none -> 17.5 us  [swap(): return lax.ppermute(block, axis, [(i, i ^ k) for i in range(SIDE)])]
    all_to_all x2 -> x0, waiting for transfers between devices: 13.6 us -> none  [the longest x1 8.59 us: body(): lax.all_to_all(shares, 'ep', split_axis=0, concat_axis=0, tiled=True)]
    ppermute x0 -> x13, waiting for transfers between devices: none -> 9.86 us  [swap(): return lax.ppermute(block, axis, [(i, i ^ k) for i in range(SIDE)])]
  transfers between devices with their start and end apart: 4 -> 13, of which waited for: 4 -> 5; matrix products, arithmetic and copies ran while one was open for 1% -> 0% of each run, Pallas kernels for 0% -> 35%
where the time goes in v2:
time: 60.5 us; the launch traced here: 60.3 us
  Pallas kernels  32.2 us (53%)
  starting transfers between devices  17.5 us (29%)
  waiting for transfers between devices  9.86 us (16%)
  other arithmetic  0.62 us (1%)
    ppermute x13, starting transfers between devices, swap(): return lax.ppermute(block, axis, [(i, i ^ k) for i in range(SIDE)])  17.5 us
    ppermute x13, waiting for transfers between devices, swap(): return lax.ppermute(block, axis, [(i, i ^ k) for i in range(SIDE)])  9.86 us
    pallas_call x1, Pallas kernels, fetch_entry(): kernel_call(fetch_entry_kernel, 'fetch_entry', (pltpu.VMEM(shape, BF16),)...  6.45 us
    pallas_call x1, Pallas kernels, attention(): kernel_call(attention_kernel, 'attention', (jax.ShapeDtypeStruct((rows, w...  4.75 us
    pallas_call x2, Pallas kernels, leaves(): kernel_call(functools.partial(leave_kernel, other, 1024), name, jax.Shape...  4.68 us
    pallas_call x1, Pallas kernels, fetch(): kernel_call(functools.partial(fetch_kernel, start), name, pltpu.VMEM(shap...  4.58 us
    pallas_call x1, Pallas kernels, entries(): kernel_call(functools.partial(entry_next_kernel, starts[1]), 'entry1', (p...  2.8 us
    pallas_call x1, Pallas kernels, entries(): kernel_call(functools.partial(entry_first_kernel, starts[0]), 'entry0', (...  2.79 us
  transfers between devices with their start and end apart: 13, of which 5 were waited for; matrix products, arithmetic and copies ran while one was open for 0% of the time, Pallas kernels for 35%

profile of v2, /device:TPU:0, one launch (start us, length us, event | category | flops | bytes accessed | tf_op | source)
XLA Modules:
  0.0 60.3 jit_solution(18370392387051749390)
XLA Ops:
  0.0 4.8 %attention.1 = (bf16[8,3200]{1,0:T(8,128)(2,1)S(1)}, bf16[2048,1024]{1,0:T(8,128)(2,1)S(1)}, bf16[16,192,1024]{2,1,0:T(8,128)(2,1)S(1)}) custom-call(s32[8]{0:T(128)} %lengths_far.1, bf16[8,2048]{1,0:T(8,128)(2,1)} %queries_far.1, bf16[8,512,128]{2,1,0:T(8,128)(2,1)} %bitcast.4, s32[8,8]{1,0:T(8,128)} %ids_far.1, f32[8,8]{1,0:T(8,128)} %route_far.1, ...), custom_call_target="tpu_custom_call" | custom-call | flops 10000000 | bytes 12000000 | tf_op jit(solution)/shard_map/attention/pallas_call | solution.py:148
  4.8 3.1 %collective-permute-start = (bf16[8,3200]{1,0:T(8,128)(2,1)S(1)}, bf16[8,3200]{1,0:T(8,128)(2,1)S(1)}, u32[]{:S(2)}, u32[]{:S(2)}) collective-permute-start(bf16[8,3200]{1,0:T(8,128)(2,1)S(1)} %get-tuple-element.25.after.b0), channel_id=1, source_target_pairs={{0,4},{4,0},{8,12},{12,8},{1,5},{5,1},{9,13},{13,9},{2,6},{6,2},{1... | collective-permute-start | bytes 153608 | tf_op jit(solution)/shard_map/ppermute | solution.py:30
  7.9 2.6 %collective-permute-start.1 = (bf16[8,3200]{1,0:T(8,128)(2,1)S(1)}, bf16[8,3200]{1,0:T(8,128)(2,1)S(1)}, u32[]{:S(2)}, u32[]{:S(2)}) collective-permute-start(bf16[8,3200]{1,0:T(8,128)(2,1)S(1)} %get-tuple-element.25.after.b0), channel_id=1, source_target_pairs={{0,8},{4,12},{8,0},{12,4},{1,9},{5,13},{9,1},{13,5},{2,10},{6,14},... | collective-permute-start | bytes 153608 | tf_op jit(solution)/shard_map/ppermute | solution.py:30
  10.4 0.0 collective-permute-start.2
  10.4 6.5 %fetch_entry.1 = (bf16[16,192,1024]{2,1,0:T(8,128)(2,1)S(1)}, bf16[16,192,1024]{2,1,0:T(8,128)(2,1)S(1)}, bf16[16,192,1024]{2,1,0:T(8,128)(2,1)S(1)}) custom-call(bf16[8,3200]{1,0:T(8,128)(2,1)S(1)} %get-tuple-element.25.after.b0, bf16[16,192,4096]{2,1,0:T(8,128)(2,1)} %bitcast.3), custom_call_target="tpu_custom_call" | custom-call | bytes 18874368 | tf_op jit(solution)/shard_map/fetch_entry/pallas_call | solution.py:189
  16.9 0.0 collective-permute-done.b1
  16.9 0.0 collective-permute-done.1.b2
  16.9 0.0 collective-permute-done.2.b3
  16.9 1.8 %projection.1 = (f32[32,1024]{1,0:T(8,128)S(1)}, f32[32,128]{1,0:T(8,128)S(1)}) custom-call(s32[32]{0:T(128)} %slot_far.1, bf16[8,3200]{1,0:T(8,128)(2,1)S(1)} %get-tuple-element.25.after.b0, bf16[8,3200]{1,0:T(8,128)(2,1)S(1)} %collective-permute-done.b1, bf16[8,3200]{1,0:T(8,128)(2,1)S(1)} %collective-permute-done.1.b2, ...), custom_call_target="tpu_custom_call" | custom-call | flops 140000000 | bytes 4500000 | tf_op jit(solution)/shard_map/projection/pallas_call | solution.py:250
  18.7 0.1 collective-permute-start.3
  18.8 1.3 %collective-permute-done.3.b = f32[32,1024]{1,0:T(8,128)S(1)} collective-permute-done((f32[32,1024]{1,0:T(8,128)S(1)}, f32[32,1024]{1,0:T(8,128)S(1)}, u32[]{:S(2)}, u32[]{:S(2)}) %collective-permute-start.3) | collective-permute-done | bytes 131104 | tf_op jit(solution)/shard_map/ppermute | solution.py:30
  20.2 1.8 %collective-permute-start.4 = (f32[32,1024]{1,0:T(8,128)S(1)}, f32[32,1024]{1,0:T(8,128)S(1)}, u32[]{:S(2)}, u32[]{:S(2)}) collective-permute-start(f32[32,1024]{1,0:T(8,128)S(1)} %add.16.after.a), channel_id=1, source_target_pairs={{0,2},{1,3},{2,0},{3,1},{4,6},{5,7},{6,4},{7,5},{8,10},{9,11},{10,... | collective-permute-start | bytes 393224 | tf_op jit(solution)/shard_map/ppermute | solution.py:30
  21.9 4.6 %fetch_leave.1.unused.a = bf16[8,192,4096]{2,1,0:T(8,128)(2,1)S(1)} custom-call(f32[32,1024]{1,0:T(8,128)S(1)} %add.16.after.a, bf16[16,192,4096]{2,1,0:T(8,128)(2,1)} %source.5), custom_call_target="tpu_custom_call" | custom-call | bytes 12582912 | tf_op jit(solution)/shard_map/fetch_leave/pallas_call | solution.py:209
  26.5 0.0 collective-permute-done.4.b
  26.5 0.1 stream.1
  26.6 0.7 %collective-permute-start.7 = (bf16[32,1152]{1,0:T(8,128)(2,1)S(1)}, bf16[32,1152]{1,0:T(8,128)(2,1)S(1)}, u32[]{:S(2)}, u32[]{:S(2)}) collective-permute-start(bf16[32,1152]{1,0:T(8,128)(2,1)S(1)} %get-tuple-element.29.packed.p0), channel_id=1, source_target_pairs={{0,4},{4,0},{8,12},{12,8},{1,5},{5,1},{9,13},{13,9},{2,6},{6,2},{1... | collective-permute-start | bytes 221192 | tf_op jit(solution)/shard_map/ppermute | solution.py:30
  27.4 3.5 %collective-permute-start.6 = (bf16[32,1152]{1,0:T(8,128)(2,1)S(1)}, bf16[32,1152]{1,0:T(8,128)(2,1)S(1)}, u32[]{:S(2)}, u32[]{:S(2)}) collective-permute-start(bf16[32,1152]{1,0:T(8,128)(2,1)S(1)} %get-tuple-element.29.packed.p0), channel_id=1, source_target_pairs={{0,8},{4,12},{8,0},{12,4},{1,9},{5,13},{9,1},{13,5},{2,10},{6,14},... | collective-permute-start | bytes 221192 | tf_op jit(solution)/shard_map/ppermute | solution.py:30
  30.9 0.2 collective-permute-start.5
  31.1 2.8 %entry0.1 = (f32[3072,32]{1,0:T(8,128)S(1)}, bf16[4,192,4096]{2,1,0:T(8,128)(2,1)S(1)}) custom-call(bf16[32,1152]{1,0:T(8,128)(2,1)S(1)} %get-tuple-element.29.packed.p0, bf16[16,192,1024]{2,1,0:T(8,128)(2,1)S(1)} %get-tuple-element.32.near, bf16[16,192,4096]{2,1,0:T(8,128)(2,1)} %source.5), custom_call_target="tpu_custom_call" | custom-call | flops 201326592 | bytes 6291456 | tf_op jit(solution)/shard_map/entry0/pallas_call | solution.py:363
  33.9 0.0 collective-permute-done.7.packed.p1
  33.9 2.8 %entry1.1 = (f32[3072,32]{1,0:T(8,128)S(1)}, bf16[4,192,4096]{2,1,0:T(8,128)(2,1)S(1)}) custom-call(bf16[32,1152]{1,0:T(8,128)(2,1)S(1)} %collective-permute-done.7.packed.p1, bf16[16,192,1024]{2,1,0:T(8,128)(2,1)S(1)} %get-tuple-element.31.near, f32[3072,32]{1,0:T(8,128)S(1)} %get-tuple-element.33.before, ...), custom_call_target="tpu_custom_call", output_to_operand_aliasing={{0}: (2, {})} | custom-call | flops 201326592 | bytes 6291456 | tf_op jit(solution)/shard_map/entry1/pallas_call | solution.py:371
  36.7 0.0 collective-permute-done.6.packed.p2
  36.7 2.0 %entry2.1.before = f32[3072,32]{1,0:T(8,128)S(1)} custom-call(bf16[32,1152]{1,0:T(8,128)(2,1)S(1)} %collective-permute-done.6.packed.p2, bf16[16,192,1024]{2,1,0:T(8,128)(2,1)S(1)} %get-tuple-element.30.near, f32[3072,32]{1,0:T(8,128)S(1)} %get-tuple-element.34.before), custom_call_target="tpu_custom_call", output_to_operand_aliasing={{}: (2, {})} | custom-call | flops 201326592 | bytes 6291456 | tf_op jit(solution)/shard_map/entry2/pallas_call | solution.py:380
  38.7 0.0 collective-permute-done.5.packed
  38.7 2.2 %entry3.1.scaled.unused = bf16[3072,64]{1,0:T(8,128)(2,1)S(1)} custom-call(bf16[32,1152]{1,0:T(8,128)(2,1)S(1)} %collective-permute-done.5.packed, bf16[16,192,1024]{2,1,0:T(8,128)(2,1)S(1)} %get-tuple-element.27.unused.near, f32[3072,32]{1,0:T(8,128)S(1)} %entry2.1.before, f32[32,128]{1,0:T(8,128)S(1)} %get-tuple-element.35.routing, ...), custom_call_target="tpu_custom_call" | custom-call | flops 201326592 | bytes 6291456 | tf_op jit(solution)/shard_map/entry3/pallas_call | solution.py:383
  40.9 2.3 %leave_away.1.unused = bf16[32,2048]{1,0:T(8,128)(2,1)S(1)} custom-call(bf16[3072,64]{1,0:T(8,128)(2,1)S(1)} %entry3.1.scaled.unused, bf16[8,192,4096]{2,1,0:T(8,128)(2,1)S(1)} %fetch_leave.1.unused.a, bf16[4,192,4096]{2,1,0:T(8,128)(2,1)S(1)} %get-tuple-element.36.b, bf16[4,192,4096]{2,1,0:T(8,128)(2,1)S(1)} %get-tuple-element.37.c, ...), custom_call_target="tpu_custom_call" | custom-call | flops 805306368 | bytes 12582912 | tf_op jit(solution)/shard_map/leave_away/pallas_call | solution.py:421
  43.2 1.0 %collective-permute-start.8 = (bf16[32,2048]{1,0:T(8,128)(2,1)S(1)}, bf16[32,2048]{1,0:T(8,128)(2,1)S(1)}, u32[]{:S(2)}, u32[]{:S(2)}) collective-permute-start(bf16[32,2048]{1,0:T(8,128)(2,1)S(1)} %leave_away.1.unused), channel_id=1, source_target_pairs={{0,2},{1,3},{2,0},{3,1},{4,6},{5,7},{6,4},{7,5},{8,10},{9,11},{10,... | collective-permute-start | bytes 393224 | tf_op jit(solution)/shard_map/ppermute | solution.py:30
  44.2 2.3 %leave_here.1.mine = f32[32,2048]{1,0:T(8,128)S(1)} custom-call(bf16[3072,64]{1,0:T(8,128)(2,1)S(1)} %entry3.1.scaled.unused, bf16[8,192,4096]{2,1,0:T(8,128)(2,1)S(1)} %fetch_leave.1.unused.a, bf16[4,192,4096]{2,1,0:T(8,128)(2,1)S(1)} %get-tuple-element.36.b, bf16[4,192,4096]{2,1,0:T(8,128)(2,1)S(1)} %get-tuple-element.37.c, ...), custom_call_target="tpu_custom_call" | custom-call | flops 805306368 | bytes 12582912 | tf_op jit(solution)/shard_map/leave_here/pallas_call | solution.py:421
  46.6 1.7 %collective-permute-done.8.received = bf16[32,2048]{1,0:T(8,128)(2,1)S(1)} collective-permute-done((bf16[32,2048]{1,0:T(8,128)(2,1)S(1)}, bf16[32,2048]{1,0:T(8,128)(2,1)S(1)}, u32[]{:S(2)}, u32[]{:S(2)}) %collective-permute-start.8) | collective-permute-done | bytes 131104 | tf_op jit(solution)/shard_map/ppermute | solution.py:30
  48.3 0.1 collective-permute-start.9
  48.4 1.3 %collective-permute-done.9.received = f32[32,1024]{1,0:T(8,128)S(1)} collective-permute-done((f32[32,1024]{1,0:T(8,128)S(1)}, f32[32,1024]{1,0:T(8,128)S(1)}, u32[]{:S(2)}, u32[]{:S(2)}) %collective-permute-start.9) | collective-permute-done | bytes 131104 | tf_op jit(solution)/shard_map/ppermute | solution.py:30
  49.7 0.4 collective-permute-start.10
  50.1 3.8 %collective-permute-start.11 = (f32[8,1024]{1,0:T(8,128)S(1)}, f32[8,1024]{1,0:T(8,128)S(1)}, u32[]{:S(2)}, u32[]{:S(2)}) collective-permute-start(f32[8,1024]{1,0:T(8,128)S(1)} %get-tuple-element.43), channel_id=1, source_target_pairs={{0,8},{4,12},{8,0},{12,4},{1,9},{5,13},{9,1},{13,5},{2,10},{6,14},... | collective-permute-start | bytes 98312 | tf_op jit(solution)/shard_map/ppermute | solution.py:30
  54.0 0.2 collective-permute-start.12
  54.2 0.0 collective-permute-done.10
  54.2 2.2 %collective-permute-done.11 = f32[8,1024]{1,0:T(8,128)S(1)} collective-permute-done((f32[8,1024]{1,0:T(8,128)S(1)}, f32[8,1024]{1,0:T(8,128)S(1)}, u32[]{:S(2)}, u32[]{:S(2)}) %collective-permute-start.11) | collective-permute-done | bytes 32800 | tf_op jit(solution)/shard_map/ppermute | solution.py:30
  56.3 3.3 %collective-permute-done.12 = f32[8,1024]{1,0:T(8,128)S(1)} collective-permute-done((f32[8,1024]{1,0:T(8,128)S(1)}, f32[8,1024]{1,0:T(8,128)S(1)}, u32[]{:S(2)}, u32[]{:S(2)}) %collective-permute-start.12) | collective-permute-done | bytes 32800 | tf_op jit(solution)/shard_map/ppermute | solution.py:30
  59.7 0.6 %add_convert_fusion = bf16[8,1024]{1,0:T(8,128)(2,1)} fusion(f32[8,1024]{1,0:T(8,128)S(1)} %collective-permute-done.12, f32[8,1024]{1,0:T(8,128)S(1)} %collective-permute-done.11, f32[8,1024]{1,0:T(8,128)S(1)} %get-tuple-element.41, f32[8,1024]{1,0:T(8,128)S(1)} %collective-permute-done.10), kind=kLoop, calls=%fused_computation | loop fusion | flops 32768 | bytes 147456 | tf_op jit(solution)/shard_map/convert_element_type | solution.py:505
  (3 shorter events, 0.1 us)
Async XLA Ops:
  4.8 12.1 %collective-permute-start = (bf16[8,3200]{1,0:T(8,128)(2,1)S(1)}, bf16[8,3200]{1,0:T(8,128)(2,1)S(1)}, u32[]{:S(2)}, u32[]{:S(2)}) collective-permute-start(bf16[8,3200]{1,0:T(8,128)(2,1)S(1)} %get-tuple-element.25.after.b0), channel_id=1, source_target_pairs={{0,4},{4,0},{8,12},{12,8},{1,5},{5,1},{9,13},{13,9},{2,6},{6,2},{1... | collective-permute-start | bytes 153608 | tf_op jit(solution)/shard_map/ppermute | solution.py:30
  7.9 9.1 %collective-permute-start.1 = (bf16[8,3200]{1,0:T(8,128)(2,1)S(1)}, bf16[8,3200]{1,0:T(8,128)(2,1)S(1)}, u32[]{:S(2)}, u32[]{:S(2)}) collective-permute-start(bf16[8,3200]{1,0:T(8,128)(2,1)S(1)} %get-tuple-element.25.after.b0), channel_id=1, source_target_pairs={{0,8},{4,12},{8,0},{12,4},{1,9},{5,13},{9,1},{13,5},{2,10},{6,14},... | collective-permute-start | bytes 153608 | tf_op jit(solution)/shard_map/ppermute | solution.py:30
  10.4 6.5 %collective-permute-start.2 = (bf16[8,3200]{1,0:T(8,128)(2,1)S(1)}, bf16[8,3200]{1,0:T(8,128)(2,1)S(1)}, u32[]{:S(2)}, u32[]{:S(2)}) collective-permute-start(bf16[8,3200]{1,0:T(8,128)(2,1)S(1)} %get-tuple-element.25.after.b0), channel_id=1, source_target_pairs={{0,12},{4,8},{8,4},{12,0},{1,13},{5,9},{9,5},{13,1},{2,14},{6,10},... | collective-permute-start | bytes 153608 | tf_op jit(solution)/shard_map/ppermute | solution.py:30
  18.7 1.4 %collective-permute-start.3 = (f32[32,1024]{1,0:T(8,128)S(1)}, f32[32,1024]{1,0:T(8,128)S(1)}, u32[]{:S(2)}, u32[]{:S(2)}) collective-permute-start(f32[32,1024]{1,0:T(8,128)S(1)} %get-tuple-element.28.a), channel_id=1, source_target_pairs={{0,1},{1,0},{2,3},{3,2},{4,5},{5,4},{6,7},{7,6},{8,9},{9,8},{10,11... | collective-permute-start | bytes 393224 | tf_op jit(solution)/shard_map/ppermute | solution.py:30
  20.2 6.4 %collective-permute-start.4 = (f32[32,1024]{1,0:T(8,128)S(1)}, f32[32,1024]{1,0:T(8,128)S(1)}, u32[]{:S(2)}, u32[]{:S(2)}) collective-permute-start(f32[32,1024]{1,0:T(8,128)S(1)} %add.16.after.a), channel_id=1, source_target_pairs={{0,2},{1,3},{2,0},{3,1},{4,6},{5,7},{6,4},{7,5},{8,10},{9,11},{10,... | collective-permute-start | bytes 393224 | tf_op jit(solution)/shard_map/ppermute | solution.py:30
  26.6 7.3 %collective-permute-start.7 = (bf16[32,1152]{1,0:T(8,128)(2,1)S(1)}, bf16[32,1152]{1,0:T(8,128)(2,1)S(1)}, u32[]{:S(2)}, u32[]{:S(2)}) collective-permute-start(bf16[32,1152]{1,0:T(8,128)(2,1)S(1)} %get-tuple-element.29.packed.p0), channel_id=1, source_target_pairs={{0,4},{4,0},{8,12},{12,8},{1,5},{5,1},{9,13},{13,9},{2,6},{6,2},{1... | collective-permute-start | bytes 221192 | tf_op jit(solution)/shard_map/ppermute | solution.py:30
  27.4 9.3 %collective-permute-start.6 = (bf16[32,1152]{1,0:T(8,128)(2,1)S(1)}, bf16[32,1152]{1,0:T(8,128)(2,1)S(1)}, u32[]{:S(2)}, u32[]{:S(2)}) collective-permute-start(bf16[32,1152]{1,0:T(8,128)(2,1)S(1)} %get-tuple-element.29.packed.p0), channel_id=1, source_target_pairs={{0,8},{4,12},{8,0},{12,4},{1,9},{5,13},{9,1},{13,5},{2,10},{6,14},... | collective-permute-start | bytes 221192 | tf_op jit(solution)/shard_map/ppermute | solution.py:30
  30.9 7.8 %collective-permute-start.5 = (bf16[32,1152]{1,0:T(8,128)(2,1)S(1)}, bf16[32,1152]{1,0:T(8,128)(2,1)S(1)}, u32[]{:S(2)}, u32[]{:S(2)}) collective-permute-start(bf16[32,1152]{1,0:T(8,128)(2,1)S(1)} %get-tuple-element.29.packed.p0), channel_id=1, source_target_pairs={{0,12},{4,8},{8,4},{12,0},{1,13},{5,9},{9,5},{13,1},{2,14},{6,10},... | collective-permute-start | bytes 221192 | tf_op jit(solution)/shard_map/ppermute | solution.py:30
  43.2 5.0 %collective-permute-start.8 = (bf16[32,2048]{1,0:T(8,128)(2,1)S(1)}, bf16[32,2048]{1,0:T(8,128)(2,1)S(1)}, u32[]{:S(2)}, u32[]{:S(2)}) collective-permute-start(bf16[32,2048]{1,0:T(8,128)(2,1)S(1)} %leave_away.1.unused), channel_id=1, source_target_pairs={{0,2},{1,3},{2,0},{3,1},{4,6},{5,7},{6,4},{7,5},{8,10},{9,11},{10,... | collective-permute-start | bytes 393224 | tf_op jit(solution)/shard_map/ppermute | solution.py:30
  48.3 1.4 %collective-permute-start.9 = (f32[32,1024]{1,0:T(8,128)S(1)}, f32[32,1024]{1,0:T(8,128)S(1)}, u32[]{:S(2)}, u32[]{:S(2)}) collective-permute-start(f32[32,1024]{1,0:T(8,128)S(1)} %get-tuple-element.39), channel_id=1, source_target_pairs={{0,1},{1,0},{2,3},{3,2},{4,5},{5,4},{6,7},{7,6},{8,9},{9,8},{10,11... | collective-permute-start | bytes 393224 | tf_op jit(solution)/shard_map/ppermute | solution.py:30
  49.7 4.5 %collective-permute-start.10 = (f32[8,1024]{1,0:T(8,128)S(1)}, f32[8,1024]{1,0:T(8,128)S(1)}, u32[]{:S(2)}, u32[]{:S(2)}) collective-permute-start(f32[8,1024]{1,0:T(8,128)S(1)} %get-tuple-element.42), channel_id=1, source_target_pairs={{0,4},{4,0},{8,12},{12,8},{1,5},{5,1},{9,13},{13,9},{2,6},{6,2},{1... | collective-permute-start | bytes 98312 | tf_op jit(solution)/shard_map/ppermute | solution.py:30
  50.1 6.2 %collective-permute-start.11 = (f32[8,1024]{1,0:T(8,128)S(1)}, f32[8,1024]{1,0:T(8,128)S(1)}, u32[]{:S(2)}, u32[]{:S(2)}) collective-permute-start(f32[8,1024]{1,0:T(8,128)S(1)} %get-tuple-element.43), channel_id=1, source_target_pairs={{0,8},{4,12},{8,0},{12,4},{1,9},{5,13},{9,1},{13,5},{2,10},{6,14},... | collective-permute-start | bytes 98312 | tf_op jit(solution)/shard_map/ppermute | solution.py:30
  54.0 5.7 %collective-permute-start.12 = (f32[8,1024]{1,0:T(8,128)S(1)}, f32[8,1024]{1,0:T(8,128)S(1)}, u32[]{:S(2)}, u32[]{:S(2)}) collective-permute-start(f32[8,1024]{1,0:T(8,128)S(1)} %get-tuple-element.44), channel_id=1, source_target_pairs={{0,12},{4,8},{8,4},{12,0},{1,13},{5,9},{9,5},{13,1},{2,14},{6,10},... | collective-permute-start | bytes 98312 | tf_op jit(solution)/shard_map/ppermute | solution.py:30

commit v3 on v0

--- a/solution.py
+++ b/solution.py
@@ -1,8 +1,11 @@
+import functools
 import math
 
 import jax
 import jax.numpy as jnp
 from jax import lax
+from jax.experimental import pallas as pl
+from jax.experimental.pallas import tpu as pltpu
 from jax.sharding import PartitionSpec as P
 
 D = 4096
@@ -13,6 +16,513 @@
 TOPK = 8
 CAP = 2
 CACHE_LENGTH = 256
+SIDE = 4
+BF16 = jnp.bfloat16
+F32 = jnp.float32
+MIB = 1 << 20
+HERE = pl.BlockSpec(memory_space=pltpu.VMEM)
+SCALARS = pl.BlockSpec(memory_space=pltpu.SMEM)
+ANYWHERE = pl.BlockSpec(memory_space=pl.ANY)
+DMA = pltpu.SemaphoreType.DMA
+
+
+def swap(block, axis, k):
+    return lax.ppermute(block, axis, [(i, i ^ k) for i in range(SIDE)])
+
+
+def far(array):
+    return pltpu.with_memory_space_constraint(array, pltpu.HBM)
+
+
+def split3(value):
+    high = value.astype(BF16)
+    rest = value - high.astype(F32)
+    middle = rest.astype(BF16)
+    low = (rest - middle.astype(F32)).astype(BF16)
+    return high, middle, low
+
+
+def hosted(body, inputs, outputs, loads):
+    n = len(loads)
+
+    def kernel(*refs):
+        sources = refs[inputs : inputs + n]
+        targets = refs[inputs + n + outputs : inputs + n + outputs + n]
+        ins, outs = refs[:inputs], refs[inputs + n : inputs + n + outputs]
+        copies = []
+        for i, (load, source, target) in enumerate(zip(loads, sources, targets)):
+            _, first, count, place = load
+            width = target.shape[2]
+            columns = pl.ds(pl.multiple_of(place() * width, width), width)
+            source = source.at[pl.ds(first, count), :, columns]
+            copies.append(pltpu.make_async_copy(source, target, refs[-1].at[i]))
+        begin = lambda: [copy.start() for copy in copies]
+        rest = refs[inputs + outputs + 2 * n : -1]
+        if body is attention_kernel:
+            body(*ins, *outs, *rest, begin)
+        else:
+            begin()
+            body(*ins, *outs, *rest)
+        for copy in copies:
+            copy.wait()
+
+    return kernel
+
+
+def kernel_call(
+    body, name, args, specs, outs, scratch=(), loads=(), parts=1, limit=4, cost=(0, 0, 0), aliases=None
+):
+    targets = [
+        pltpu.VMEM((count, array.shape[1], array.shape[2] // part), BF16)
+        for (array, _, count, _), part in zip(loads, parts if loads else ())
+    ]
+    flops, bytes_accessed, transcendentals = cost
+    bytes_accessed += sum(2 * math.prod(target.shape) for target in targets)
+    results = pl.pallas_call(
+        hosted(body, len(args), len(outs), loads) if loads else body,
+        out_shape=(*outs, *targets),
+        in_specs=[*specs] + [ANYWHERE] * len(loads),
+        out_specs=(HERE,) * (len(outs) + len(targets)),
+        scratch_shapes=[*scratch] + ([DMA((len(loads),))] if loads else []),
+        input_output_aliases=aliases or {},
+        compiler_params=pltpu.CompilerParams(vmem_limit_bytes=limit * MIB),
+        cost_estimate=pl.CostEstimate(
+            flops=flops, bytes_accessed=bytes_accessed, transcendentals=transcendentals
+        ),
+        name=name,
+    )(*args, *(far(array) for array, *_ in loads))
+    return results[: len(outs)], results[len(outs) :]
+
+
+class Loads:
+    def __init__(self, entry, leave):
+        self.entry, self.leave = entry, leave
+        self.near = {}
+
+    def call(self, body, name, args, specs, outs, pieces=(), **more):
+        loads, parts = [], []
+        for what, which, first, count in pieces:
+            if what == "entry":
+                loads.append((self.entry, first, count, functools.partial(self.block, which)))
+                parts.append(SIDE)
+            else:
+                loads.append((self.leave, first, count, functools.partial(self.half, which)))
+                parts.append(2)
+        results, arrays = kernel_call(
+            body, name, args, specs, outs, loads=tuple(loads), parts=parts, **more
+        )
+        for (what, which, _, _), array in zip(pieces, arrays):
+            self.near.setdefault((what, which), []).append(array)
+        return results
+
+    @staticmethod
+    def block(k):
+        return lax.axis_index("ep") ^ k
+
+    @staticmethod
+    def half(other):
+        return (lax.axis_index("hd") // 2) ^ other
+
+
+def shaped(shape, dtype=F32):
+    return jax.ShapeDtypeStruct(shape, dtype)
+
+
+def attention_kernel(
+    lengths_far,
+    queries_far,
+    cache_far,
+    ids_far,
+    route_far,
+    residual_far,
+    weight_far,
+    out,
+    weight,
+    lengths,
+    queries,
+    cache,
+    ids,
+    route,
+    residual,
+    staged,
+    gathered,
+    sems,
+    begin,
+):
+    pairs = (
+        (lengths_far, lengths),
+        (queries_far, queries),
+        (cache_far, cache),
+        (ids_far, ids),
+        (route_far, route),
+        (residual_far, residual),
+        (weight_far, weight),
+    )
+    copies = [pltpu.make_async_copy(*pair, sems.at[i]) for i, pair in enumerate(pairs)]
+    for copy in copies:
+        copy.start()
+    begin()
+    rows = queries.shape[0]
+    heads = queries.shape[1] // HEAD_SIZE
+    everyone = rows * heads
+    copies[1].wait()
+    for h in range(heads):
+        lanes = slice(h * HEAD_SIZE, (h + 1) * HEAD_SIZE)
+        staged[pl.ds(h, rows, stride=heads), :] = queries[:, lanes].astype(F32)
+    turned = staged[...].T.astype(BF16)
+    copies[0].wait()
+    slot = lax.broadcasted_iota(jnp.int32, (1, everyone), 1) // heads
+    limit = jnp.zeros((1, everyone), jnp.int32)
+    for s in range(rows):
+        limit = jnp.where(slot == s, 2 * lengths[s], limit)
+    place = lax.broadcasted_iota(jnp.int32, (2 * CACHE_LENGTH, everyone), 0)
+    visible = jnp.logical_and(place % 2 == 0, place < limit)
+    copies[2].wait()
+    scores = jnp.dot(cache[0], turned, preferred_element_type=F32)
+    for s in range(1, rows):
+        more = jnp.dot(cache[s], turned, preferred_element_type=F32)
+        scores = jnp.where(slot == s, more, scores)
+    scores = jnp.where(visible, scores * (1.0 / math.sqrt(HEAD_SIZE)), -1e30)
+    raised = jnp.where(visible, jnp.exp(scores - jnp.max(scores, axis=0, keepdims=True)), 0.0)
+    weights = raised / jnp.sum(raised, axis=0, keepdims=True)
+    moved = pltpu.roll(weights, 1, 0).T.astype(BF16)
+    for s in range(rows):
+        span = slice(s * heads, (s + 1) * heads)
+        gathered[span, :] = jnp.dot(moved[span], cache[s], preferred_element_type=F32)
+    width = heads * HEAD_SIZE
+    for h in range(heads):
+        lanes = slice(h * HEAD_SIZE, (h + 1) * HEAD_SIZE)
+        out[:, lanes] = gathered[pl.ds(h, rows, stride=heads), :].astype(BF16)
+    copies[3].wait()
+    copies[4].wait()
+    row = lax.broadcasted_iota(jnp.int32, (TOPK, 128), 0)
+    lane = lax.broadcasted_iota(jnp.int32, (TOPK, 128), 1)
+    total = jnp.zeros((rows, 128), F32)
+    for j, part in enumerate((ids[...].astype(F32).astype(BF16), *split3(route[...]))):
+        spread = (lane == row + j * TOPK).astype(F32).astype(BF16)
+        total = total + jnp.dot(part, spread, preferred_element_type=F32)
+    out[:, width : width + 128] = total.astype(BF16)
+    copies[5].wait()
+    out[:, width + 128 :] = residual[...]
+    copies[6].wait()
+
+
+def attention(loads, pieces, lengths, queries, cache, ids, route, residual, weight):
+    rows, width = queries.shape
+    staged = pltpu.VMEM((rows * width // HEAD_SIZE, HEAD_SIZE), F32)
+    return loads.call(
+        attention_kernel,
+        "attention",
+        tuple(map(far, (lengths, queries, cache, ids, route, residual, weight))),
+        [ANYWHERE] * 7,
+        (shaped((rows, width + 128 + residual.shape[1]), BF16), pltpu.VMEM(weight.shape, BF16)),
+        pieces,
+        scratch=[
+            pltpu.SMEM(lengths.shape, jnp.int32),
+            pltpu.VMEM(queries.shape, BF16),
+            pltpu.VMEM(cache.shape, BF16),
+            pltpu.VMEM(ids.shape, jnp.int32),
+            pltpu.VMEM(route.shape, F32),
+            pltpu.VMEM(residual.shape, BF16),
+            staged,
+            staged,
+            DMA((7,)),
+        ],
+        cost=(140_000_000, 12_000_000, 65536),
+    )
+
+
+def fetch_kernel(after, mark):
+    del after
+    mark[...] = jnp.zeros_like(mark)
+
+
+def fetch(loads, pieces, name, after):
+    return loads.call(
+        fetch_kernel, name, (after,), [ANYWHERE], (shaped((8, 128)),), pieces, limit=1
+    )[0]
+
+
+def projection_kernel(slot_far, b0, b1, b2, b3, weight, unused, out, routing, slot_of, kept, sem):
+    del unused
+    copy = pltpu.make_async_copy(slot_far, slot_of, sem)
+    copy.start()
+    blocks = (b0, b1, b2, b3)
+    rows = b0.shape[0]
+    width = weight.shape[0]
+    everyone = SIDE * rows
+    me = lax.axis_index("ep")
+    held = jnp.concatenate([b[:, :width].astype(F32) for b in blocks], axis=0).astype(BF16)
+    row = lax.broadcasted_iota(jnp.int32, (everyone, everyone), 0)
+    column = lax.broadcasted_iota(jnp.int32, (everyone, everyone), 1)
+    wanted = jnp.zeros((everyone, everyone), jnp.int32)
+    for k, block in enumerate(blocks):
+        span = pl.ds(pl.multiple_of((me ^ k) * rows, rows), rows)
+        routing[span, :] = block[:, width : width + 128].astype(F32)
+        kept[span, :] = block[:, width + 128 :].astype(F32)
+    copy.wait()
+    for r in range(everyone):
+        slot = slot_of[r]
+        wanted = jnp.where(row == r, ((slot // rows) ^ me) * rows + slot % rows, wanted)
+    order = (wanted == column).astype(F32).astype(BF16)
+    ordered = jnp.dot(order, held, preferred_element_type=F32).astype(BF16)
+    own = (me == lax.axis_index("hd")).astype(F32)
+    out[...] = jnp.dot(ordered, weight[...], preferred_element_type=F32) + own * kept[...]
+
+
+def projection(loads, pieces, slot_of, blocks, weight, unused):
+    everyone = SIDE * blocks[0].shape[0]
+    wide = (everyone, weight.shape[1])
+    return loads.call(
+        projection_kernel,
+        "projection",
+        (far(slot_of), *blocks, weight, unused),
+        [ANYWHERE] + [HERE] * 5 + [ANYWHERE],
+        (shaped(wide), shaped((everyone, 128))),
+        pieces,
+        scratch=[pltpu.SMEM(slot_of.shape, jnp.int32), pltpu.VMEM(wide, F32), DMA],
+        limit=6,
+        cost=(140_000_000, 4_500_000, 0),
+    )
+
+
+def add_kernel(a, b, out):
+    out[...] = a[...] + b[...]
+
+
+def add(a, b):
+    outs = (shaped(a.shape),)
+    return kernel_call(add_kernel, "add", (a, b), [HERE] * 2, outs, cost=(a.size, a.size, 0))[0][0]
+
+
+def stream_kernel(a, b, unused, stream, packed):
+    del unused
+    total = a[...] + b[...]
+    stream[...] = total
+    width = total.shape[1]
+    packed[:, :width] = total.astype(BF16)
+    squares = jnp.sum(total * total, axis=1, keepdims=True)
+    lane = lax.broadcasted_iota(jnp.int32, (total.shape[0], 128), 1)
+    parts = [part.astype(F32) for part in split3(jnp.broadcast_to(squares, lane.shape))]
+    spread = jnp.where(lane == 0, parts[0], jnp.where(lane == 1, parts[1], parts[2]))
+    packed[:, width:] = jnp.where(lane < 3, spread, 0.0).astype(BF16)
+
+
+def streams(a, b, unused):
+    rows, width = a.shape
+    outs = (shaped(a.shape), shaped((rows, width + 128), BF16))
+    return kernel_call(
+        stream_kernel,
+        "stream",
+        (a, b, unused),
+        [HERE, HERE, ANYWHERE],
+        outs,
+        cost=(a.size * 4, a.size * 4, 0),
+    )[0]
+
+
+def entry_kernel(k, n, packed, *refs):
+    near, before, out = refs[:n], refs[n] if k else None, refs[-1]
+    width = near[0].shape[2]
+    turned = packed[:, :width].astype(F32).T.astype(BF16)
+    at = 0
+    for array in near:
+        for e in range(array.shape[0]):
+            part = jnp.dot(array[e], turned, preferred_element_type=F32)
+            span = slice(at, at + part.shape[0])
+            out[span, :] = before[span, :] + part if k else part
+            at = span.stop
+
+
+def entry_last_kernel(n, packed, *refs):
+    near, (before, routing, p0, p1, p2, out) = refs[:n], refs[n:]
+    hidden, width = near[0].shape[1:]
+    rows = packed.shape[0]
+    turned = packed[:, :width].astype(F32).T.astype(BF16)
+    squares = jnp.zeros((rows, 128), F32)
+    for block in (p0, p1, p2, packed):
+        squares = squares + block[:, width:].astype(F32)
+    mean = jnp.sum(squares.T, axis=0, keepdims=True) / (SIDE * width)
+    scale = lax.rsqrt(mean + 1e-06)
+    table = routing[...].T
+    ids = table[0:TOPK, :]
+    weight = table[TOPK : 2 * TOPK, :] + table[2 * TOPK : 3 * TOPK, :]
+    weight = weight + table[3 * TOPK : 4 * TOPK, :]
+    base = lax.axis_index("ep") * (before.shape[0] // hidden)
+    number = 0
+    pair = []
+    for array in near:
+        for e in range(array.shape[0]):
+            at = number * hidden
+            chosen = ids == (base + number).astype(F32)
+            share = jnp.sum(jnp.where(chosen, weight, 0.0), axis=0, keepdims=True)
+            part = jnp.dot(array[e], turned, preferred_element_type=F32)
+            total = (before[at : at + hidden, :] + part) * scale
+            active = (total / (1.0 + jnp.exp(-total))).astype(BF16).astype(F32) * share
+            high = active.astype(BF16).astype(F32)
+            pair.append(jnp.concatenate([high, active - high], axis=1))
+            number += 1
+            if len(pair) == 2:
+                end = number * hidden
+                both = jnp.concatenate(pair, axis=0)
+                out[:, end - 2 * hidden : end] = both.T.astype(BF16)
+                pair = []
+
+
+def entries(loads, plan, packs, routing):
+    count, hidden, width = loads.leave.shape
+    rows = packs[0].shape[0]
+    cost = (2 * rows * count * hidden * width // SIDE, 2 * count * hidden * width // SIDE, 0)
+    total = None
+    for k in range(SIDE):
+        near = tuple(loads.near["entry", k])
+        args = (packs[k], *near) + ((total,) if k else ())
+        n = len(near)
+        if k < SIDE - 1:
+            body = functools.partial(entry_kernel, k, n)
+            outs = (shaped((count * hidden, rows)),)
+            aliases = {n + 1: 0} if k else None
+        else:
+            args += (routing, *packs[:-1])
+            body = functools.partial(entry_last_kernel, n)
+            outs = (shaped((2 * rows, count * hidden), BF16),)
+            aliases = None
+        (total,) = loads.call(
+            body,
+            f"entry{k}",
+            args,
+            [HERE] * len(args),
+            outs,
+            plan.get(f"entry{k}", ()),
+            cost=cost,
+            aliases=aliases,
+        )
+    return total
+
+
+def leave_kernel(n, step, scaled, *refs):
+    near, out = refs[:n], refs[-1]
+    rows, count = out.shape
+    for c in range(0, count, step):
+        total = jnp.zeros((2 * rows, step), F32)
+        at = 0
+        for array in near:
+            depth = array.shape[0] * array.shape[1]
+            flat = array.reshape(depth, array.shape[2])
+            total = total + jnp.dot(
+                scaled[:, at : at + depth], flat[:, c : c + step], preferred_element_type=F32
+            )
+            at += depth
+        out[:, c : c + step] = (total[:rows] + total[rows:]).astype(out.dtype)
+
+
+def leaves(loads, pieces, name, other, dtype, scaled, unused):
+    near = tuple(loads.near["leave", other])
+    count, hidden, width = loads.leave.shape
+    rows = scaled.shape[0] // 2
+    return loads.call(
+        functools.partial(leave_kernel, len(near), 1024),
+        name,
+        (scaled, *near, unused),
+        [HERE] * (1 + len(near)) + [ANYWHERE],
+        (shaped((rows, width // 2), dtype),),
+        pieces,
+        cost=(2 * rows * count * hidden * width, count * hidden * width, 0),
+        limit=6,
+    )[0]
+
+
+def halve_kernel(mine, received, keep, send):
+    width = keep.shape[1]
+    core = lax.axis_index("hd") % 2
+    for out, which in ((send, 1 - core), (keep, core)):
+        columns = pl.ds(pl.multiple_of(which * width, width), width)
+        out[...] = mine[:, columns] + received[:, columns].astype(F32)
+
+
+def halve(mine, received):
+    rows, width = mine.shape
+    outs = (shaped((rows, width // 2)),) * 2
+    cost = (mine.size, mine.size * 6, 0)
+    return kernel_call(halve_kernel, "halve", (mine, received), [HERE] * 2, outs, cost=cost)[0]
+
+
+def share_kernel(own, received, stream, o0, o1, o2, o3):
+    rows = o0.shape[0]
+    me = lax.axis_index("ep")
+    here = (me == lax.axis_index("hd")).astype(F32)
+    for k, out in enumerate((o0, o1, o2, o3)):
+        span = pl.ds(pl.multiple_of((me ^ k) * rows, rows), rows)
+        out[...] = own[span, :] + received[span, :] + here * stream[span, :]
+
+
+def share(own, received, stream):
+    rows, width = own.shape
+    outs = (shaped((rows // SIDE, width)),) * SIDE
+    cost = (own.size * 3, own.size * 16, 0)
+    args = (own, received, stream)
+    return kernel_call(share_kernel, "share", args, [HERE] * 3, outs, cost=cost)[0]
+
+
+def plan_of(count):
+    half, quarter = count // 2, count // 4
+    cut = (count // 8, half, count * 3 // 8, count * 3 // 8)
+    return {
+        "attention": [("entry", 0, 0, half)],
+        "fetch0": [("entry", 0, half, half), ("entry", 1, 0, count)],
+        "projection": [("entry", 2, 0, half)],
+        "fetch1": [("entry", 2, half, half), ("entry", 3, 0, half)],
+        "entry0": [("entry", 3, half, half), ("leave", 1, 0, cut[0])],
+        "entry1": [("leave", 1, cut[0], cut[2])],
+        "entry2": [("leave", 1, cut[0] + cut[2], count - cut[0] - cut[2])],
+        "entry3": [("leave", 0, 0, cut[3])],
+        "leave1": [("leave", 0, cut[3], count - cut[3])],
+    }
+
+
+def square_body(
+    residual,
+    queries,
+    key_value_cache,
+    lengths,
+    slot_of,
+    out_weight,
+    expert_ids,
+    route_weight,
+    in_weight,
+    down_weight,
+):
+    rows = queries.shape[0]
+    cache = key_value_cache.reshape(rows, 2 * CACHE_LENGTH, HEAD_SIZE)
+    loads = Loads(jnp.swapaxes(in_weight, 1, 2), down_weight)
+    plan = plan_of(down_weight.shape[0])
+    attended, weight = attention(
+        loads,
+        plan["attention"],
+        lengths,
+        queries,
+        cache,
+        expert_ids,
+        route_weight,
+        residual,
+        out_weight,
+    )
+    blocks = [attended] + [swap(attended, "ep", k) for k in (1, 2, 3)]
+    mark = fetch(loads, plan["fetch0"], "fetch0", attended)
+    partial_value, routing = projection(loads, plan["projection"], slot_of, blocks, weight, mark)
+    pair = add(partial_value, swap(partial_value, "hd", 1))
+    far_pair = swap(pair, "hd", 2)
+    mark = fetch(loads, plan["fetch1"], "fetch1", pair)
+    stream, packed = streams(pair, far_pair, mark)
+    packs = [packed] + [swap(packed, "ep", k) for k in (1, 2, 3)]
+    scaled = entries(loads, plan, packs, routing)
+    theirs = leaves(loads, plan["leave1"], "leave1", 1, BF16, scaled, scaled)
+    mine = leaves(loads, (), "leave0", 0, F32, scaled, theirs)
+    keep, send = halve(mine, swap(theirs, "hd", 2))
+    total, *others = share(keep, swap(send, "hd", 1), stream)
+    for k, block in enumerate(others):
+        total = total + swap(block, "ep", k + 1)
+    return total.astype(BF16)
 
 
 def expert_pass(block, in_weight, down_weight):
@@ -120,4 +630,5 @@
         P("ep", "hd", None),
     )
     out_specs = P(("groups", "ep"), "hd")
-    return jax.shard_map(body, mesh=mesh, in_specs=in_specs, out_specs=out_specs, check_vma=False)
+    chosen = square_body if mesh.shape["ep"] == mesh.shape["hd"] == SIDE else body
+    return jax.shard_map(chosen, mesh=mesh, in_specs=in_specs, out_specs=out_specs, check_vma=False)

time: 177 us -> 67.1 us (0.38)
  blocking collectives: 56.9 us -> 0 us
  waiting for transfers between devices: 55.4 us -> 10.7 us
  Pallas kernels: 0 us -> 37.5 us
  matrix products: 25.8 us -> 0 us
  between operations: 13.5 us -> 0.16 us
  local copies, waits for them, and re-layouts: 9.82 us -> 0 us
  starting transfers between devices: 9.62 us -> 17.9 us
  other arithmetic: 4.85 us -> 0.62 us
    reduce_scatter x2 -> x0, waiting for transfers between devices: 41.8 us -> none  [the longest x1 23.3 us: body(): lax.psum_scatter(results.astype(jnp.bfloat16), 'hd', scatter_dimension=2,...]
    pallas_call x0 -> x14, Pallas kernels: none -> 37.5 us  [kernel_call(): pl.pallas_call(hosted(body, len(args), len(outs), loads) if loads else bo...]
    all_to_all x1 -> x0, blocking collectives: 30.8 us -> none  [body(): lax.all_to_all(outgoing, 'ep', split_axis=0, concat_axis=0, tiled=True)]
    dot_general x7 -> x0, matrix products: 24.6 us -> none  [the longest x1 19.5 us: expert_pass(): jnp.einsum('secf,efd->secd', hidden, down_weight, preferred_element_type=...]
    all_gather x2 -> x0, blocking collectives: 20.3 us -> none  [the longest x1 15.1 us: body(): lax.all_gather(attended, 'ep', axis=0, tiled=True)]
    ppermute x0 -> x13, starting transfers between devices: none -> 17.9 us  [swap(): return lax.ppermute(block, axis, [(i, i ^ k) for i in range(SIDE)])]
    all_to_all x2 -> x0, waiting for transfers between devices: 13.6 us -> none  [the longest x1 8.59 us: body(): lax.all_to_all(shares, 'ep', split_axis=0, concat_axis=0, tiled=True)]
    ppermute x0 -> x13, waiting for transfers between devices: none -> 10.7 us  [swap(): return lax.ppermute(block, axis, [(i, i ^ k) for i in range(SIDE)])]
  transfers between devices with their start and end apart: 4 -> 13, of which waited for: 4 -> 7; matrix products, arithmetic and copies ran while one was open for 1% -> 0% of each run, Pallas kernels for 0% -> 33%
where the time goes in v3:
time: 67.1 us; the launch traced here: 66.9 us
  Pallas kernels  37.5 us (56%)
  starting transfers between devices  17.9 us (27%)
  waiting for transfers between devices  10.7 us (16%)
    pallas_call x14, Pallas kernels, kernel_call(): pl.pallas_call(hosted(body, len(args), len(outs), loads) if loads else bo...  37.5 us
    ppermute x13, starting transfers between devices, swap(): return lax.ppermute(block, axis, [(i, i ^ k) for i in range(SIDE)])  17.9 us
    ppermute x13, waiting for transfers between devices, swap(): return lax.ppermute(block, axis, [(i, i ^ k) for i in range(SIDE)])  10.7 us
  transfers between devices with their start and end apart: 13, of which 7 were waited for; matrix products, arithmetic and copies ran while one was open for 0% of the time, Pallas kernels for 33%

profile of v3, /device:TPU:0, one launch (start us, length us, event | category | flops | bytes accessed | tf_op | source)
XLA Modules:
  0.0 66.9 jit_solution(16617595519160145240)
XLA Ops:
  0.0 3.6 %attention.1 = (bf16[8,3200]{1,0:T(8,128)(2,1)S(1)}, bf16[2048,1024]{1,0:T(8,128)(2,1)S(1)}, bf16[8,192,1024]{2,1,0:T(8,128)(2,1)S(1)}) custom-call(s32[8]{0:T(128)} %refs_0_.2, bf16[8,2048]{1,0:T(8,128)(2,1)} %refs_1_.1, bf16[8,512,128]{2,1,0:T(8,128)(2,1)} %bitcast.9, s32[8,8]{1,0:T(8,128)} %refs_3_.2, f32[8,8]{1,0:T(8,128)} %refs_4_.3, ...), custom_call_target="tpu_custom_call" | custom-call | flops 140000000 | bytes 15145728 | tf_op jit(solution)/shard_map/attention/pallas_call | solution.py:81
  3.6 5.1 %collective-permute-start.2 = (bf16[8,3200]{1,0:T(8,128)(2,1)S(1)}, bf16[8,3200]{1,0:T(8,128)(2,1)S(1)}, u32[]{:S(2)}, u32[]{:S(2)}) collective-permute-start(bf16[8,3200]{1,0:T(8,128)(2,1)S(1)} %get-tuple-element.36.refs_0_.refs_1_), channel_id=1, source_target_pairs={{0,12},{4,8},{8,4},{12,0},{1,13},{5,9},{9,5},{13,1},{2,14},{6,10},... | collective-permute-start | bytes 153608 | tf_op jit(solution)/shard_map/ppermute | solution.py:30
  8.7 0.0 collective-permute-start.1
  8.7 0.6 collective-permute-start
  9.4 3.8 %fetch0.1 = (f32[8,128]{1,0:T(8,128)S(1)}, bf16[8,192,1024]{2,1,0:T(8,128)(2,1)S(1)}, bf16[16,192,1024]{2,1,0:T(8,128)(2,1)S(1)}) custom-call(bf16[8,3200]{1,0:T(8,128)(2,1)S(1)} %get-tuple-element.36.refs_0_.refs_1_, bf16[16,192,4096]{2,1,0:T(8,128)(2,1)} %bitcast.3, bf16[16,192,4096]{2,1,0:T(8,128)(2,1)} %bitcast.4), custom_call_target="tpu_custom_call" | custom-call | bytes 9437184 | tf_op jit(solution)/shard_map/fetch0/pallas_call | solution.py:81
  13.1 0.0 collective-permute-done.2.refs_4_
  13.2 0.6 collective-permute-done.1.refs_3_
  13.7 0.0 collective-permute-done.refs_2_
  13.7 1.9 %projection.1 = (f32[32,1024]{1,0:T(8,128)S(1)}, f32[32,128]{1,0:T(8,128)S(1)}, bf16[8,192,1024]{2,1,0:T(8,128)(2,1)S(1)}) custom-call(s32[32]{0:T(128)} %refs_0_.3, bf16[8,3200]{1,0:T(8,128)(2,1)S(1)} %get-tuple-element.36.refs_0_.refs_1_, bf16[8,3200]{1,0:T(8,128)(2,1)S(1)} %collective-permute-done.refs_2_, ...), custom_call_target="tpu_custom_call" | custom-call | flops 140000000 | bytes 7645728 | tf_op jit(solution)/shard_map/projection/pallas_call | solution.py:81
  15.7 0.1 collective-permute-start.3
  15.8 1.3 %collective-permute-done.3.b = f32[32,1024]{1,0:T(8,128)S(1)} collective-permute-done((f32[32,1024]{1,0:T(8,128)S(1)}, f32[32,1024]{1,0:T(8,128)S(1)}, u32[]{:S(2)}, u32[]{:S(2)}) %collective-permute-start.3) | collective-permute-done | bytes 131104 | tf_op jit(solution)/shard_map/ppermute | solution.py:30
  17.1 1.6 %collective-permute-start.4 = (f32[32,1024]{1,0:T(8,128)S(1)}, f32[32,1024]{1,0:T(8,128)S(1)}, u32[]{:S(2)}, u32[]{:S(2)}) collective-permute-start(f32[32,1024]{1,0:T(8,128)S(1)} %add.16.refs_0_.a), channel_id=1, source_target_pairs={{0,2},{1,3},{2,0},{3,1},{4,6},{5,7},{6,4},{7,5},{8,10},{9,11},{10,... | collective-permute-start | bytes 393224 | tf_op jit(solution)/shard_map/ppermute | solution.py:30
  18.7 2.9 %fetch1.1 = (f32[8,128]{1,0:T(8,128)S(1)}, bf16[8,192,1024]{2,1,0:T(8,128)(2,1)S(1)}, bf16[8,192,1024]{2,1,0:T(8,128)(2,1)S(1)}) custom-call(f32[32,1024]{1,0:T(8,128)S(1)} %add.16.refs_0_.a, bf16[16,192,4096]{2,1,0:T(8,128)(2,1)} %bitcast.6, bf16[16,192,4096]{2,1,0:T(8,128)(2,1)} %bitcast.7), custom_call_target="tpu_custom_call" | custom-call | bytes 6291456 | tf_op jit(solution)/shard_map/fetch1/pallas_call | solution.py:81
  21.5 1.2 %collective-permute-done.4.b = f32[32,1024]{1,0:T(8,128)S(1)} collective-permute-done((f32[32,1024]{1,0:T(8,128)S(1)}, f32[32,1024]{1,0:T(8,128)S(1)}, u32[]{:S(2)}, u32[]{:S(2)}) %collective-permute-start.4) | collective-permute-done | bytes 131104 | tf_op jit(solution)/shard_map/ppermute | solution.py:30
  22.7 0.1 stream.1
  22.8 0.9 %collective-permute-start.7 = (bf16[32,1152]{1,0:T(8,128)(2,1)S(1)}, bf16[32,1152]{1,0:T(8,128)(2,1)S(1)}, u32[]{:S(2)}, u32[]{:S(2)}) collective-permute-start(bf16[32,1152]{1,0:T(8,128)(2,1)S(1)} %get-tuple-element.41.refs_0_.refs_5_), channel_id=1, source_target_pairs={{0,4},{4,0},{8,12},{12,8},{1,5},{5,1},{9,13},{13,9},{2,6},{6,2},{1... | collective-permute-start | bytes 221192 | tf_op jit(solution)/shard_map/ppermute | solution.py:30
  23.7 2.9 %collective-permute-start.6 = (bf16[32,1152]{1,0:T(8,128)(2,1)S(1)}, bf16[32,1152]{1,0:T(8,128)(2,1)S(1)}, u32[]{:S(2)}, u32[]{:S(2)}) collective-permute-start(bf16[32,1152]{1,0:T(8,128)(2,1)S(1)} %get-tuple-element.41.refs_0_.refs_5_), channel_id=1, source_target_pairs={{0,8},{4,12},{8,0},{12,4},{1,9},{5,13},{9,1},{13,5},{2,10},{6,14},... | collective-permute-start | bytes 221192 | tf_op jit(solution)/shard_map/ppermute | solution.py:30
  26.6 0.6 collective-permute-start.5
  27.3 4.2 %entry0.1 = (f32[3072,32]{1,0:T(8,128)S(1)}, bf16[8,192,1024]{2,1,0:T(8,128)(2,1)S(1)}, bf16[2,192,2048]{2,1,0:T(8,128)(2,1)S(1)}) custom-call(bf16[32,1152]{1,0:T(8,128)(2,1)S(1)} %get-tuple-element.41.refs_0_.refs_5_, bf16[8,192,1024]{2,1,0:T(8,128)(2,1)S(1)} %get-tuple-element.43.refs_1_, bf16[8,192,1024]{2,1,0:T(8,128)(2,1)S(1)} %get-tuple-element.44.refs_2_, ...), custom_call_target="tpu_custom_call" | custom-call | flops 201326592 | bytes 11010048 | tf_op jit(solution)/shard_map/entry0/pallas_call | solution.py:81
  31.5 0.0 collective-permute-done.7.refs_0_.refs_6_
  31.5 4.2 %entry1.1 = (f32[3072,32]{1,0:T(8,128)S(1)}, bf16[6,192,2048]{2,1,0:T(8,128)(2,1)S(1)}) custom-call(bf16[32,1152]{1,0:T(8,128)(2,1)S(1)} %collective-permute-done.7.refs_0_.refs_6_, bf16[16,192,1024]{2,1,0:T(8,128)(2,1)S(1)} %get-tuple-element.48.refs_1_, f32[3072,32]{1,0:T(8,128)S(1)} %get-tuple-element.49.refs_2_, ...), custom_call_target="tpu_custom_call", output_to_operand_aliasing={{0}: (2, {})} | custom-call | flops 201326592 | bytes 11010048 | tf_op jit(solution)/shard_map/entry1/pallas_call | solution.py:81
  35.7 0.0 collective-permute-done.6.refs_0_.refs_7_
  35.7 4.7 %entry2.1 = (f32[3072,32]{1,0:T(8,128)S(1)}, bf16[8,192,2048]{2,1,0:T(8,128)(2,1)S(1)}) custom-call(bf16[32,1152]{1,0:T(8,128)(2,1)S(1)} %collective-permute-done.6.refs_0_.refs_7_, bf16[8,192,1024]{2,1,0:T(8,128)(2,1)S(1)} %get-tuple-element.46.refs_1_, bf16[8,192,1024]{2,1,0:T(8,128)(2,1)S(1)} %get-tuple-element.47.refs_2_, ...), custom_call_target="tpu_custom_call", output_to_operand_aliasing={{0}: (3, {})} | custom-call | flops 201326592 | bytes 12582912 | tf_op jit(solution)/shard_map/entry2/pallas_call | solution.py:81
  40.4 0.0 collective-permute-done.5.refs_0_
  40.4 4.4 %entry3.1 = (bf16[64,3072]{1,0:T(8,128)(2,1)S(1)}, bf16[6,192,2048]{2,1,0:T(8,128)(2,1)S(1)}) custom-call(bf16[32,1152]{1,0:T(8,128)(2,1)S(1)} %collective-permute-done.5.refs_0_, bf16[8,192,1024]{2,1,0:T(8,128)(2,1)S(1)} %get-tuple-element.42.refs_1_, bf16[8,192,1024]{2,1,0:T(8,128)(2,1)S(1)} %get-tuple-element.45.refs_2_, ...), custom_call_target="tpu_custom_call" | custom-call | flops 201326592 | bytes 11010048 | tf_op jit(solution)/shard_map/entry3/pallas_call | solution.py:81
  44.8 5.4 %leave1.1 = (bf16[32,2048]{1,0:T(8,128)(2,1)S(1)}, bf16[10,192,2048]{2,1,0:T(8,128)(2,1)S(1)}) custom-call(bf16[64,3072]{1,0:T(8,128)(2,1)S(1)} %get-tuple-element.53.refs_0_.refs_4_.scaled, bf16[2,192,2048]{2,1,0:T(8,128)(2,1)S(1)} %get-tuple-element.55.refs_1_, bf16[6,192,2048]{2,1,0:T(8,128)(2,1)S(1)} %get-tuple-element.56.refs_2_, ...), custom_call_target="tpu_custom_call" | custom-call | flops 805306368 | bytes 20447232 | tf_op jit(solution)/shard_map/leave1/pallas_call | solution.py:81
  50.2 1.6 %collective-permute-start.8 = (bf16[32,2048]{1,0:T(8,128)(2,1)S(1)}, bf16[32,2048]{1,0:T(8,128)(2,1)S(1)}, u32[]{:S(2)}, u32[]{:S(2)}) collective-permute-start(bf16[32,2048]{1,0:T(8,128)(2,1)S(1)} %get-tuple-element.59.refs_2_), channel_id=1, source_target_pairs={{0,2},{1,3},{2,0},{3,1},{4,6},{5,7},{6,4},{7,5},{8,10},{9,11},{10,... | collective-permute-start | bytes 393224 | tf_op jit(solution)/shard_map/ppermute | solution.py:30
  51.8 2.3 %leave0.1.mine = f32[32,2048]{1,0:T(8,128)S(1)} custom-call(bf16[64,3072]{1,0:T(8,128)(2,1)S(1)} %get-tuple-element.53.refs_0_.refs_4_.scaled, bf16[6,192,2048]{2,1,0:T(8,128)(2,1)S(1)} %get-tuple-element.54.refs_0_, bf16[10,192,2048]{2,1,0:T(8,128)(2,1)S(1)} %get-tuple-element.58.refs_1_, bf16[32,2048]{1,0:T(8,128)(2,1)S(1)} %get-tuple-element.59.refs_2_), custom_call_target="tpu_custom_call" | custom-call | flops 805306368 | bytes 12582912 | tf_op jit(solution)/shard_map/leave0/pallas_call | solution.py:81
  54.1 1.2 %collective-permute-done.8.received = bf16[32,2048]{1,0:T(8,128)(2,1)S(1)} collective-permute-done((bf16[32,2048]{1,0:T(8,128)(2,1)S(1)}, bf16[32,2048]{1,0:T(8,128)(2,1)S(1)}, u32[]{:S(2)}, u32[]{:S(2)}) %collective-permute-start.8) | collective-permute-done | bytes 131104 | tf_op jit(solution)/shard_map/ppermute | solution.py:30
  55.3 0.1 collective-permute-start.9
  55.4 1.3 %collective-permute-done.9.received = f32[32,1024]{1,0:T(8,128)S(1)} collective-permute-done((f32[32,1024]{1,0:T(8,128)S(1)}, f32[32,1024]{1,0:T(8,128)S(1)}, u32[]{:S(2)}, u32[]{:S(2)}) %collective-permute-start.9) | collective-permute-done | bytes 131104 | tf_op jit(solution)/shard_map/ppermute | solution.py:30
  56.7 0.1 collective-permute-start.10
  56.8 3.7 %collective-permute-start.11 = (f32[8,1024]{1,0:T(8,128)S(1)}, f32[8,1024]{1,0:T(8,128)S(1)}, u32[]{:S(2)}, u32[]{:S(2)}) collective-permute-start(f32[8,1024]{1,0:T(8,128)S(1)} %get-tuple-element.65), channel_id=1, source_target_pairs={{0,8},{4,12},{8,0},{12,4},{1,9},{5,13},{9,1},{13,5},{2,10},{6,14},... | collective-permute-start | bytes 98312 | tf_op jit(solution)/shard_map/ppermute | solution.py:30
  60.5 0.6 collective-permute-start.12
  61.2 0.0 collective-permute-done.10
  61.2 1.4 %collective-permute-done.11 = f32[8,1024]{1,0:T(8,128)S(1)} collective-permute-done((f32[8,1024]{1,0:T(8,128)S(1)}, f32[8,1024]{1,0:T(8,128)S(1)}, u32[]{:S(2)}, u32[]{:S(2)}) %collective-permute-start.11) | collective-permute-done | bytes 32800 | tf_op jit(solution)/shard_map/ppermute | solution.py:30
  62.6 3.7 %collective-permute-done.12 = f32[8,1024]{1,0:T(8,128)S(1)} collective-permute-done((f32[8,1024]{1,0:T(8,128)S(1)}, f32[8,1024]{1,0:T(8,128)S(1)}, u32[]{:S(2)}, u32[]{:S(2)}) %collective-permute-start.12) | collective-permute-done | bytes 32800 | tf_op jit(solution)/shard_map/ppermute | solution.py:30
  66.3 0.6 add_convert_fusion
  (3 shorter events, 0.1 us)
Async XLA Ops:
  3.6 9.5 %collective-permute-start.2 = (bf16[8,3200]{1,0:T(8,128)(2,1)S(1)}, bf16[8,3200]{1,0:T(8,128)(2,1)S(1)}, u32[]{:S(2)}, u32[]{:S(2)}) collective-permute-start(bf16[8,3200]{1,0:T(8,128)(2,1)S(1)} %get-tuple-element.36.refs_0_.refs_1_), channel_id=1, source_target_pairs={{0,12},{4,8},{8,4},{12,0},{1,13},{5,9},{9,5},{13,1},{2,14},{6,10},... | collective-permute-start | bytes 153608 | tf_op jit(solution)/shard_map/ppermute | solution.py:30
  8.7 5.0 %collective-permute-start.1 = (bf16[8,3200]{1,0:T(8,128)(2,1)S(1)}, bf16[8,3200]{1,0:T(8,128)(2,1)S(1)}, u32[]{:S(2)}, u32[]{:S(2)}) collective-permute-start(bf16[8,3200]{1,0:T(8,128)(2,1)S(1)} %get-tuple-element.36.refs_0_.refs_1_), channel_id=1, source_target_pairs={{0,8},{4,12},{8,0},{12,4},{1,9},{5,13},{9,1},{13,5},{2,10},{6,14},... | collective-permute-start | bytes 153608 | tf_op jit(solution)/shard_map/ppermute | solution.py:30
  8.7 5.0 %collective-permute-start = (bf16[8,3200]{1,0:T(8,128)(2,1)S(1)}, bf16[8,3200]{1,0:T(8,128)(2,1)S(1)}, u32[]{:S(2)}, u32[]{:S(2)}) collective-permute-start(bf16[8,3200]{1,0:T(8,128)(2,1)S(1)} %get-tuple-element.36.refs_0_.refs_1_), channel_id=1, source_target_pairs={{0,4},{4,0},{8,12},{12,8},{1,5},{5,1},{9,13},{13,9},{2,6},{6,2},{1... | collective-permute-start | bytes 153608 | tf_op jit(solution)/shard_map/ppermute | solution.py:30
  15.7 1.4 %collective-permute-start.3 = (f32[32,1024]{1,0:T(8,128)S(1)}, f32[32,1024]{1,0:T(8,128)S(1)}, u32[]{:S(2)}, u32[]{:S(2)}) collective-permute-start(f32[32,1024]{1,0:T(8,128)S(1)} %get-tuple-element.39.a), channel_id=1, source_target_pairs={{0,1},{1,0},{2,3},{3,2},{4,5},{5,4},{6,7},{7,6},{8,9},{9,8},{10,11... | collective-permute-start | bytes 393224 | tf_op jit(solution)/shard_map/ppermute | solution.py:30
  17.1 5.6 %collective-permute-start.4 = (f32[32,1024]{1,0:T(8,128)S(1)}, f32[32,1024]{1,0:T(8,128)S(1)}, u32[]{:S(2)}, u32[]{:S(2)}) collective-permute-start(f32[32,1024]{1,0:T(8,128)S(1)} %add.16.refs_0_.a), channel_id=1, source_target_pairs={{0,2},{1,3},{2,0},{3,1},{4,6},{5,7},{6,4},{7,5},{8,10},{9,11},{10,... | collective-permute-start | bytes 393224 | tf_op jit(solution)/shard_map/ppermute | solution.py:30
  22.8 8.6 %collective-permute-start.7 = (bf16[32,1152]{1,0:T(8,128)(2,1)S(1)}, bf16[32,1152]{1,0:T(8,128)(2,1)S(1)}, u32[]{:S(2)}, u32[]{:S(2)}) collective-permute-start(bf16[32,1152]{1,0:T(8,128)(2,1)S(1)} %get-tuple-element.41.refs_0_.refs_5_), channel_id=1, source_target_pairs={{0,4},{4,0},{8,12},{12,8},{1,5},{5,1},{9,13},{13,9},{2,6},{6,2},{1... | collective-permute-start | bytes 221192 | tf_op jit(solution)/shard_map/ppermute | solution.py:30
  23.7 12.0 %collective-permute-start.6 = (bf16[32,1152]{1,0:T(8,128)(2,1)S(1)}, bf16[32,1152]{1,0:T(8,128)(2,1)S(1)}, u32[]{:S(2)}, u32[]{:S(2)}) collective-permute-start(bf16[32,1152]{1,0:T(8,128)(2,1)S(1)} %get-tuple-element.41.refs_0_.refs_5_), channel_id=1, source_target_pairs={{0,8},{4,12},{8,0},{12,4},{1,9},{5,13},{9,1},{13,5},{2,10},{6,14},... | collective-permute-start | bytes 221192 | tf_op jit(solution)/shard_map/ppermute | solution.py:30
  26.6 13.7 %collective-permute-start.5 = (bf16[32,1152]{1,0:T(8,128)(2,1)S(1)}, bf16[32,1152]{1,0:T(8,128)(2,1)S(1)}, u32[]{:S(2)}, u32[]{:S(2)}) collective-permute-start(bf16[32,1152]{1,0:T(8,128)(2,1)S(1)} %get-tuple-element.41.refs_0_.refs_5_), channel_id=1, source_target_pairs={{0,12},{4,8},{8,4},{12,0},{1,13},{5,9},{9,5},{13,1},{2,14},{6,10},... | collective-permute-start | bytes 221192 | tf_op jit(solution)/shard_map/ppermute | solution.py:30
  50.2 5.0 %collective-permute-start.8 = (bf16[32,2048]{1,0:T(8,128)(2,1)S(1)}, bf16[32,2048]{1,0:T(8,128)(2,1)S(1)}, u32[]{:S(2)}, u32[]{:S(2)}) collective-permute-start(bf16[32,2048]{1,0:T(8,128)(2,1)S(1)} %get-tuple-element.59.refs_2_), channel_id=1, source_target_pairs={{0,2},{1,3},{2,0},{3,1},{4,6},{5,7},{6,4},{7,5},{8,10},{9,11},{10,... | collective-permute-start | bytes 393224 | tf_op jit(solution)/shard_map/ppermute | solution.py:30
  55.3 1.4 %collective-permute-start.9 = (f32[32,1024]{1,0:T(8,128)S(1)}, f32[32,1024]{1,0:T(8,128)S(1)}, u32[]{:S(2)}, u32[]{:S(2)}) collective-permute-start(f32[32,1024]{1,0:T(8,128)S(1)} %get-tuple-element.61), channel_id=1, source_target_pairs={{0,1},{1,0},{2,3},{3,2},{4,5},{5,4},{6,7},{7,6},{8,9},{9,8},{10,11... | collective-permute-start | bytes 393224 | tf_op jit(solution)/shard_map/ppermute | solution.py:30
  56.7 4.5 %collective-permute-start.10 = (f32[8,1024]{1,0:T(8,128)S(1)}, f32[8,1024]{1,0:T(8,128)S(1)}, u32[]{:S(2)}, u32[]{:S(2)}) collective-permute-start(f32[8,1024]{1,0:T(8,128)S(1)} %get-tuple-element.64), channel_id=1, source_target_pairs={{0,4},{4,0},{8,12},{12,8},{1,5},{5,1},{9,13},{13,9},{2,6},{6,2},{1... | collective-permute-start | bytes 98312 | tf_op jit(solution)/shard_map/ppermute | solution.py:30
  56.8 5.8 %collective-permute-start.11 = (f32[8,1024]{1,0:T(8,128)S(1)}, f32[8,1024]{1,0:T(8,128)S(1)}, u32[]{:S(2)}, u32[]{:S(2)}) collective-permute-start(f32[8,1024]{1,0:T(8,128)S(1)} %get-tuple-element.65), channel_id=1, source_target_pairs={{0,8},{4,12},{8,0},{12,4},{1,9},{5,13},{9,1},{13,5},{2,10},{6,14},... | collective-permute-start | bytes 98312 | tf_op jit(solution)/shard_map/ppermute | solution.py:30
  60.5 5.7 %collective-permute-start.12 = (f32[8,1024]{1,0:T(8,128)S(1)}, f32[8,1024]{1,0:T(8,128)S(1)}, u32[]{:S(2)}, u32[]{:S(2)}) collective-permute-start(f32[8,1024]{1,0:T(8,128)S(1)} %get-tuple-element.66), channel_id=1, source_target_pairs={{0,12},{4,8},{8,4},{12,0},{1,13},{5,9},{9,5},{13,1},{2,14},{6,10},... | collective-permute-start | bytes 98312 | tf_op jit(solution)/shard_map/ppermute | solution.py:30

commit v4 on v3

--- a/solution.py
+++ b/solution.py
@@ -51,10 +51,9 @@
         ins, outs = refs[:inputs], refs[inputs + n : inputs + n + outputs]
         copies = []
         for i, (load, source, target) in enumerate(zip(loads, sources, targets)):
-            _, first, count, place = load
-            width = target.shape[2]
-            columns = pl.ds(pl.multiple_of(place() * width, width), width)
-            source = source.at[pl.ds(first, count), :, columns]
+            _, first, count = load
+            depth = target.shape[0]
+            source = source.at[pl.ds(first * (depth // count), depth)]
             copies.append(pltpu.make_async_copy(source, target, refs[-1].at[i]))
         begin = lambda: [copy.start() for copy in copies]
         rest = refs[inputs + outputs + 2 * n : -1]
@@ -62,7 +61,11 @@
             body(*ins, *outs, *rest, begin)
         else:
             begin()
-            body(*ins, *outs, *rest)
+
+            @pl.when(lax.axis_index("ep") >= 0)
+            def _():
+                body(*ins, *outs, *rest)
+
         for copy in copies:
             copy.wait()
 
@@ -70,11 +73,10 @@
 
 
 def kernel_call(
-    body, name, args, specs, outs, scratch=(), loads=(), parts=1, limit=4, cost=(0, 0, 0), aliases=None
+    body, name, args, specs, outs, scratch=(), loads=(), limit=4, cost=(0, 0, 0), aliases=None
 ):
     targets = [
-        pltpu.VMEM((count, array.shape[1], array.shape[2] // part), BF16)
-        for (array, _, count, _), part in zip(loads, parts if loads else ())
+        pltpu.VMEM((count * array.shape[1], array.shape[2]), BF16) for array, _, count in loads
     ]
     flops, bytes_accessed, transcendentals = cost
     bytes_accessed += sum(2 * math.prod(target.shape) for target in targets)
@@ -90,38 +92,26 @@
             flops=flops, bytes_accessed=bytes_accessed, transcendentals=transcendentals
         ),
         name=name,
-    )(*args, *(far(array) for array, *_ in loads))
+    )(*args, *(far(array.reshape(-1, array.shape[2])) for array, *_ in loads))
     return results[: len(outs)], results[len(outs) :]
 
 
 class Loads:
     def __init__(self, entry, leave):
         self.entry, self.leave = entry, leave
-        self.near = {}
+        self.near = {"entry": [], "leave": []}
 
     def call(self, body, name, args, specs, outs, pieces=(), **more):
-        loads, parts = [], []
-        for what, which, first, count in pieces:
-            if what == "entry":
-                loads.append((self.entry, first, count, functools.partial(self.block, which)))
-                parts.append(SIDE)
-            else:
-                loads.append((self.leave, first, count, functools.partial(self.half, which)))
-                parts.append(2)
-        results, arrays = kernel_call(
-            body, name, args, specs, outs, loads=tuple(loads), parts=parts, **more
-        )
-        for (what, which, _, _), array in zip(pieces, arrays):
-            self.near.setdefault((what, which), []).append(array)
+        loads = tuple((getattr(self, what), first, count) for what, first, count in pieces)
+        results, arrays = kernel_call(body, name, args, specs, outs, loads=loads, **more)
+        for (what, first, count), array in zip(pieces, arrays):
+            self.near[what].append((first, count, array))
         return results
 
-    @staticmethod
-    def block(k):
-        return lax.axis_index("ep") ^ k
-
-    @staticmethod
-    def half(other):
-        return (lax.axis_index("hd") // 2) ^ other
+    def pieces(self, what, first, last):
+        chosen = [p for p in self.near[what] if first <= p[0] and p[0] + p[1] <= last]
+        assert sum(p[1] for p in chosen) == last - first
+        return tuple(p[2] for p in sorted(chosen, key=lambda p: p[0]))
 
 
 def shaped(shape, dtype=F32):
@@ -136,14 +126,17 @@
     route_far,
     residual_far,
     weight_far,
+    slot_far,
     out,
     weight,
+    order,
     lengths,
     queries,
     cache,
     ids,
     route,
     residual,
+    slot_of,
     staged,
     gathered,
     sems,
@@ -156,6 +149,7 @@
         (ids_far, ids),
         (route_far, route),
         (residual_far, residual),
+        (slot_far, slot_of),
         (weight_far, weight),
     )
     copies = [pltpu.make_async_copy(*pair, sems.at[i]) for i, pair in enumerate(pairs)]
@@ -177,6 +171,27 @@
         limit = jnp.where(slot == s, 2 * lengths[s], limit)
     place = lax.broadcasted_iota(jnp.int32, (2 * CACHE_LENGTH, everyone), 0)
     visible = jnp.logical_and(place % 2 == 0, place < limit)
+    width = heads * HEAD_SIZE
+    copies[3].wait()
+    copies[4].wait()
+    row = lax.broadcasted_iota(jnp.int32, (TOPK, 128), 0)
+    lane = lax.broadcasted_iota(jnp.int32, (TOPK, 128), 1)
+    total = jnp.zeros((rows, 128), F32)
+    for j, part in enumerate((ids[...].astype(F32).astype(BF16), *split3(route[...]))):
+        spread = (lane == row + j * TOPK).astype(F32).astype(BF16)
+        total = total + jnp.dot(part, spread, preferred_element_type=F32)
+    out[:, width : width + 128] = total.astype(BF16)
+    copies[5].wait()
+    out[:, width + 128 :] = residual[...]
+    copies[6].wait()
+    me = lax.axis_index("ep")
+    row = lax.broadcasted_iota(jnp.int32, order.shape, 0)
+    wanted = jnp.zeros(order.shape, jnp.int32)
+    for r in range(order.shape[0]):
+        held = slot_of[r]
+        wanted = jnp.where(row == r, ((held // rows) ^ me) * rows + held % rows, wanted)
+    column = lax.broadcasted_iota(jnp.int32, order.shape, 1)
+    order[...] = (wanted == column).astype(F32).astype(BF16)
     copies[2].wait()
     scores = jnp.dot(cache[0], turned, preferred_element_type=F32)
     for s in range(1, rows):
@@ -189,33 +204,25 @@
     for s in range(rows):
         span = slice(s * heads, (s + 1) * heads)
         gathered[span, :] = jnp.dot(moved[span], cache[s], preferred_element_type=F32)
-    width = heads * HEAD_SIZE
     for h in range(heads):
         lanes = slice(h * HEAD_SIZE, (h + 1) * HEAD_SIZE)
         out[:, lanes] = gathered[pl.ds(h, rows, stride=heads), :].astype(BF16)
-    copies[3].wait()
-    copies[4].wait()
-    row = lax.broadcasted_iota(jnp.int32, (TOPK, 128), 0)
-    lane = lax.broadcasted_iota(jnp.int32, (TOPK, 128), 1)
-    total = jnp.zeros((rows, 128), F32)
-    for j, part in enumerate((ids[...].astype(F32).astype(BF16), *split3(route[...]))):
-        spread = (lane == row + j * TOPK).astype(F32).astype(BF16)
-        total = total + jnp.dot(part, spread, preferred_element_type=F32)
-    out[:, width : width + 128] = total.astype(BF16)
-    copies[5].wait()
-    out[:, width + 128 :] = residual[...]
-    copies[6].wait()
-
-
-def attention(loads, pieces, lengths, queries, cache, ids, route, residual, weight):
+    copies[7].wait()
+
+
+def attention(loads, pieces, lengths, queries, cache, ids, route, residual, weight, slot_of):
     rows, width = queries.shape
     staged = pltpu.VMEM((rows * width // HEAD_SIZE, HEAD_SIZE), F32)
     return loads.call(
         attention_kernel,
         "attention",
-        tuple(map(far, (lengths, queries, cache, ids, route, residual, weight))),
-        [ANYWHERE] * 7,
-        (shaped((rows, width + 128 + residual.shape[1]), BF16), pltpu.VMEM(weight.shape, BF16)),
+        tuple(map(far, (lengths, queries, cache, ids, route, residual, weight, slot_of))),
+        [ANYWHERE] * 8,
+        (
+            shaped((rows, width + 128 + residual.shape[1]), BF16),
+            pltpu.VMEM(weight.shape, BF16),
+            shaped((slot_of.shape[0], slot_of.shape[0]), BF16),
+        ),
         pieces,
         scratch=[
             pltpu.SMEM(lengths.shape, jnp.int32),
@@ -224,9 +231,10 @@
             pltpu.VMEM(ids.shape, jnp.int32),
             pltpu.VMEM(route.shape, F32),
             pltpu.VMEM(residual.shape, BF16),
+            pltpu.SMEM(slot_of.shape, jnp.int32),
             staged,
             staged,
-            DMA((7,)),
+            DMA((8,)),
         ],
         cost=(140_000_000, 12_000_000, 65536),
     )
@@ -243,44 +251,33 @@
     )[0]
 
 
-def projection_kernel(slot_far, b0, b1, b2, b3, weight, unused, out, routing, slot_of, kept, sem):
+def projection_kernel(order, b0, b1, b2, b3, weight, unused, out, routing, kept):
     del unused
-    copy = pltpu.make_async_copy(slot_far, slot_of, sem)
-    copy.start()
     blocks = (b0, b1, b2, b3)
     rows = b0.shape[0]
     width = weight.shape[0]
-    everyone = SIDE * rows
     me = lax.axis_index("ep")
-    held = jnp.concatenate([b[:, :width].astype(F32) for b in blocks], axis=0).astype(BF16)
-    row = lax.broadcasted_iota(jnp.int32, (everyone, everyone), 0)
-    column = lax.broadcasted_iota(jnp.int32, (everyone, everyone), 1)
-    wanted = jnp.zeros((everyone, everyone), jnp.int32)
     for k, block in enumerate(blocks):
         span = pl.ds(pl.multiple_of((me ^ k) * rows, rows), rows)
         routing[span, :] = block[:, width : width + 128].astype(F32)
         kept[span, :] = block[:, width + 128 :].astype(F32)
-    copy.wait()
-    for r in range(everyone):
-        slot = slot_of[r]
-        wanted = jnp.where(row == r, ((slot // rows) ^ me) * rows + slot % rows, wanted)
-    order = (wanted == column).astype(F32).astype(BF16)
-    ordered = jnp.dot(order, held, preferred_element_type=F32).astype(BF16)
+    held = jnp.concatenate([b[:, :width].astype(F32) for b in blocks], axis=0).astype(BF16)
+    ordered = jnp.dot(order[...], held, preferred_element_type=F32).astype(BF16)
     own = (me == lax.axis_index("hd")).astype(F32)
     out[...] = jnp.dot(ordered, weight[...], preferred_element_type=F32) + own * kept[...]
 
 
-def projection(loads, pieces, slot_of, blocks, weight, unused):
+def projection(loads, pieces, order, blocks, weight, unused):
     everyone = SIDE * blocks[0].shape[0]
     wide = (everyone, weight.shape[1])
     return loads.call(
         projection_kernel,
         "projection",
-        (far(slot_of), *blocks, weight, unused),
-        [ANYWHERE] + [HERE] * 5 + [ANYWHERE],
+        (order, *blocks, weight, unused),
+        [HERE] * 6 + [ANYWHERE],
         (shaped(wide), shaped((everyone, 128))),
         pieces,
-        scratch=[pltpu.SMEM(slot_of.shape, jnp.int32), pltpu.VMEM(wide, F32), DMA],
+        scratch=[pltpu.VMEM(wide, F32)],
         limit=6,
         cost=(140_000_000, 4_500_000, 0),
     )
@@ -321,43 +318,37 @@
     )[0]
 
 
-def entry_kernel(k, n, packed, *refs):
-    near, before, out = refs[:n], refs[n] if k else None, refs[-1]
-    width = near[0].shape[2]
-    turned = packed[:, :width].astype(F32).T.astype(BF16)
-    at = 0
-    for array in near:
-        for e in range(array.shape[0]):
-            part = jnp.dot(array[e], turned, preferred_element_type=F32)
-            span = slice(at, at + part.shape[0])
-            out[span, :] = before[span, :] + part if k else part
-            at = span.stop
-
-
-def entry_last_kernel(n, packed, *refs):
-    near, (before, routing, p0, p1, p2, out) = refs[:n], refs[n:]
-    hidden, width = near[0].shape[1:]
-    rows = packed.shape[0]
-    turned = packed[:, :width].astype(F32).T.astype(BF16)
+def entry_kernel(base, first, n, hidden, *refs):
+    packs, routing, near, rest = refs[:SIDE], refs[SIDE], refs[SIDE + 1 : SIDE + 1 + n], refs[SIDE + 1 + n :]
+    rows, width = packs[0].shape
+    width = width - 128
+    me = lax.axis_index("ep")
+    if first:
+        _, out, turned = rest
+        for k, packed in enumerate(packs):
+            span = pl.ds(pl.multiple_of((me ^ k) * width, width), width)
+            turned[span, :] = packed[:, :width].astype(F32).T.astype(BF16)
+    else:
+        turned, out = rest
     squares = jnp.zeros((rows, 128), F32)
-    for block in (p0, p1, p2, packed):
-        squares = squares + block[:, width:].astype(F32)
+    for packed in packs:
+        squares = squares + packed[:, width:].astype(F32)
     mean = jnp.sum(squares.T, axis=0, keepdims=True) / (SIDE * width)
     scale = lax.rsqrt(mean + 1e-06)
     table = routing[...].T
     ids = table[0:TOPK, :]
     weight = table[TOPK : 2 * TOPK, :] + table[2 * TOPK : 3 * TOPK, :]
     weight = weight + table[3 * TOPK : 4 * TOPK, :]
-    base = lax.axis_index("ep") * (before.shape[0] // hidden)
+    count = EXPERTS // SIDE
     number = 0
     pair = []
     for array in near:
-        for e in range(array.shape[0]):
-            at = number * hidden
-            chosen = ids == (base + number).astype(F32)
+        for start in range(0, array.shape[0], hidden):
+            chosen = ids == (me * count + base + number).astype(F32)
             share = jnp.sum(jnp.where(chosen, weight, 0.0), axis=0, keepdims=True)
-            part = jnp.dot(array[e], turned, preferred_element_type=F32)
-            total = (before[at : at + hidden, :] + part) * scale
+            total = scale * jnp.dot(
+                array[start : start + hidden, :], turned[...], preferred_element_type=F32
+            )
             active = (total / (1.0 + jnp.exp(-total))).astype(BF16).astype(F32) * share
             high = active.astype(BF16).astype(F32)
             pair.append(jnp.concatenate([high, active - high], axis=1))
@@ -369,67 +360,63 @@
                 pair = []
 
 
-def entries(loads, plan, packs, routing):
+def entries(loads, pieces, base, last, packs, routing, mark=None, turned=None):
+    _, hidden, width = loads.leave.shape
+    count = last - base
+    rows = packs[0].shape[0]
+    near = loads.pieces("entry", base, last)
+    first = turned is None
+    args = (*packs, routing, *near) + ((mark,) if first else (turned,))
+    outs = (shaped((2 * rows, count * hidden), BF16),)
+    if first:
+        outs += (shaped((width, rows), BF16),)
+    return loads.call(
+        functools.partial(entry_kernel, base, first, len(near), hidden),
+        f"entry{base}",
+        args,
+        [HERE] * len(args),
+        outs,
+        pieces,
+        cost=(2 * rows * count * hidden * width, 2 * count * hidden * width, 0),
+    )
+
+
+def leave_kernel(other, n, m, step, *refs):
+    scaled, near, out = refs[:m], refs[m : m + n], refs[-1]
+    rows, half = out.shape
+    chip = (lax.axis_index("hd") // 2) ^ other
+    for c in range(0, half, step):
+        columns = pl.ds(pl.multiple_of(chip * half + c, step), step)
+        total = jnp.zeros((2 * rows, step), F32)
+        which, at = 0, 0
+        for array in near:
+            done = 0
+            while done < array.shape[0]:
+                depth = min(array.shape[0] - done, scaled[which].shape[1] - at)
+                total = total + jnp.dot(
+                    scaled[which][:, at : at + depth],
+                    array[done : done + depth, columns],
+                    preferred_element_type=F32,
+                )
+                done, at = done + depth, at + depth
+                if at == scaled[which].shape[1]:
+                    which, at = which + 1, 0
+        out[:, c : c + step] = (total[:rows] + total[rows:]).astype(out.dtype)
+
+
+def leaves(loads, name, other, dtype, scaled, unused):
     count, hidden, width = loads.leave.shape
-    rows = packs[0].shape[0]
-    cost = (2 * rows * count * hidden * width // SIDE, 2 * count * hidden * width // SIDE, 0)
-    total = None
-    for k in range(SIDE):
-        near = tuple(loads.near["entry", k])
-        args = (packs[k], *near) + ((total,) if k else ())
-        n = len(near)
-        if k < SIDE - 1:
-            body = functools.partial(entry_kernel, k, n)
-            outs = (shaped((count * hidden, rows)),)
-            aliases = {n + 1: 0} if k else None
-        else:
-            args += (routing, *packs[:-1])
-            body = functools.partial(entry_last_kernel, n)
-            outs = (shaped((2 * rows, count * hidden), BF16),)
-            aliases = None
-        (total,) = loads.call(
-            body,
-            f"entry{k}",
-            args,
-            [HERE] * len(args),
-            outs,
-            plan.get(f"entry{k}", ()),
-            cost=cost,
-            aliases=aliases,
-        )
-    return total
-
-
-def leave_kernel(n, step, scaled, *refs):
-    near, out = refs[:n], refs[-1]
-    rows, count = out.shape
-    for c in range(0, count, step):
-        total = jnp.zeros((2 * rows, step), F32)
-        at = 0
-        for array in near:
-            depth = array.shape[0] * array.shape[1]
-            flat = array.reshape(depth, array.shape[2])
-            total = total + jnp.dot(
-                scaled[:, at : at + depth], flat[:, c : c + step], preferred_element_type=F32
-            )
-            at += depth
-        out[:, c : c + step] = (total[:rows] + total[rows:]).astype(out.dtype)
-
-
-def leaves(loads, pieces, name, other, dtype, scaled, unused):
-    near = tuple(loads.near["leave", other])
-    count, hidden, width = loads.leave.shape
-    rows = scaled.shape[0] // 2
-    return loads.call(
-        functools.partial(leave_kernel, len(near), 1024),
+    near = loads.pieces("leave", 0, count)
+    rows = scaled[0].shape[0] // 2
+    return kernel_call(
+        functools.partial(leave_kernel, other, len(near), len(scaled), 1024),
         name,
-        (scaled, *near, unused),
-        [HERE] * (1 + len(near)) + [ANYWHERE],
+        (*scaled, *near, unused),
+        [HERE] * (len(scaled) + len(near)) + [ANYWHERE],
         (shaped((rows, width // 2), dtype),),
-        pieces,
         cost=(2 * rows * count * hidden * width, count * hidden * width, 0),
         limit=6,
-    )[0]
+    )[0][0]
 
 
 def halve_kernel(mine, received, keep, send):
@@ -464,20 +451,15 @@
     return kernel_call(share_kernel, "share", args, [HERE] * 3, outs, cost=cost)[0]
 
 
-def plan_of(count):
-    half, quarter = count // 2, count // 4
-    cut = (count // 8, half, count * 3 // 8, count * 3 // 8)
-    return {
-        "attention": [("entry", 0, 0, half)],
-        "fetch0": [("entry", 0, half, half), ("entry", 1, 0, count)],
-        "projection": [("entry", 2, 0, half)],
-        "fetch1": [("entry", 2, half, half), ("entry", 3, 0, half)],
-        "entry0": [("entry", 3, half, half), ("leave", 1, 0, cut[0])],
-        "entry1": [("leave", 1, cut[0], cut[2])],
-        "entry2": [("leave", 1, cut[0] + cut[2], count - cut[0] - cut[2])],
-        "entry3": [("leave", 0, 0, cut[3])],
-        "leave1": [("leave", 0, cut[3], count - cut[3])],
-    }
+PLAN = {
+    "attention": [("entry", 0, 2)],
+    "fetch0": [("entry", 2, 6), ("entry", 8, 2)],
+    "projection": [],
+    "fetch1": [("entry", 10, 6)],
+    "fetch2": [("leave", 0, 5)],
+    "entry0": [("leave", 5, 6)],
+    "entry8": [("leave", 11, 5)],
+}
 
 
 def square_body(
@@ -495,8 +477,8 @@
     rows = queries.shape[0]
     cache = key_value_cache.reshape(rows, 2 * CACHE_LENGTH, HEAD_SIZE)
     loads = Loads(jnp.swapaxes(in_weight, 1, 2), down_weight)
-    plan = plan_of(down_weight.shape[0])
-    attended, weight = attention(
+    plan = PLAN
+    attended, weight, order = attention(
         loads,
         plan["attention"],
         lengths,
@@ -506,22 +488,26 @@
         route_weight,
         residual,
         out_weight,
+        slot_of,
     )
     blocks = [attended] + [swap(attended, "ep", k) for k in (1, 2, 3)]
     mark = fetch(loads, plan["fetch0"], "fetch0", attended)
-    partial_value, routing = projection(loads, plan["projection"], slot_of, blocks, weight, mark)
+    partial_value, routing = projection(loads, plan["projection"], order, blocks, weight, mark)
     pair = add(partial_value, swap(partial_value, "hd", 1))
     far_pair = swap(pair, "hd", 2)
     mark = fetch(loads, plan["fetch1"], "fetch1", pair)
     stream, packed = streams(pair, far_pair, mark)
     packs = [packed] + [swap(packed, "ep", k) for k in (1, 2, 3)]
-    scaled = entries(loads, plan, packs, routing)
-    theirs = leaves(loads, plan["leave1"], "leave1", 1, BF16, scaled, scaled)
-    mine = leaves(loads, (), "leave0", 0, F32, scaled, theirs)
+    mark = fetch(loads, plan["fetch2"], "fetch2", packed)
+    scaled, turned = entries(loads, plan["entry0"], 0, 8, packs, routing, mark)
+    (more,) = entries(loads, plan["entry8"], 8, 16, packs, routing, turned=turned)
+    scaled = (scaled, more)
+    theirs = leaves(loads, "leave1", 1, BF16, scaled, more)
+    mine = leaves(loads, "leave0", 0, F32, scaled, theirs)
     keep, send = halve(mine, swap(theirs, "hd", 2))
     total, *others = share(keep, swap(send, "hd", 1), stream)
-    for k, block in enumerate(others):
-        total = total + swap(block, "ep", k + 1)
+    for k in (3, 2, 1):
+        total = total + swap(others[k - 1], "ep", k)
     return total.astype(BF16)
 
 

time: 67.1 us -> 56.9 us (0.85)
  Pallas kernels: 37.5 us -> 29 us
  waiting for transfers between devices: 10.7 us -> 9.13 us
    pallas_call x14 -> x13, Pallas kernels: 37.5 us -> 29 us  [kernel_call(): pl.pallas_call(hosted(body, len(args), len(outs), loads) if loads else bo...]
    ppermute x13, waiting for transfers between devices: 10.7 us -> 9.13 us  [swap(): return lax.ppermute(block, axis, [(i, i ^ k) for i in range(SIDE)])]
  transfers between devices with their start and end apart: 13 -> 13, of which waited for: 7 -> 7; matrix products, arithmetic and copies ran while one was open for 0% -> 0% of each run, Pallas kernels for 33% -> 25%
where the time goes in v4:
time: 56.9 us; the launch traced here: 56.7 us
  Pallas kernels  29 us (51%)
  starting transfers between devices  17.9 us (31%)
  waiting for transfers between devices  9.13 us (16%)
  other arithmetic  0.62 us (1%)
    pallas_call x13, Pallas kernels, kernel_call(): pl.pallas_call(hosted(body, len(args), len(outs), loads) if loads else bo...  29 us
    ppermute x13, starting transfers between devices, swap(): return lax.ppermute(block, axis, [(i, i ^ k) for i in range(SIDE)])  17.9 us
    ppermute x13, waiting for transfers between devices, swap(): return lax.ppermute(block, axis, [(i, i ^ k) for i in range(SIDE)])  9.13 us
  transfers between devices with their start and end apart: 13, of which 7 were waited for; matrix products, arithmetic and copies ran while one was open for 0% of the time, Pallas kernels for 25%

profile of v4, /device:TPU:0, one launch (start us, length us, event | category | flops | bytes accessed | tf_op | source)
XLA Modules:
  0.0 56.7 jit_solution(12692891005335381425)
XLA Ops:
  0.0 3.6 %attention.1 = (bf16[8,3200]{1,0:T(8,128)(2,1)S(1)}, bf16[2048,1024]{1,0:T(8,128)(2,1)S(1)}, bf16[32,32]{1,0:T(8,128)(2,1)S(1)}, bf16[384,4096]{1,0:T(8,128)(2,1)S(1)}) custom-call(s32[8]{0:T(128)} %refs_0_.1, bf16[8,2048]{1,0:T(8,128)(2,1)} %refs_1_.1, bf16[8,512,128]{2,1,0:T(8,128)(2,1)} %bitcast.12, s32[8,8]{1,0:T(8,128)} %refs_3_.1, f32[8,8]{1,0:T(8,128)} %refs_4_.1, ...), custom_call_target="tpu_custom_call" | custom-call | flops 140000000 | bytes 15145728 | tf_op jit(solution)/shard_map/attention/pallas_call | solution.py:83
  3.6 5.1 %collective-permute-start.2 = (bf16[8,3200]{1,0:T(8,128)(2,1)S(1)}, bf16[8,3200]{1,0:T(8,128)(2,1)S(1)}, u32[]{:S(2)}, u32[]{:S(2)}) collective-permute-start(bf16[8,3200]{1,0:T(8,128)(2,1)S(1)} %get-tuple-element.32.refs_0_.b0), channel_id=1, source_target_pairs={{0,12},{4,8},{8,4},{12,0},{1,13},{5,9},{9,5},{13,1},{2,14},{6,10},... | collective-permute-start | bytes 153608 | tf_op jit(solution)/shard_map/ppermute | solution.py:30
  8.7 0.0 collective-permute-start.1
  8.7 0.6 %collective-permute-start = (bf16[8,3200]{1,0:T(8,128)(2,1)S(1)}, bf16[8,3200]{1,0:T(8,128)(2,1)S(1)}, u32[]{:S(2)}, u32[]{:S(2)}) collective-permute-start(bf16[8,3200]{1,0:T(8,128)(2,1)S(1)} %get-tuple-element.32.refs_0_.b0), channel_id=1, source_target_pairs={{0,4},{4,0},{8,12},{12,8},{1,5},{5,1},{9,13},{13,9},{2,6},{6,2},{1... | collective-permute-start | bytes 153608 | tf_op jit(solution)/shard_map/ppermute | solution.py:30
  9.4 4.6 %fetch0.1 = (f32[8,128]{1,0:T(8,128)S(1)}, bf16[1152,4096]{1,0:T(8,128)(2,1)S(1)}, bf16[384,4096]{1,0:T(8,128)(2,1)S(1)}) custom-call(bf16[8,3200]{1,0:T(8,128)(2,1)S(1)} %get-tuple-element.32.refs_0_.b0, bf16[3072,4096]{1,0:T(8,128)(2,1)} %bitcast.6, bf16[3072,4096]{1,0:T(8,128)(2,1)} %bitcast.7), custom_call_target="tpu_custom_call" | custom-call | bytes 12582912 | tf_op jit(solution)/shard_map/fetch0/pallas_call | solution.py:83
  14.0 0.0 collective-permute-done.2.b3
  14.0 0.0 collective-permute-done.1.b2
  14.0 0.0 collective-permute-done.b1
  14.0 0.9 %projection.1 = (f32[32,1024]{1,0:T(8,128)S(1)}, f32[32,128]{1,0:T(8,128)S(1)}) custom-call(bf16[32,32]{1,0:T(8,128)(2,1)S(1)} %get-tuple-element.31.order, bf16[8,3200]{1,0:T(8,128)(2,1)S(1)} %get-tuple-element.32.refs_0_.b0, bf16[8,3200]{1,0:T(8,128)(2,1)S(1)} %collective-permute-done.b1, bf16[8,3200]{1,0:T(8,128)(2,1)S(1)} %collective-permute-done.1.b2, ...), custom_call_target="tpu_custom_call" | custom-call | flops 140000000 | bytes 4500000 | tf_op jit(solution)/shard_map/projection/pallas_call | solution.py:83
  14.9 0.0 collective-permute-start.3
  15.0 1.3 %collective-permute-done.3.b = f32[32,1024]{1,0:T(8,128)S(1)} collective-permute-done((f32[32,1024]{1,0:T(8,128)S(1)}, f32[32,1024]{1,0:T(8,128)S(1)}, u32[]{:S(2)}, u32[]{:S(2)}) %collective-permute-start.3) | collective-permute-done | bytes 131104 | tf_op jit(solution)/shard_map/ppermute | solution.py:30
  16.3 1.7 %collective-permute-start.4 = (f32[32,1024]{1,0:T(8,128)S(1)}, f32[32,1024]{1,0:T(8,128)S(1)}, u32[]{:S(2)}, u32[]{:S(2)}) collective-permute-start(f32[32,1024]{1,0:T(8,128)S(1)} %add.16.refs_0_.a), channel_id=1, source_target_pairs={{0,2},{1,3},{2,0},{3,1},{4,6},{5,7},{6,4},{7,5},{8,10},{9,11},{10,... | collective-permute-start | bytes 393224 | tf_op jit(solution)/shard_map/ppermute | solution.py:30
  18.0 3.7 %fetch1.1 = (f32[8,128]{1,0:T(8,128)S(1)}, bf16[1152,4096]{1,0:T(8,128)(2,1)S(1)}) custom-call(f32[32,1024]{1,0:T(8,128)S(1)} %add.16.refs_0_.a, bf16[3072,4096]{1,0:T(8,128)(2,1)} %bitcast.8), custom_call_target="tpu_custom_call" | custom-call | bytes 9437184 | tf_op jit(solution)/shard_map/fetch1/pallas_call | solution.py:83
  21.7 0.2 collective-permute-done.4.b
  21.9 0.1 stream.1
  22.0 3.8 %collective-permute-start.7 = (bf16[32,1152]{1,0:T(8,128)(2,1)S(1)}, bf16[32,1152]{1,0:T(8,128)(2,1)S(1)}, u32[]{:S(2)}, u32[]{:S(2)}) collective-permute-start(bf16[32,1152]{1,0:T(8,128)(2,1)S(1)} %get-tuple-element.37.refs_0_), channel_id=1, source_target_pairs={{0,12},{4,8},{8,4},{12,0},{1,13},{5,9},{9,5},{13,1},{2,14},{6,10},... | collective-permute-start | bytes 221192 | tf_op jit(solution)/shard_map/ppermute | solution.py:30
  25.9 0.0 collective-permute-start.6
  25.9 0.6 %collective-permute-start.5 = (bf16[32,1152]{1,0:T(8,128)(2,1)S(1)}, bf16[32,1152]{1,0:T(8,128)(2,1)S(1)}, u32[]{:S(2)}, u32[]{:S(2)}) collective-permute-start(bf16[32,1152]{1,0:T(8,128)(2,1)S(1)} %get-tuple-element.37.refs_0_), channel_id=1, source_target_pairs={{0,4},{4,0},{8,12},{12,8},{1,5},{5,1},{9,13},{13,9},{2,6},{6,2},{1... | collective-permute-start | bytes 221192 | tf_op jit(solution)/shard_map/ppermute | solution.py:30
  26.5 3.2 %fetch2.1 = (f32[8,128]{1,0:T(8,128)S(1)}, bf16[960,4096]{1,0:T(8,128)(2,1)S(1)}) custom-call(bf16[32,1152]{1,0:T(8,128)(2,1)S(1)} %get-tuple-element.37.refs_0_, bf16[3072,4096]{1,0:T(8,128)(2,1)} %bitcast.9), custom_call_target="tpu_custom_call" | custom-call | bytes 7864320 | tf_op jit(solution)/shard_map/fetch2/pallas_call | solution.py:83
  29.8 0.0 collective-permute-done.7.refs_3_
  29.8 2.0 %collective-permute-done.6.refs_2_ = bf16[32,1152]{1,0:T(8,128)(2,1)S(1)} collective-permute-done((bf16[32,1152]{1,0:T(8,128)(2,1)S(1)}, bf16[32,1152]{1,0:T(8,128)(2,1)S(1)}, u32[]{:S(2)}, u32[]{:S(2)}) %collective-permute-start.6) | collective-permute-done | bytes 73760 | tf_op jit(solution)/shard_map/ppermute | solution.py:30
  31.8 0.0 collective-permute-done.5.refs_1_
  31.8 4.0 %entry0.1 = (bf16[64,1536]{1,0:T(8,128)(2,1)S(1)}, bf16[4096,32]{1,0:T(8,128)(2,1)S(1)}, bf16[1152,4096]{1,0:T(8,128)(2,1)S(1)}) custom-call(bf16[32,1152]{1,0:T(8,128)(2,1)S(1)} %get-tuple-element.37.refs_0_, bf16[32,1152]{1,0:T(8,128)(2,1)S(1)} %collective-permute-done.5.refs_1_, bf16[32,1152]{1,0:T(8,128)(2,1)S(1)} %collective-permute-done.6.refs_2_, ...), custom_call_target="tpu_custom_call" | custom-call | flops 402653184 | bytes 22020096 | tf_op jit(solution)/shard_map/entry0/pallas_call | solution.py:83
  35.8 3.9 %entry8.1 = (bf16[64,1536]{1,0:T(8,128)(2,1)S(1)}, bf16[960,4096]{1,0:T(8,128)(2,1)S(1)}) custom-call(bf16[32,1152]{1,0:T(8,128)(2,1)S(1)} %get-tuple-element.37.refs_0_, bf16[32,1152]{1,0:T(8,128)(2,1)S(1)} %collective-permute-done.5.refs_1_, bf16[32,1152]{1,0:T(8,128)(2,1)S(1)} %collective-permute-done.6.refs_2_, ...), custom_call_target="tpu_custom_call" | custom-call | flops 402653184 | bytes 20447232 | tf_op jit(solution)/shard_map/entry8/pallas_call | solution.py:83
  39.7 2.4 %leave1.1.refs_5_ = bf16[32,2048]{1,0:T(8,128)(2,1)S(1)} custom-call(bf16[64,1536]{1,0:T(8,128)(2,1)S(1)} %get-tuple-element.42.refs_0_, bf16[64,1536]{1,0:T(8,128)(2,1)S(1)} %get-tuple-element.46.refs_1_.refs_5_, bf16[960,4096]{1,0:T(8,128)(2,1)S(1)} %get-tuple-element.47.refs_2_, bf16[1152,4096]{1,0:T(8,128)(2,1)S(1)} %get-tuple-element.48.refs_3_, ...), custom_call_target="tpu_custom_call" | custom-call | flops 805306368 | bytes 12582912 | tf_op jit(solution)/shard_map/leave1/pallas_call | solution.py:83
  42.1 1.4 %collective-permute-start.8 = (bf16[32,2048]{1,0:T(8,128)(2,1)S(1)}, bf16[32,2048]{1,0:T(8,128)(2,1)S(1)}, u32[]{:S(2)}, u32[]{:S(2)}) collective-permute-start(bf16[32,2048]{1,0:T(8,128)(2,1)S(1)} %leave1.1.refs_5_), channel_id=1, source_target_pairs={{0,2},{1,3},{2,0},{3,1},{4,6},{5,7},{6,4},{7,5},{8,10},{9,11},{10,... | collective-permute-start | bytes 393224 | tf_op jit(solution)/shard_map/ppermute | solution.py:30
  43.5 2.4 %leave0.1.mine = f32[32,2048]{1,0:T(8,128)S(1)} custom-call(bf16[64,1536]{1,0:T(8,128)(2,1)S(1)} %get-tuple-element.42.refs_0_, bf16[64,1536]{1,0:T(8,128)(2,1)S(1)} %get-tuple-element.46.refs_1_.refs_5_, bf16[960,4096]{1,0:T(8,128)(2,1)S(1)} %get-tuple-element.47.refs_2_, bf16[1152,4096]{1,0:T(8,128)(2,1)S(1)} %get-tuple-element.48.refs_3_, ...), custom_call_target="tpu_custom_call" | custom-call | flops 805306368 | bytes 12582912 | tf_op jit(solution)/shard_map/leave0/pallas_call | solution.py:83
  45.9 1.2 %collective-permute-done.8.received = bf16[32,2048]{1,0:T(8,128)(2,1)S(1)} collective-permute-done((bf16[32,2048]{1,0:T(8,128)(2,1)S(1)}, bf16[32,2048]{1,0:T(8,128)(2,1)S(1)}, u32[]{:S(2)}, u32[]{:S(2)}) %collective-permute-start.8) | collective-permute-done | bytes 131104 | tf_op jit(solution)/shard_map/ppermute | solution.py:30
  47.1 0.1 collective-permute-start.9
  47.2 1.3 %collective-permute-done.9.received = f32[32,1024]{1,0:T(8,128)S(1)} collective-permute-done((f32[32,1024]{1,0:T(8,128)S(1)}, f32[32,1024]{1,0:T(8,128)S(1)}, u32[]{:S(2)}, u32[]{:S(2)}) %collective-permute-start.9) | collective-permute-done | bytes 131104 | tf_op jit(solution)/shard_map/ppermute | solution.py:30
  48.6 2.7 %collective-permute-start.10 = (f32[8,1024]{1,0:T(8,128)S(1)}, f32[8,1024]{1,0:T(8,128)S(1)}, u32[]{:S(2)}, u32[]{:S(2)}) collective-permute-start(f32[8,1024]{1,0:T(8,128)S(1)} %get-tuple-element.54), channel_id=1, source_target_pairs={{0,12},{4,8},{8,4},{12,0},{1,13},{5,9},{9,5},{13,1},{2,14},{6,10},... | collective-permute-start | bytes 98312 | tf_op jit(solution)/shard_map/ppermute | solution.py:30
  51.3 0.0 collective-permute-start.11
  51.3 1.7 %collective-permute-start.12 = (f32[8,1024]{1,0:T(8,128)S(1)}, f32[8,1024]{1,0:T(8,128)S(1)}, u32[]{:S(2)}, u32[]{:S(2)}) collective-permute-start(f32[8,1024]{1,0:T(8,128)S(1)} %get-tuple-element.56), channel_id=1, source_target_pairs={{0,4},{4,0},{8,12},{12,8},{1,5},{5,1},{9,13},{13,9},{2,6},{6,2},{1... | collective-permute-start | bytes 98312 | tf_op jit(solution)/shard_map/ppermute | solution.py:30
  53.0 1.4 %collective-permute-done.10 = f32[8,1024]{1,0:T(8,128)S(1)} collective-permute-done((f32[8,1024]{1,0:T(8,128)S(1)}, f32[8,1024]{1,0:T(8,128)S(1)}, u32[]{:S(2)}, u32[]{:S(2)}) %collective-permute-start.10) | collective-permute-done | bytes 32800 | tf_op jit(solution)/shard_map/ppermute | solution.py:30
  54.4 1.6 %collective-permute-done.11 = f32[8,1024]{1,0:T(8,128)S(1)} collective-permute-done((f32[8,1024]{1,0:T(8,128)S(1)}, f32[8,1024]{1,0:T(8,128)S(1)}, u32[]{:S(2)}, u32[]{:S(2)}) %collective-permute-start.11) | collective-permute-done | bytes 32800 | tf_op jit(solution)/shard_map/ppermute | solution.py:30
  56.1 0.0 collective-permute-done.12
  56.1 0.6 %add_convert_fusion = bf16[8,1024]{1,0:T(8,128)(2,1)} fusion(f32[8,1024]{1,0:T(8,128)S(1)} %collective-permute-done.12, f32[8,1024]{1,0:T(8,128)S(1)} %collective-permute-done.11, f32[8,1024]{1,0:T(8,128)S(1)} %get-tuple-element.53, f32[8,1024]{1,0:T(8,128)S(1)} %collective-permute-done.10), kind=kLoop, calls=%fused_computation | loop fusion | flops 32768 | bytes 147456 | tf_op jit(solution)/shard_map/convert_element_type | solution.py:511
  (3 shorter events, 0.1 us)
Async XLA Ops:
  3.6 10.4 %collective-permute-start.2 = (bf16[8,3200]{1,0:T(8,128)(2,1)S(1)}, bf16[8,3200]{1,0:T(8,128)(2,1)S(1)}, u32[]{:S(2)}, u32[]{:S(2)}) collective-permute-start(bf16[8,3200]{1,0:T(8,128)(2,1)S(1)} %get-tuple-element.32.refs_0_.b0), channel_id=1, source_target_pairs={{0,12},{4,8},{8,4},{12,0},{1,13},{5,9},{9,5},{13,1},{2,14},{6,10},... | collective-permute-start | bytes 153608 | tf_op jit(solution)/shard_map/ppermute | solution.py:30
  8.7 5.3 %collective-permute-start.1 = (bf16[8,3200]{1,0:T(8,128)(2,1)S(1)}, bf16[8,3200]{1,0:T(8,128)(2,1)S(1)}, u32[]{:S(2)}, u32[]{:S(2)}) collective-permute-start(bf16[8,3200]{1,0:T(8,128)(2,1)S(1)} %get-tuple-element.32.refs_0_.b0), channel_id=1, source_target_pairs={{0,8},{4,12},{8,0},{12,4},{1,9},{5,13},{9,1},{13,5},{2,10},{6,14},... | collective-permute-start | bytes 153608 | tf_op jit(solution)/shard_map/ppermute | solution.py:30
  8.7 5.3 %collective-permute-start = (bf16[8,3200]{1,0:T(8,128)(2,1)S(1)}, bf16[8,3200]{1,0:T(8,128)(2,1)S(1)}, u32[]{:S(2)}, u32[]{:S(2)}) collective-permute-start(bf16[8,3200]{1,0:T(8,128)(2,1)S(1)} %get-tuple-element.32.refs_0_.b0), channel_id=1, source_target_pairs={{0,4},{4,0},{8,12},{12,8},{1,5},{5,1},{9,13},{13,9},{2,6},{6,2},{1... | collective-permute-start | bytes 153608 | tf_op jit(solution)/shard_map/ppermute | solution.py:30
  14.9 1.4 %collective-permute-start.3 = (f32[32,1024]{1,0:T(8,128)S(1)}, f32[32,1024]{1,0:T(8,128)S(1)}, u32[]{:S(2)}, u32[]{:S(2)}) collective-permute-start(f32[32,1024]{1,0:T(8,128)S(1)} %get-tuple-element.35.a), channel_id=1, source_target_pairs={{0,1},{1,0},{2,3},{3,2},{4,5},{5,4},{6,7},{7,6},{8,9},{9,8},{10,11... | collective-permute-start | bytes 393224 | tf_op jit(solution)/shard_map/ppermute | solution.py:30
  16.3 5.6 %collective-permute-start.4 = (f32[32,1024]{1,0:T(8,128)S(1)}, f32[32,1024]{1,0:T(8,128)S(1)}, u32[]{:S(2)}, u32[]{:S(2)}) collective-permute-start(f32[32,1024]{1,0:T(8,128)S(1)} %add.16.refs_0_.a), channel_id=1, source_target_pairs={{0,2},{1,3},{2,0},{3,1},{4,6},{5,7},{6,4},{7,5},{8,10},{9,11},{10,... | collective-permute-start | bytes 393224 | tf_op jit(solution)/shard_map/ppermute | solution.py:30
  22.0 7.7 %collective-permute-start.7 = (bf16[32,1152]{1,0:T(8,128)(2,1)S(1)}, bf16[32,1152]{1,0:T(8,128)(2,1)S(1)}, u32[]{:S(2)}, u32[]{:S(2)}) collective-permute-start(bf16[32,1152]{1,0:T(8,128)(2,1)S(1)} %get-tuple-element.37.refs_0_), channel_id=1, source_target_pairs={{0,12},{4,8},{8,4},{12,0},{1,13},{5,9},{9,5},{13,1},{2,14},{6,10},... | collective-permute-start | bytes 221192 | tf_op jit(solution)/shard_map/ppermute | solution.py:30
  25.9 5.9 %collective-permute-start.6 = (bf16[32,1152]{1,0:T(8,128)(2,1)S(1)}, bf16[32,1152]{1,0:T(8,128)(2,1)S(1)}, u32[]{:S(2)}, u32[]{:S(2)}) collective-permute-start(bf16[32,1152]{1,0:T(8,128)(2,1)S(1)} %get-tuple-element.37.refs_0_), channel_id=1, source_target_pairs={{0,8},{4,12},{8,0},{12,4},{1,9},{5,13},{9,1},{13,5},{2,10},{6,14},... | collective-permute-start | bytes 221192 | tf_op jit(solution)/shard_map/ppermute | solution.py:30
  25.9 5.9 %collective-permute-start.5 = (bf16[32,1152]{1,0:T(8,128)(2,1)S(1)}, bf16[32,1152]{1,0:T(8,128)(2,1)S(1)}, u32[]{:S(2)}, u32[]{:S(2)}) collective-permute-start(bf16[32,1152]{1,0:T(8,128)(2,1)S(1)} %get-tuple-element.37.refs_0_), channel_id=1, source_target_pairs={{0,4},{4,0},{8,12},{12,8},{1,5},{5,1},{9,13},{13,9},{2,6},{6,2},{1... | collective-permute-start | bytes 221192 | tf_op jit(solution)/shard_map/ppermute | solution.py:30
  42.1 5.0 %collective-permute-start.8 = (bf16[32,2048]{1,0:T(8,128)(2,1)S(1)}, bf16[32,2048]{1,0:T(8,128)(2,1)S(1)}, u32[]{:S(2)}, u32[]{:S(2)}) collective-permute-start(bf16[32,2048]{1,0:T(8,128)(2,1)S(1)} %leave1.1.refs_5_), channel_id=1, source_target_pairs={{0,2},{1,3},{2,0},{3,1},{4,6},{5,7},{6,4},{7,5},{8,10},{9,11},{10,... | collective-permute-start | bytes 393224 | tf_op jit(solution)/shard_map/ppermute | solution.py:30
  47.1 1.4 %collective-permute-start.9 = (f32[32,1024]{1,0:T(8,128)S(1)}, f32[32,1024]{1,0:T(8,128)S(1)}, u32[]{:S(2)}, u32[]{:S(2)}) collective-permute-start(f32[32,1024]{1,0:T(8,128)S(1)} %get-tuple-element.51), channel_id=1, source_target_pairs={{0,1},{1,0},{2,3},{3,2},{4,5},{5,4},{6,7},{7,6},{8,9},{9,8},{10,11... | collective-permute-start | bytes 393224 | tf_op jit(solution)/shard_map/ppermute | solution.py:30
  48.6 5.9 %collective-permute-start.10 = (f32[8,1024]{1,0:T(8,128)S(1)}, f32[8,1024]{1,0:T(8,128)S(1)}, u32[]{:S(2)}, u32[]{:S(2)}) collective-permute-start(f32[8,1024]{1,0:T(8,128)S(1)} %get-tuple-element.54), channel_id=1, source_target_pairs={{0,12},{4,8},{8,4},{12,0},{1,13},{5,9},{9,5},{13,1},{2,14},{6,10},... | collective-permute-start | bytes 98312 | tf_op jit(solution)/shard_map/ppermute | solution.py:30
  51.3 4.8 %collective-permute-start.11 = (f32[8,1024]{1,0:T(8,128)S(1)}, f32[8,1024]{1,0:T(8,128)S(1)}, u32[]{:S(2)}, u32[]{:S(2)}) collective-permute-start(f32[8,1024]{1,0:T(8,128)S(1)} %get-tuple-element.55), channel_id=1, source_target_pairs={{0,8},{4,12},{8,0},{12,4},{1,9},{5,13},{9,1},{13,5},{2,10},{6,14},... | collective-permute-start | bytes 98312 | tf_op jit(solution)/shard_map/ppermute | solution.py:30
  51.3 4.8 %collective-permute-start.12 = (f32[8,1024]{1,0:T(8,128)S(1)}, f32[8,1024]{1,0:T(8,128)S(1)}, u32[]{:S(2)}, u32[]{:S(2)}) collective-permute-start(f32[8,1024]{1,0:T(8,128)S(1)} %get-tuple-element.56), channel_id=1, source_target_pairs={{0,4},{4,0},{8,12},{12,8},{1,5},{5,1},{9,13},{13,9},{2,6},{6,2},{1... | collective-permute-start | bytes 98312 | tf_op jit(solution)/shard_map/ppermute | solution.py:30

commit v5 on v4

--- a/solution.py
+++ b/solution.py
@@ -51,9 +51,14 @@
         ins, outs = refs[:inputs], refs[inputs + n : inputs + n + outputs]
         copies = []
         for i, (load, source, target) in enumerate(zip(loads, sources, targets)):
-            _, first, count = load
-            depth = target.shape[0]
-            source = source.at[pl.ds(first * (depth // count), depth)]
+            _, first, count, other = load
+            depth, width = target.shape
+            rows = pl.ds(first * (depth // count), depth)
+            if other is None:
+                source = source.at[rows]
+            else:
+                chip = (lax.axis_index("hd") // 2) ^ other
+                source = source.at[rows, pl.ds(pl.multiple_of(chip * width, width), width)]
             copies.append(pltpu.make_async_copy(source, target, refs[-1].at[i]))
         begin = lambda: [copy.start() for copy in copies]
         rest = refs[inputs + outputs + 2 * n : -1]
@@ -76,7 +81,8 @@
     body, name, args, specs, outs, scratch=(), loads=(), limit=4, cost=(0, 0, 0), aliases=None
 ):
     targets = [
-        pltpu.VMEM((count * array.shape[1], array.shape[2]), BF16) for array, _, count in loads
+        pltpu.VMEM((count * array.shape[1], array.shape[2] // (1 if other is None else 2)), BF16)
+        for array, _, count, other in loads
     ]
     flops, bytes_accessed, transcendentals = cost
     bytes_accessed += sum(2 * math.prod(target.shape) for target in targets)
@@ -99,17 +105,22 @@
 class Loads:
     def __init__(self, entry, leave):
         self.entry, self.leave = entry, leave
-        self.near = {"entry": [], "leave": []}
+        self.near = {"entry": [], "leave": [], "away": [], "here": []}
 
     def call(self, body, name, args, specs, outs, pieces=(), **more):
-        loads = tuple((getattr(self, what), first, count) for what, first, count in pieces)
+        half = {"away": 1, "here": 0}
+        loads = tuple(
+            (self.entry if what == "entry" else self.leave, first, count, half.get(what))
+            for what, first, count in pieces
+        )
         results, arrays = kernel_call(body, name, args, specs, outs, loads=loads, **more)
         for (what, first, count), array in zip(pieces, arrays):
             self.near[what].append((first, count, array))
         return results
 
-    def pieces(self, what, first, last):
-        chosen = [p for p in self.near[what] if first <= p[0] and p[0] + p[1] <= last]
+    def pieces(self, first, last, *kinds):
+        held = sum((self.near[what] for what in kinds), [])
+        chosen = [p for p in held if first <= p[0] and p[0] + p[1] <= last]
         assert sum(p[1] for p in chosen) == last - first
         return tuple(p[2] for p in sorted(chosen, key=lambda p: p[0]))
 
@@ -318,16 +329,47 @@
     )[0]
 
 
+def entry_own_kernel(hidden, packed, *refs):
+    near, out = refs[:-1], refs[-1]
+    width = packed.shape[1] - 128
+    start = pl.multiple_of(lax.axis_index("ep") * width, width)
+    turned = packed[:, :width].astype(F32).T.astype(BF16)
+    at = 0
+    for array in near:
+        for first in range(0, array.shape[0], hidden):
+            out[at : at + hidden, :] = jnp.dot(
+                array[first : first + hidden, pl.ds(start, width)],
+                turned,
+                preferred_element_type=F32,
+            )
+            at += hidden
+
+
+def entry_own(loads, pieces, packed, count):
+    _, hidden, width = loads.leave.shape
+    rows = packed.shape[0]
+    near = loads.pieces(0, count, "entry")
+    return loads.call(
+        functools.partial(entry_own_kernel, hidden),
+        "entry_own",
+        (packed, *near),
+        [HERE] * (1 + len(near)),
+        (shaped((count * hidden, rows)),),
+        pieces,
+        cost=(2 * rows * count * hidden * width // 4, count * hidden * width // 2, 0),
+    )[0]
+
+
 def entry_kernel(base, first, n, hidden, *refs):
-    packs, routing, near, rest = refs[:SIDE], refs[SIDE], refs[SIDE + 1 : SIDE + 1 + n], refs[SIDE + 1 + n :]
+    packs, routing, before = refs[:SIDE], refs[SIDE], refs[SIDE + 1]
+    near, rest = refs[SIDE + 2 : SIDE + 2 + n], refs[SIDE + 2 + n :]
     rows, width = packs[0].shape
     width = width - 128
     me = lax.axis_index("ep")
     if first:
-        _, out, turned = rest
+        out, turned = rest
         for k, packed in enumerate(packs):
-            span = pl.ds(pl.multiple_of((me ^ k) * width, width), width)
-            turned[span, :] = packed[:, :width].astype(F32).T.astype(BF16)
+            turned[k * width : (k + 1) * width, :] = packed[:, :width].astype(F32).T.astype(BF16)
     else:
         turned, out = rest
     squares = jnp.zeros((rows, 128), F32)
@@ -346,9 +388,17 @@
         for start in range(0, array.shape[0], hidden):
             chosen = ids == (me * count + base + number).astype(F32)
             share = jnp.sum(jnp.where(chosen, weight, 0.0), axis=0, keepdims=True)
-            total = scale * jnp.dot(
-                array[start : start + hidden, :], turned[...], preferred_element_type=F32
-            )
+            at = (base + number) * hidden
+            begun = at < before.shape[0]
+            total = before[at : at + hidden, :] if begun else 0.0
+            for k in range(1 if begun else 0, SIDE):
+                columns = pl.ds(pl.multiple_of((me ^ k) * width, width), width)
+                total = total + jnp.dot(
+                    array[start : start + hidden, columns],
+                    turned[k * width : (k + 1) * width, :],
+                    preferred_element_type=F32,
+                )
+            total = total * scale
             active = (total / (1.0 + jnp.exp(-total))).astype(BF16).astype(F32) * share
             high = active.astype(BF16).astype(F32)
             pair.append(jnp.concatenate([high, active - high], axis=1))
@@ -360,13 +410,13 @@
                 pair = []
 
 
-def entries(loads, pieces, base, last, packs, routing, mark=None, turned=None):
+def entries(loads, pieces, base, last, packs, routing, before, turned=None):
     _, hidden, width = loads.leave.shape
     count = last - base
     rows = packs[0].shape[0]
-    near = loads.pieces("entry", base, last)
+    near = loads.pieces(base, last, "entry")
     first = turned is None
-    args = (*packs, routing, *near) + ((mark,) if first else (turned,))
+    args = (*packs, routing, before, *near) + (() if first else (turned,))
     outs = (shaped((2 * rows, count * hidden), BF16),)
     if first:
         outs += (shaped((width, rows), BF16),)
@@ -382,20 +432,20 @@
 
 
 def leave_kernel(other, n, m, step, *refs):
-    scaled, near, out = refs[:m], refs[m : m + n], refs[-1]
+    scaled, near, out = refs[:m], refs[m : m + n], refs[m + n + 1]
     rows, half = out.shape
     chip = (lax.axis_index("hd") // 2) ^ other
     for c in range(0, half, step):
-        columns = pl.ds(pl.multiple_of(chip * half + c, step), step)
         total = jnp.zeros((2 * rows, step), F32)
         which, at = 0, 0
         for array in near:
+            start = c if array.shape[1] == half else pl.multiple_of(chip * half + c, step)
             done = 0
             while done < array.shape[0]:
                 depth = min(array.shape[0] - done, scaled[which].shape[1] - at)
                 total = total + jnp.dot(
                     scaled[which][:, at : at + depth],
-                    array[done : done + depth, columns],
+                    array[done : done + depth, pl.ds(start, step)],
                     preferred_element_type=F32,
                 )
                 done, at = done + depth, at + depth
@@ -404,19 +454,20 @@
         out[:, c : c + step] = (total[:rows] + total[rows:]).astype(out.dtype)
 
 
-def leaves(loads, name, other, dtype, scaled, unused):
+def leaves(loads, pieces, name, other, dtype, scaled, unused):
     count, hidden, width = loads.leave.shape
-    near = loads.pieces("leave", 0, count)
+    near = loads.pieces(0, count, "leave", "away" if other else "here")
     rows = scaled[0].shape[0] // 2
-    return kernel_call(
+    return loads.call(
         functools.partial(leave_kernel, other, len(near), len(scaled), 1024),
         name,
         (*scaled, *near, unused),
         [HERE] * (len(scaled) + len(near)) + [ANYWHERE],
         (shaped((rows, width // 2), dtype),),
+        pieces,
         cost=(2 * rows * count * hidden * width, count * hidden * width, 0),
         limit=6,
-    )[0][0]
+    )[0]
 
 
 def halve_kernel(mine, received, keep, send):
@@ -453,12 +504,13 @@
 
 PLAN = {
     "attention": [("entry", 0, 2)],
-    "fetch0": [("entry", 2, 6), ("entry", 8, 2)],
+    "fetch0": [("entry", 2, 6)],
     "projection": [],
-    "fetch1": [("entry", 10, 6)],
-    "fetch2": [("leave", 0, 5)],
-    "entry0": [("leave", 5, 6)],
-    "entry8": [("leave", 11, 5)],
+    "fetch1": [("entry", 8, 7)],
+    "own": [("leave", 0, 7)],
+    "entry0": [("entry", 15, 1), ("leave", 7, 2)],
+    "entry8": [("away", 9, 7)],
+    "leave1": [("here", 9, 7)],
 }
 
 
@@ -498,12 +550,12 @@
     mark = fetch(loads, plan["fetch1"], "fetch1", pair)
     stream, packed = streams(pair, far_pair, mark)
     packs = [packed] + [swap(packed, "ep", k) for k in (1, 2, 3)]
-    mark = fetch(loads, plan["fetch2"], "fetch2", packed)
-    scaled, turned = entries(loads, plan["entry0"], 0, 8, packs, routing, mark)
-    (more,) = entries(loads, plan["entry8"], 8, 16, packs, routing, turned=turned)
+    before = entry_own(loads, plan["own"], packed, 15)
+    scaled, turned = entries(loads, plan["entry0"], 0, 8, packs, routing, before)
+    (more,) = entries(loads, plan["entry8"], 8, 16, packs, routing, before, turned)
     scaled = (scaled, more)
-    theirs = leaves(loads, "leave1", 1, BF16, scaled, more)
-    mine = leaves(loads, "leave0", 0, F32, scaled, theirs)
+    theirs = leaves(loads, plan["leave1"], "leave1", 1, BF16, scaled, more)
+    mine = leaves(loads, (), "leave0", 0, F32, scaled, theirs)
     keep, send = halve(mine, swap(theirs, "hd", 2))
     total, *others = share(keep, swap(send, "hd", 1), stream)
     for k in (3, 2, 1):

time: 56.9 us -> 55 us (0.967)
  Pallas kernels: 29 us -> 27.7 us
  waiting for transfers between devices: 9.13 us -> 8.55 us
    pallas_call x13, Pallas kernels: 29 us -> 27.7 us  [kernel_call(): pl.pallas_call(hosted(body, len(args), len(outs), loads) if loads else bo...]
    ppermute x13, waiting for transfers between devices: 9.13 us -> 8.55 us  [swap(): return lax.ppermute(block, axis, [(i, i ^ k) for i in range(SIDE)])]
  transfers between devices with their start and end apart: 13 -> 13, of which waited for: 7 -> 7; matrix products, arithmetic and copies ran while one was open for 0% -> 0% of each run, Pallas kernels for 25% -> 26%
where the time goes in v5:
time: 55 us; the launch traced here: 54.8 us
  Pallas kernels  27.7 us (50%)
  starting transfers between devices  17.7 us (32%)
  waiting for transfers between devices  8.55 us (16%)
  other arithmetic  0.62 us (1%)
    pallas_call x13, Pallas kernels, kernel_call(): pl.pallas_call(hosted(body, len(args), len(outs), loads) if loads else bo...  27.7 us
    ppermute x13, starting transfers between devices, swap(): return lax.ppermute(block, axis, [(i, i ^ k) for i in range(SIDE)])  17.7 us
    ppermute x13, waiting for transfers between devices, swap(): return lax.ppermute(block, axis, [(i, i ^ k) for i in range(SIDE)])  8.55 us
  transfers between devices with their start and end apart: 13, of which 7 were waited for; matrix products, arithmetic and copies ran while one was open for 0% of the time, Pallas kernels for 26%

profile of v5, /device:TPU:0, one launch (start us, length us, event | category | flops | bytes accessed | tf_op | source)
XLA Modules:
  0.0 54.8 jit_solution(10474662395881488782)
XLA Ops:
  0.0 3.6 %attention.1 = (bf16[8,3200]{1,0:T(8,128)(2,1)S(1)}, bf16[2048,1024]{1,0:T(8,128)(2,1)S(1)}, bf16[32,32]{1,0:T(8,128)(2,1)S(1)}, bf16[384,4096]{1,0:T(8,128)(2,1)S(1)}) custom-call(s32[8]{0:T(128)} %refs_0_.1, bf16[8,2048]{1,0:T(8,128)(2,1)} %refs_1_.1, bf16[8,512,128]{2,1,0:T(8,128)(2,1)} %bitcast.13, s32[8,8]{1,0:T(8,128)} %refs_3_.1, f32[8,8]{1,0:T(8,128)} %refs_4_.1, ...), custom_call_target="tpu_custom_call" | custom-call | flops 140000000 | bytes 15145728 | tf_op jit(solution)/shard_map/attention/pallas_call | solution.py:89
  3.6 5.1 %collective-permute-start.2 = (bf16[8,3200]{1,0:T(8,128)(2,1)S(1)}, bf16[8,3200]{1,0:T(8,128)(2,1)S(1)}, u32[]{:S(2)}, u32[]{:S(2)}) collective-permute-start(bf16[8,3200]{1,0:T(8,128)(2,1)S(1)} %get-tuple-element.34.refs_0_.b0), channel_id=1, source_target_pairs={{0,12},{4,8},{8,4},{12,0},{1,13},{5,9},{9,5},{13,1},{2,14},{6,10},... | collective-permute-start | bytes 153608 | tf_op jit(solution)/shard_map/ppermute | solution.py:30
  8.7 0.0 collective-permute-start.1
  8.7 0.6 %collective-permute-start = (bf16[8,3200]{1,0:T(8,128)(2,1)S(1)}, bf16[8,3200]{1,0:T(8,128)(2,1)S(1)}, u32[]{:S(2)}, u32[]{:S(2)}) collective-permute-start(bf16[8,3200]{1,0:T(8,128)(2,1)S(1)} %get-tuple-element.34.refs_0_.b0), channel_id=1, source_target_pairs={{0,4},{4,0},{8,12},{12,8},{1,5},{5,1},{9,13},{13,9},{2,6},{6,2},{1... | collective-permute-start | bytes 153608 | tf_op jit(solution)/shard_map/ppermute | solution.py:30
  9.4 3.7 %fetch0.1 = (f32[8,128]{1,0:T(8,128)S(1)}, bf16[1152,4096]{1,0:T(8,128)(2,1)S(1)}) custom-call(bf16[8,3200]{1,0:T(8,128)(2,1)S(1)} %get-tuple-element.34.refs_0_.b0, bf16[3072,4096]{1,0:T(8,128)(2,1)} %bitcast.6), custom_call_target="tpu_custom_call" | custom-call | bytes 9437184 | tf_op jit(solution)/shard_map/fetch0/pallas_call | solution.py:89
  13.1 0.0 collective-permute-done.2.b3
  13.1 0.7 %collective-permute-done.1.b2 = bf16[8,3200]{1,0:T(8,128)(2,1)S(1)} collective-permute-done((bf16[8,3200]{1,0:T(8,128)(2,1)S(1)}, bf16[8,3200]{1,0:T(8,128)(2,1)S(1)}, u32[]{:S(2)}, u32[]{:S(2)}) %collective-permute-start.1) | collective-permute-done | bytes 51232 | tf_op jit(solution)/shard_map/ppermute | solution.py:30
  13.7 0.0 collective-permute-done.b1
  13.7 0.9 %projection.1 = (f32[32,1024]{1,0:T(8,128)S(1)}, f32[32,128]{1,0:T(8,128)S(1)}) custom-call(bf16[32,32]{1,0:T(8,128)(2,1)S(1)} %get-tuple-element.33.order, bf16[8,3200]{1,0:T(8,128)(2,1)S(1)} %get-tuple-element.34.refs_0_.b0, bf16[8,3200]{1,0:T(8,128)(2,1)S(1)} %collective-permute-done.b1, bf16[8,3200]{1,0:T(8,128)(2,1)S(1)} %collective-permute-done.1.b2, ...), custom_call_target="tpu_custom_call" | custom-call | flops 140000000 | bytes 4500000 | tf_op jit(solution)/shard_map/projection/pallas_call | solution.py:89
  14.7 0.0 collective-permute-start.3
  14.7 1.3 %collective-permute-done.3.b = f32[32,1024]{1,0:T(8,128)S(1)} collective-permute-done((f32[32,1024]{1,0:T(8,128)S(1)}, f32[32,1024]{1,0:T(8,128)S(1)}, u32[]{:S(2)}, u32[]{:S(2)}) %collective-permute-start.3) | collective-permute-done | bytes 131104 | tf_op jit(solution)/shard_map/ppermute | solution.py:30
  16.1 1.6 %collective-permute-start.4 = (f32[32,1024]{1,0:T(8,128)S(1)}, f32[32,1024]{1,0:T(8,128)S(1)}, u32[]{:S(2)}, u32[]{:S(2)}) collective-permute-start(f32[32,1024]{1,0:T(8,128)S(1)} %add.16.refs_0_.a), channel_id=1, source_target_pairs={{0,2},{1,3},{2,0},{3,1},{4,6},{5,7},{6,4},{7,5},{8,10},{9,11},{10,... | collective-permute-start | bytes 393224 | tf_op jit(solution)/shard_map/ppermute | solution.py:30
  17.6 4.1 %fetch1.1 = (f32[8,128]{1,0:T(8,128)S(1)}, bf16[1344,4096]{1,0:T(8,128)(2,1)S(1)}) custom-call(f32[32,1024]{1,0:T(8,128)S(1)} %add.16.refs_0_.a, bf16[3072,4096]{1,0:T(8,128)(2,1)} %bitcast.7), custom_call_target="tpu_custom_call" | custom-call | bytes 11010048 | tf_op jit(solution)/shard_map/fetch1/pallas_call | solution.py:89
  21.8 0.0 collective-permute-done.4.b
  21.8 0.1 stream.1
  21.9 3.2 %collective-permute-start.7 = (bf16[32,1152]{1,0:T(8,128)(2,1)S(1)}, bf16[32,1152]{1,0:T(8,128)(2,1)S(1)}, u32[]{:S(2)}, u32[]{:S(2)}) collective-permute-start(bf16[32,1152]{1,0:T(8,128)(2,1)S(1)} %get-tuple-element.39.refs_0_), channel_id=1, source_target_pairs={{0,12},{4,8},{8,4},{12,0},{1,13},{5,9},{9,5},{13,1},{2,14},{6,10},... | collective-permute-start | bytes 221192 | tf_op jit(solution)/shard_map/ppermute | solution.py:30
  25.1 0.0 collective-permute-start.6
  25.1 1.3 %collective-permute-start.5 = (bf16[32,1152]{1,0:T(8,128)(2,1)S(1)}, bf16[32,1152]{1,0:T(8,128)(2,1)S(1)}, u32[]{:S(2)}, u32[]{:S(2)}) collective-permute-start(bf16[32,1152]{1,0:T(8,128)(2,1)S(1)} %get-tuple-element.39.refs_0_), channel_id=1, source_target_pairs={{0,4},{4,0},{8,12},{12,8},{1,5},{5,1},{9,13},{13,9},{2,6},{6,2},{1... | collective-permute-start | bytes 221192 | tf_op jit(solution)/shard_map/ppermute | solution.py:30
  26.3 4.1 %entry_own.1 = (f32[2880,32]{1,0:T(8,128)S(1)}, bf16[1344,4096]{1,0:T(8,128)(2,1)S(1)}) custom-call(bf16[32,1152]{1,0:T(8,128)(2,1)S(1)} %get-tuple-element.39.refs_0_, bf16[384,4096]{1,0:T(8,128)(2,1)S(1)} %get-tuple-element.41.refs_1_.refs_6_, bf16[1152,4096]{1,0:T(8,128)(2,1)S(1)} %get-tuple-element.42.refs_2_.refs_7_, ...), custom_call_target="tpu_custom_call" | custom-call | flops 188743680 | bytes 16908288 | tf_op jit(solution)/shard_map/entry_own/pallas_call | solution.py:89
  30.5 0.0 collective-permute-done.7.refs_3_
  30.5 0.7 %collective-permute-done.6.refs_2_ = bf16[32,1152]{1,0:T(8,128)(2,1)S(1)} collective-permute-done((bf16[32,1152]{1,0:T(8,128)(2,1)S(1)}, bf16[32,1152]{1,0:T(8,128)(2,1)S(1)}, u32[]{:S(2)}, u32[]{:S(2)}) %collective-permute-start.6) | collective-permute-done | bytes 73760 | tf_op jit(solution)/shard_map/ppermute | solution.py:30
  31.2 0.0 collective-permute-done.5.refs_1_
  31.2 3.1 %entry0.1 = (bf16[64,1536]{1,0:T(8,128)(2,1)S(1)}, bf16[4096,32]{1,0:T(8,128)(2,1)S(1)}, bf16[192,4096]{1,0:T(8,128)(2,1)S(1)}, bf16[384,4096]{1,0:T(8,128)(2,1)S(1)}) custom-call(bf16[32,1152]{1,0:T(8,128)(2,1)S(1)} %get-tuple-element.39.refs_0_, bf16[32,1152]{1,0:T(8,128)(2,1)S(1)} %collective-permute-done.5.refs_1_, ...), custom_call_target="tpu_custom_call" | custom-call | flops 402653184 | bytes 17301504 | tf_op jit(solution)/shard_map/entry0/pallas_call | solution.py:89
  34.3 3.0 %entry8.1 = (bf16[64,1536]{1,0:T(8,128)(2,1)S(1)}, bf16[1344,2048]{1,0:T(8,128)(2,1)S(1)}) custom-call(bf16[32,1152]{1,0:T(8,128)(2,1)S(1)} %get-tuple-element.39.refs_0_, bf16[32,1152]{1,0:T(8,128)(2,1)S(1)} %collective-permute-done.5.refs_1_, bf16[32,1152]{1,0:T(8,128)(2,1)S(1)} %collective-permute-done.6.refs_2_, ...), custom_call_target="tpu_custom_call" | custom-call | flops 402653184 | bytes 18087936 | tf_op jit(solution)/shard_map/entry8/pallas_call | solution.py:89
  37.3 2.6 %leave1.1 = (bf16[32,2048]{1,0:T(8,128)(2,1)S(1)}, bf16[1344,2048]{1,0:T(8,128)(2,1)S(1)}) custom-call(bf16[64,1536]{1,0:T(8,128)(2,1)S(1)} %get-tuple-element.45.refs_0_, bf16[64,1536]{1,0:T(8,128)(2,1)S(1)} %get-tuple-element.48.refs_1_.refs_5_, bf16[1344,4096]{1,0:T(8,128)(2,1)S(1)} %get-tuple-element.49.refs_2_, ...), custom_call_target="tpu_custom_call" | custom-call | flops 805306368 | bytes 18087936 | tf_op jit(solution)/shard_map/leave1/pallas_call | solution.py:89
  39.9 1.4 %collective-permute-start.8 = (bf16[32,2048]{1,0:T(8,128)(2,1)S(1)}, bf16[32,2048]{1,0:T(8,128)(2,1)S(1)}, u32[]{:S(2)}, u32[]{:S(2)}) collective-permute-start(bf16[32,2048]{1,0:T(8,128)(2,1)S(1)} %get-tuple-element.53.refs_5_), channel_id=1, source_target_pairs={{0,2},{1,3},{2,0},{3,1},{4,6},{5,7},{6,4},{7,5},{8,10},{9,11},{10,... | collective-permute-start | bytes 393224 | tf_op jit(solution)/shard_map/ppermute | solution.py:30
  41.3 2.4 %leave0.1.mine = f32[32,2048]{1,0:T(8,128)S(1)} custom-call(bf16[64,1536]{1,0:T(8,128)(2,1)S(1)} %get-tuple-element.45.refs_0_, bf16[64,1536]{1,0:T(8,128)(2,1)S(1)} %get-tuple-element.48.refs_1_.refs_5_, bf16[1344,4096]{1,0:T(8,128)(2,1)S(1)} %get-tuple-element.49.refs_2_, bf16[384,4096]{1,0:T(8,128)(2,1)S(1)} %get-tuple-element.50.refs_3_, ...), custom_call_target="tpu_custom_call" | custom-call | flops 805306368 | bytes 12582912 | tf_op jit(solution)/shard_map/leave0/pallas_call | solution.py:89
  43.7 1.6 %collective-permute-done.8.received = bf16[32,2048]{1,0:T(8,128)(2,1)S(1)} collective-permute-done((bf16[32,2048]{1,0:T(8,128)(2,1)S(1)}, bf16[32,2048]{1,0:T(8,128)(2,1)S(1)}, u32[]{:S(2)}, u32[]{:S(2)}) %collective-permute-start.8) | collective-permute-done | bytes 131104 | tf_op jit(solution)/shard_map/ppermute | solution.py:30
  45.4 0.1 collective-permute-start.9
  45.5 1.3 %collective-permute-done.9.received = f32[32,1024]{1,0:T(8,128)S(1)} collective-permute-done((f32[32,1024]{1,0:T(8,128)S(1)}, f32[32,1024]{1,0:T(8,128)S(1)}, u32[]{:S(2)}, u32[]{:S(2)}) %collective-permute-start.9) | collective-permute-done | bytes 131104 | tf_op jit(solution)/shard_map/ppermute | solution.py:30
  46.9 2.5 %collective-permute-start.10 = (f32[8,1024]{1,0:T(8,128)S(1)}, f32[8,1024]{1,0:T(8,128)S(1)}, u32[]{:S(2)}, u32[]{:S(2)}) collective-permute-start(f32[8,1024]{1,0:T(8,128)S(1)} %get-tuple-element.58), channel_id=1, source_target_pairs={{0,12},{4,8},{8,4},{12,0},{1,13},{5,9},{9,5},{13,1},{2,14},{6,10},... | collective-permute-start | bytes 98312 | tf_op jit(solution)/shard_map/ppermute | solution.py:30
  49.3 0.0 collective-permute-start.11
  49.3 2.0 %collective-permute-start.12 = (f32[8,1024]{1,0:T(8,128)S(1)}, f32[8,1024]{1,0:T(8,128)S(1)}, u32[]{:S(2)}, u32[]{:S(2)}) collective-permute-start(f32[8,1024]{1,0:T(8,128)S(1)} %get-tuple-element.60), channel_id=1, source_target_pairs={{0,4},{4,0},{8,12},{12,8},{1,5},{5,1},{9,13},{13,9},{2,6},{6,2},{1... | collective-permute-start | bytes 98312 | tf_op jit(solution)/shard_map/ppermute | solution.py:30
  51.3 1.3 %collective-permute-done.10 = f32[8,1024]{1,0:T(8,128)S(1)} collective-permute-done((f32[8,1024]{1,0:T(8,128)S(1)}, f32[8,1024]{1,0:T(8,128)S(1)}, u32[]{:S(2)}, u32[]{:S(2)}) %collective-permute-start.10) | collective-permute-done | bytes 32800 | tf_op jit(solution)/shard_map/ppermute | solution.py:30
  52.6 1.5 %collective-permute-done.11 = f32[8,1024]{1,0:T(8,128)S(1)} collective-permute-done((f32[8,1024]{1,0:T(8,128)S(1)}, f32[8,1024]{1,0:T(8,128)S(1)}, u32[]{:S(2)}, u32[]{:S(2)}) %collective-permute-start.11) | collective-permute-done | bytes 32800 | tf_op jit(solution)/shard_map/ppermute | solution.py:30
  54.1 0.0 collective-permute-done.12
  54.1 0.6 %add_convert_fusion = bf16[8,1024]{1,0:T(8,128)(2,1)} fusion(f32[8,1024]{1,0:T(8,128)S(1)} %collective-permute-done.12, f32[8,1024]{1,0:T(8,128)S(1)} %collective-permute-done.11, f32[8,1024]{1,0:T(8,128)S(1)} %get-tuple-element.57, f32[8,1024]{1,0:T(8,128)S(1)} %collective-permute-done.10), kind=kLoop, calls=%fused_computation | loop fusion | flops 32768 | bytes 147456 | tf_op jit(solution)/shard_map/convert_element_type | solution.py:563
  (3 shorter events, 0.1 us)
Async XLA Ops:
  3.6 9.5 %collective-permute-start.2 = (bf16[8,3200]{1,0:T(8,128)(2,1)S(1)}, bf16[8,3200]{1,0:T(8,128)(2,1)S(1)}, u32[]{:S(2)}, u32[]{:S(2)}) collective-permute-start(bf16[8,3200]{1,0:T(8,128)(2,1)S(1)} %get-tuple-element.34.refs_0_.b0), channel_id=1, source_target_pairs={{0,12},{4,8},{8,4},{12,0},{1,13},{5,9},{9,5},{13,1},{2,14},{6,10},... | collective-permute-start | bytes 153608 | tf_op jit(solution)/shard_map/ppermute | solution.py:30
  8.7 5.0 %collective-permute-start.1 = (bf16[8,3200]{1,0:T(8,128)(2,1)S(1)}, bf16[8,3200]{1,0:T(8,128)(2,1)S(1)}, u32[]{:S(2)}, u32[]{:S(2)}) collective-permute-start(bf16[8,3200]{1,0:T(8,128)(2,1)S(1)} %get-tuple-element.34.refs_0_.b0), channel_id=1, source_target_pairs={{0,8},{4,12},{8,0},{12,4},{1,9},{5,13},{9,1},{13,5},{2,10},{6,14},... | collective-permute-start | bytes 153608 | tf_op jit(solution)/shard_map/ppermute | solution.py:30
  8.7 5.0 %collective-permute-start = (bf16[8,3200]{1,0:T(8,128)(2,1)S(1)}, bf16[8,3200]{1,0:T(8,128)(2,1)S(1)}, u32[]{:S(2)}, u32[]{:S(2)}) collective-permute-start(bf16[8,3200]{1,0:T(8,128)(2,1)S(1)} %get-tuple-element.34.refs_0_.b0), channel_id=1, source_target_pairs={{0,4},{4,0},{8,12},{12,8},{1,5},{5,1},{9,13},{13,9},{2,6},{6,2},{1... | collective-permute-start | bytes 153608 | tf_op jit(solution)/shard_map/ppermute | solution.py:30
  14.7 1.4 %collective-permute-start.3 = (f32[32,1024]{1,0:T(8,128)S(1)}, f32[32,1024]{1,0:T(8,128)S(1)}, u32[]{:S(2)}, u32[]{:S(2)}) collective-permute-start(f32[32,1024]{1,0:T(8,128)S(1)} %get-tuple-element.37.a), channel_id=1, source_target_pairs={{0,1},{1,0},{2,3},{3,2},{4,5},{5,4},{6,7},{7,6},{8,9},{9,8},{10,11... | collective-permute-start | bytes 393224 | tf_op jit(solution)/shard_map/ppermute | solution.py:30
  16.1 5.7 %collective-permute-start.4 = (f32[32,1024]{1,0:T(8,128)S(1)}, f32[32,1024]{1,0:T(8,128)S(1)}, u32[]{:S(2)}, u32[]{:S(2)}) collective-permute-start(f32[32,1024]{1,0:T(8,128)S(1)} %add.16.refs_0_.a), channel_id=1, source_target_pairs={{0,2},{1,3},{2,0},{3,1},{4,6},{5,7},{6,4},{7,5},{8,10},{9,11},{10,... | collective-permute-start | bytes 393224 | tf_op jit(solution)/shard_map/ppermute | solution.py:30
  21.9 8.6 %collective-permute-start.7 = (bf16[32,1152]{1,0:T(8,128)(2,1)S(1)}, bf16[32,1152]{1,0:T(8,128)(2,1)S(1)}, u32[]{:S(2)}, u32[]{:S(2)}) collective-permute-start(bf16[32,1152]{1,0:T(8,128)(2,1)S(1)} %get-tuple-element.39.refs_0_), channel_id=1, source_target_pairs={{0,12},{4,8},{8,4},{12,0},{1,13},{5,9},{9,5},{13,1},{2,14},{6,10},... | collective-permute-start | bytes 221192 | tf_op jit(solution)/shard_map/ppermute | solution.py:30
  25.1 6.2 %collective-permute-start.6 = (bf16[32,1152]{1,0:T(8,128)(2,1)S(1)}, bf16[32,1152]{1,0:T(8,128)(2,1)S(1)}, u32[]{:S(2)}, u32[]{:S(2)}) collective-permute-start(bf16[32,1152]{1,0:T(8,128)(2,1)S(1)} %get-tuple-element.39.refs_0_), channel_id=1, source_target_pairs={{0,8},{4,12},{8,0},{12,4},{1,9},{5,13},{9,1},{13,5},{2,10},{6,14},... | collective-permute-start | bytes 221192 | tf_op jit(solution)/shard_map/ppermute | solution.py:30
  25.1 6.2 %collective-permute-start.5 = (bf16[32,1152]{1,0:T(8,128)(2,1)S(1)}, bf16[32,1152]{1,0:T(8,128)(2,1)S(1)}, u32[]{:S(2)}, u32[]{:S(2)}) collective-permute-start(bf16[32,1152]{1,0:T(8,128)(2,1)S(1)} %get-tuple-element.39.refs_0_), channel_id=1, source_target_pairs={{0,4},{4,0},{8,12},{12,8},{1,5},{5,1},{9,13},{13,9},{2,6},{6,2},{1... | collective-permute-start | bytes 221192 | tf_op jit(solution)/shard_map/ppermute | solution.py:30
  39.9 5.5 %collective-permute-start.8 = (bf16[32,2048]{1,0:T(8,128)(2,1)S(1)}, bf16[32,2048]{1,0:T(8,128)(2,1)S(1)}, u32[]{:S(2)}, u32[]{:S(2)}) collective-permute-start(bf16[32,2048]{1,0:T(8,128)(2,1)S(1)} %get-tuple-element.53.refs_5_), channel_id=1, source_target_pairs={{0,2},{1,3},{2,0},{3,1},{4,6},{5,7},{6,4},{7,5},{8,10},{9,11},{10,... | collective-permute-start | bytes 393224 | tf_op jit(solution)/shard_map/ppermute | solution.py:30
  45.4 1.4 %collective-permute-start.9 = (f32[32,1024]{1,0:T(8,128)S(1)}, f32[32,1024]{1,0:T(8,128)S(1)}, u32[]{:S(2)}, u32[]{:S(2)}) collective-permute-start(f32[32,1024]{1,0:T(8,128)S(1)} %get-tuple-element.55), channel_id=1, source_target_pairs={{0,1},{1,0},{2,3},{3,2},{4,5},{5,4},{6,7},{7,6},{8,9},{9,8},{10,11... | collective-permute-start | bytes 393224 | tf_op jit(solution)/shard_map/ppermute | solution.py:30
  46.9 5.8 %collective-permute-start.10 = (f32[8,1024]{1,0:T(8,128)S(1)}, f32[8,1024]{1,0:T(8,128)S(1)}, u32[]{:S(2)}, u32[]{:S(2)}) collective-permute-start(f32[8,1024]{1,0:T(8,128)S(1)} %get-tuple-element.58), channel_id=1, source_target_pairs={{0,12},{4,8},{8,4},{12,0},{1,13},{5,9},{9,5},{13,1},{2,14},{6,10},... | collective-permute-start | bytes 98312 | tf_op jit(solution)/shard_map/ppermute | solution.py:30
  49.3 4.8 %collective-permute-start.11 = (f32[8,1024]{1,0:T(8,128)S(1)}, f32[8,1024]{1,0:T(8,128)S(1)}, u32[]{:S(2)}, u32[]{:S(2)}) collective-permute-start(f32[8,1024]{1,0:T(8,128)S(1)} %get-tuple-element.59), channel_id=1, source_target_pairs={{0,8},{4,12},{8,0},{12,4},{1,9},{5,13},{9,1},{13,5},{2,10},{6,14},... | collective-permute-start | bytes 98312 | tf_op jit(solution)/shard_map/ppermute | solution.py:30
  49.3 4.8 %collective-permute-start.12 = (f32[8,1024]{1,0:T(8,128)S(1)}, f32[8,1024]{1,0:T(8,128)S(1)}, u32[]{:S(2)}, u32[]{:S(2)}) collective-permute-start(f32[8,1024]{1,0:T(8,128)S(1)} %get-tuple-element.60), channel_id=1, source_target_pairs={{0,4},{4,0},{8,12},{12,8},{1,5},{5,1},{9,13},{13,9},{2,6},{6,2},{1... | collective-permute-start | bytes 98312 | tf_op jit(solution)/shard_map/ppermute | solution.py:30

commit v6 on v5

--- a/solution.py
+++ b/solution.py
@@ -87,11 +87,11 @@
     flops, bytes_accessed, transcendentals = cost
     bytes_accessed += sum(2 * math.prod(target.shape) for target in targets)
     results = pl.pallas_call(
-        hosted(body, len(args), len(outs), loads) if loads else body,
+        hosted(body, len(args), len(outs), loads) if loads or body is attention_kernel else body,
         out_shape=(*outs, *targets),
         in_specs=[*specs] + [ANYWHERE] * len(loads),
         out_specs=(HERE,) * (len(outs) + len(targets)),
-        scratch_shapes=[*scratch] + ([DMA((len(loads),))] if loads else []),
+        scratch_shapes=[*scratch] + ([DMA((max(1, len(loads)),))] if loads or body is attention_kernel else []),
         input_output_aliases=aliases or {},
         compiler_params=pltpu.CompilerParams(vmem_limit_bytes=limit * MIB),
         cost_estimate=pl.CostEstimate(
@@ -503,12 +503,12 @@
 
 
 PLAN = {
-    "attention": [("entry", 0, 2)],
-    "fetch0": [("entry", 2, 6)],
+    "attention": [],
+    "fetch0": [("entry", 0, 6)],
     "projection": [],
-    "fetch1": [("entry", 8, 7)],
-    "own": [("leave", 0, 7)],
-    "entry0": [("entry", 15, 1), ("leave", 7, 2)],
+    "fetch1": [("entry", 6, 2), ("entry", 8, 5)],
+    "own": [("leave", 0, 8)],
+    "entry0": [("entry", 13, 3), ("leave", 8, 1)],
     "entry8": [("away", 9, 7)],
     "leave1": [("here", 9, 7)],
 }
@@ -550,7 +550,7 @@
     mark = fetch(loads, plan["fetch1"], "fetch1", pair)
     stream, packed = streams(pair, far_pair, mark)
     packs = [packed] + [swap(packed, "ep", k) for k in (1, 2, 3)]
-    before = entry_own(loads, plan["own"], packed, 15)
+    before = entry_own(loads, plan["own"], packed, 13)
     scaled, turned = entries(loads, plan["entry0"], 0, 8, packs, routing, before)
     (more,) = entries(loads, plan["entry8"], 8, 16, packs, routing, before, turned)
     scaled = (scaled, more)

time: 55 us -> 54.4 us (0.989)
  transfers between devices with their start and end apart: 13 -> 13, of which waited for: 7 -> 7; matrix products, arithmetic and copies ran while one was open for 0% -> 0% of each run, Pallas kernels for 26% -> 27%
where the time goes in v6:
time: 54.4 us; the launch traced here: 54.1 us
  Pallas kernels  27.5 us (51%)
  starting transfers between devices  17.7 us (33%)
  waiting for transfers between devices  8.27 us (15%)
  other arithmetic  0.62 us (1%)
    pallas_call x13, Pallas kernels, kernel_call(): pl.pallas_call(hosted(body, len(args), len(outs), loads) if loads or body...  27.5 us
    ppermute x13, starting transfers between devices, swap(): return lax.ppermute(block, axis, [(i, i ^ k) for i in range(SIDE)])  17.7 us
    ppermute x13, waiting for transfers between devices, swap(): return lax.ppermute(block, axis, [(i, i ^ k) for i in range(SIDE)])  8.27 us
  transfers between devices with their start and end apart: 13, of which 7 were waited for; matrix products, arithmetic and copies ran while one was open for 0% of the time, Pallas kernels for 27%

profile of v6, /device:TPU:0, one launch (start us, length us, event | category | flops | bytes accessed | tf_op | source)
XLA Modules:
  0.0 54.1 jit_solution(8626050013587871726)
XLA Ops:
  0.0 2.7 %attention.1 = (bf16[8,3200]{1,0:T(8,128)(2,1)S(1)}, bf16[2048,1024]{1,0:T(8,128)(2,1)S(1)}, bf16[32,32]{1,0:T(8,128)(2,1)S(1)}) custom-call(s32[8]{0:T(128)} %refs_0_.1, bf16[8,2048]{1,0:T(8,128)(2,1)} %refs_1_.1, bf16[8,512,128]{2,1,0:T(8,128)(2,1)} %bitcast.13, s32[8,8]{1,0:T(8,128)} %refs_3_.1, f32[8,8]{1,0:T(8,128)} %refs_4_.1, ...), custom_call_target="tpu_custom_call" | custom-call | flops 140000000 | bytes 12000000 | tf_op jit(solution)/shard_map/attention/pallas_call | solution.py:89
  2.7 5.1 %collective-permute-start.2 = (bf16[8,3200]{1,0:T(8,128)(2,1)S(1)}, bf16[8,3200]{1,0:T(8,128)(2,1)S(1)}, u32[]{:S(2)}, u32[]{:S(2)}) collective-permute-start(bf16[8,3200]{1,0:T(8,128)(2,1)S(1)} %get-tuple-element.34.refs_0_.b0), channel_id=1, source_target_pairs={{0,12},{4,8},{8,4},{12,0},{1,13},{5,9},{9,5},{13,1},{2,14},{6,10},... | collective-permute-start | bytes 153608 | tf_op jit(solution)/shard_map/ppermute | solution.py:30
  7.8 0.0 collective-permute-start.1
  7.8 0.6 %collective-permute-start = (bf16[8,3200]{1,0:T(8,128)(2,1)S(1)}, bf16[8,3200]{1,0:T(8,128)(2,1)S(1)}, u32[]{:S(2)}, u32[]{:S(2)}) collective-permute-start(bf16[8,3200]{1,0:T(8,128)(2,1)S(1)} %get-tuple-element.34.refs_0_.b0), channel_id=1, source_target_pairs={{0,4},{4,0},{8,12},{12,8},{1,5},{5,1},{9,13},{13,9},{2,6},{6,2},{1... | collective-permute-start | bytes 153608 | tf_op jit(solution)/shard_map/ppermute | solution.py:30
  8.4 3.7 %fetch0.1 = (f32[8,128]{1,0:T(8,128)S(1)}, bf16[1152,4096]{1,0:T(8,128)(2,1)S(1)}) custom-call(bf16[8,3200]{1,0:T(8,128)(2,1)S(1)} %get-tuple-element.34.refs_0_.b0, bf16[3072,4096]{1,0:T(8,128)(2,1)} %bitcast.5), custom_call_target="tpu_custom_call" | custom-call | bytes 9437184 | tf_op jit(solution)/shard_map/fetch0/pallas_call | solution.py:89
  12.1 0.0 collective-permute-done.2.b3
  12.1 0.7 %collective-permute-done.1.b2 = bf16[8,3200]{1,0:T(8,128)(2,1)S(1)} collective-permute-done((bf16[8,3200]{1,0:T(8,128)(2,1)S(1)}, bf16[8,3200]{1,0:T(8,128)(2,1)S(1)}, u32[]{:S(2)}, u32[]{:S(2)}) %collective-permute-start.1) | collective-permute-done | bytes 51232 | tf_op jit(solution)/shard_map/ppermute | solution.py:30
  12.8 0.0 collective-permute-done.b1
  12.8 0.9 %projection.1 = (f32[32,1024]{1,0:T(8,128)S(1)}, f32[32,128]{1,0:T(8,128)S(1)}) custom-call(bf16[32,32]{1,0:T(8,128)(2,1)S(1)} %get-tuple-element.33.order, bf16[8,3200]{1,0:T(8,128)(2,1)S(1)} %get-tuple-element.34.refs_0_.b0, bf16[8,3200]{1,0:T(8,128)(2,1)S(1)} %collective-permute-done.b1, bf16[8,3200]{1,0:T(8,128)(2,1)S(1)} %collective-permute-done.1.b2, ...), custom_call_target="tpu_custom_call" | custom-call | flops 140000000 | bytes 4500000 | tf_op jit(solution)/shard_map/projection/pallas_call | solution.py:89
  13.7 0.0 collective-permute-start.3
  13.8 1.3 %collective-permute-done.3.b = f32[32,1024]{1,0:T(8,128)S(1)} collective-permute-done((f32[32,1024]{1,0:T(8,128)S(1)}, f32[32,1024]{1,0:T(8,128)S(1)}, u32[]{:S(2)}, u32[]{:S(2)}) %collective-permute-start.3) | collective-permute-done | bytes 131104 | tf_op jit(solution)/shard_map/ppermute | solution.py:30
  15.1 1.6 %collective-permute-start.4 = (f32[32,1024]{1,0:T(8,128)S(1)}, f32[32,1024]{1,0:T(8,128)S(1)}, u32[]{:S(2)}, u32[]{:S(2)}) collective-permute-start(f32[32,1024]{1,0:T(8,128)S(1)} %add.16.refs_0_.a), channel_id=1, source_target_pairs={{0,2},{1,3},{2,0},{3,1},{4,6},{5,7},{6,4},{7,5},{8,10},{9,11},{10,... | collective-permute-start | bytes 393224 | tf_op jit(solution)/shard_map/ppermute | solution.py:30
  16.7 4.2 %fetch1.1 = (f32[8,128]{1,0:T(8,128)S(1)}, bf16[384,4096]{1,0:T(8,128)(2,1)S(1)}, bf16[960,4096]{1,0:T(8,128)(2,1)S(1)}) custom-call(f32[32,1024]{1,0:T(8,128)S(1)} %add.16.refs_0_.a, bf16[3072,4096]{1,0:T(8,128)(2,1)} %bitcast.6, bf16[3072,4096]{1,0:T(8,128)(2,1)} %bitcast.7), custom_call_target="tpu_custom_call" | custom-call | bytes 11010048 | tf_op jit(solution)/shard_map/fetch1/pallas_call | solution.py:89
  20.9 0.0 collective-permute-done.4.b
  20.9 0.1 stream.1
  21.0 3.2 %collective-permute-start.7 = (bf16[32,1152]{1,0:T(8,128)(2,1)S(1)}, bf16[32,1152]{1,0:T(8,128)(2,1)S(1)}, u32[]{:S(2)}, u32[]{:S(2)}) collective-permute-start(bf16[32,1152]{1,0:T(8,128)(2,1)S(1)} %get-tuple-element.39.refs_0_), channel_id=1, source_target_pairs={{0,12},{4,8},{8,4},{12,0},{1,13},{5,9},{9,5},{13,1},{2,14},{6,10},... | collective-permute-start | bytes 221192 | tf_op jit(solution)/shard_map/ppermute | solution.py:30
  24.2 0.0 collective-permute-start.6
  24.2 1.3 %collective-permute-start.5 = (bf16[32,1152]{1,0:T(8,128)(2,1)S(1)}, bf16[32,1152]{1,0:T(8,128)(2,1)S(1)}, u32[]{:S(2)}, u32[]{:S(2)}) collective-permute-start(bf16[32,1152]{1,0:T(8,128)(2,1)S(1)} %get-tuple-element.39.refs_0_), channel_id=1, source_target_pairs={{0,4},{4,0},{8,12},{12,8},{1,5},{5,1},{9,13},{13,9},{2,6},{6,2},{1... | collective-permute-start | bytes 221192 | tf_op jit(solution)/shard_map/ppermute | solution.py:30
  25.5 4.6 %entry_own.1 = (f32[2496,32]{1,0:T(8,128)S(1)}, bf16[1536,4096]{1,0:T(8,128)(2,1)S(1)}) custom-call(bf16[32,1152]{1,0:T(8,128)(2,1)S(1)} %get-tuple-element.39.refs_0_, bf16[1152,4096]{1,0:T(8,128)(2,1)S(1)} %get-tuple-element.41.refs_1_.refs_6_, bf16[384,4096]{1,0:T(8,128)(2,1)S(1)} %get-tuple-element.42.refs_2_.refs_7_, ...), custom_call_target="tpu_custom_call" | custom-call | flops 163577856 | bytes 17694720 | tf_op jit(solution)/shard_map/entry_own/pallas_call | solution.py:89
  30.0 0.0 collective-permute-done.7.refs_3_
  30.1 0.3 collective-permute-done.6.refs_2_
  30.4 0.0 collective-permute-done.5.refs_1_
  30.4 3.1 %entry0.1 = (bf16[64,1536]{1,0:T(8,128)(2,1)S(1)}, bf16[4096,32]{1,0:T(8,128)(2,1)S(1)}, bf16[576,4096]{1,0:T(8,128)(2,1)S(1)}, bf16[192,4096]{1,0:T(8,128)(2,1)S(1)}) custom-call(bf16[32,1152]{1,0:T(8,128)(2,1)S(1)} %get-tuple-element.39.refs_0_, bf16[32,1152]{1,0:T(8,128)(2,1)S(1)} %collective-permute-done.5.refs_1_, ...), custom_call_target="tpu_custom_call" | custom-call | flops 402653184 | bytes 18874368 | tf_op jit(solution)/shard_map/entry0/pallas_call | solution.py:89
  33.4 3.3 %entry8.1 = (bf16[64,1536]{1,0:T(8,128)(2,1)S(1)}, bf16[1344,2048]{1,0:T(8,128)(2,1)S(1)}) custom-call(bf16[32,1152]{1,0:T(8,128)(2,1)S(1)} %get-tuple-element.39.refs_0_, bf16[32,1152]{1,0:T(8,128)(2,1)S(1)} %collective-permute-done.5.refs_1_, bf16[32,1152]{1,0:T(8,128)(2,1)S(1)} %collective-permute-done.6.refs_2_, ...), custom_call_target="tpu_custom_call" | custom-call | flops 402653184 | bytes 18087936 | tf_op jit(solution)/shard_map/entry8/pallas_call | solution.py:89
  36.7 2.6 %leave1.1 = (bf16[32,2048]{1,0:T(8,128)(2,1)S(1)}, bf16[1344,2048]{1,0:T(8,128)(2,1)S(1)}) custom-call(bf16[64,1536]{1,0:T(8,128)(2,1)S(1)} %get-tuple-element.45.refs_0_, bf16[64,1536]{1,0:T(8,128)(2,1)S(1)} %get-tuple-element.48.refs_1_.refs_5_, bf16[1536,4096]{1,0:T(8,128)(2,1)S(1)} %get-tuple-element.49.refs_2_, ...), custom_call_target="tpu_custom_call" | custom-call | flops 805306368 | bytes 18087936 | tf_op jit(solution)/shard_map/leave1/pallas_call | solution.py:89
  39.3 1.3 %collective-permute-start.8 = (bf16[32,2048]{1,0:T(8,128)(2,1)S(1)}, bf16[32,2048]{1,0:T(8,128)(2,1)S(1)}, u32[]{:S(2)}, u32[]{:S(2)}) collective-permute-start(bf16[32,2048]{1,0:T(8,128)(2,1)S(1)} %get-tuple-element.53.refs_5_), channel_id=1, source_target_pairs={{0,2},{1,3},{2,0},{3,1},{4,6},{5,7},{6,4},{7,5},{8,10},{9,11},{10,... | collective-permute-start | bytes 393224 | tf_op jit(solution)/shard_map/ppermute | solution.py:30
  40.6 2.3 %leave0.1.mine = f32[32,2048]{1,0:T(8,128)S(1)} custom-call(bf16[64,1536]{1,0:T(8,128)(2,1)S(1)} %get-tuple-element.45.refs_0_, bf16[64,1536]{1,0:T(8,128)(2,1)S(1)} %get-tuple-element.48.refs_1_.refs_5_, bf16[1536,4096]{1,0:T(8,128)(2,1)S(1)} %get-tuple-element.49.refs_2_, bf16[192,4096]{1,0:T(8,128)(2,1)S(1)} %get-tuple-element.50.refs_3_, ...), custom_call_target="tpu_custom_call" | custom-call | flops 805306368 | bytes 12582912 | tf_op jit(solution)/shard_map/leave0/pallas_call | solution.py:89
  43.0 1.8 %collective-permute-done.8.received = bf16[32,2048]{1,0:T(8,128)(2,1)S(1)} collective-permute-done((bf16[32,2048]{1,0:T(8,128)(2,1)S(1)}, bf16[32,2048]{1,0:T(8,128)(2,1)S(1)}, u32[]{:S(2)}, u32[]{:S(2)}) %collective-permute-start.8) | collective-permute-done | bytes 131104 | tf_op jit(solution)/shard_map/ppermute | solution.py:30
  44.8 0.1 collective-permute-start.9
  44.9 1.3 %collective-permute-done.9.received = f32[32,1024]{1,0:T(8,128)S(1)} collective-permute-done((f32[32,1024]{1,0:T(8,128)S(1)}, f32[32,1024]{1,0:T(8,128)S(1)}, u32[]{:S(2)}, u32[]{:S(2)}) %collective-permute-start.9) | collective-permute-done | bytes 131104 | tf_op jit(solution)/shard_map/ppermute | solution.py:30
  46.2 2.5 %collective-permute-start.10 = (f32[8,1024]{1,0:T(8,128)S(1)}, f32[8,1024]{1,0:T(8,128)S(1)}, u32[]{:S(2)}, u32[]{:S(2)}) collective-permute-start(f32[8,1024]{1,0:T(8,128)S(1)} %get-tuple-element.58), channel_id=1, source_target_pairs={{0,12},{4,8},{8,4},{12,0},{1,13},{5,9},{9,5},{13,1},{2,14},{6,10},... | collective-permute-start | bytes 98312 | tf_op jit(solution)/shard_map/ppermute | solution.py:30
  48.7 0.0 collective-permute-start.11
  48.7 2.0 %collective-permute-start.12 = (f32[8,1024]{1,0:T(8,128)S(1)}, f32[8,1024]{1,0:T(8,128)S(1)}, u32[]{:S(2)}, u32[]{:S(2)}) collective-permute-start(f32[8,1024]{1,0:T(8,128)S(1)} %get-tuple-element.60), channel_id=1, source_target_pairs={{0,4},{4,0},{8,12},{12,8},{1,5},{5,1},{9,13},{13,9},{2,6},{6,2},{1... | collective-permute-start | bytes 98312 | tf_op jit(solution)/shard_map/ppermute | solution.py:30
  50.7 1.3 %collective-permute-done.10 = f32[8,1024]{1,0:T(8,128)S(1)} collective-permute-done((f32[8,1024]{1,0:T(8,128)S(1)}, f32[8,1024]{1,0:T(8,128)S(1)}, u32[]{:S(2)}, u32[]{:S(2)}) %collective-permute-start.10) | collective-permute-done | bytes 32800 | tf_op jit(solution)/shard_map/ppermute | solution.py:30
  52.0 1.5 %collective-permute-done.11 = f32[8,1024]{1,0:T(8,128)S(1)} collective-permute-done((f32[8,1024]{1,0:T(8,128)S(1)}, f32[8,1024]{1,0:T(8,128)S(1)}, u32[]{:S(2)}, u32[]{:S(2)}) %collective-permute-start.11) | collective-permute-done | bytes 32800 | tf_op jit(solution)/shard_map/ppermute | solution.py:30
  53.5 0.0 collective-permute-done.12
  53.5 0.6 %add_convert_fusion = bf16[8,1024]{1,0:T(8,128)(2,1)} fusion(f32[8,1024]{1,0:T(8,128)S(1)} %collective-permute-done.12, f32[8,1024]{1,0:T(8,128)S(1)} %collective-permute-done.11, f32[8,1024]{1,0:T(8,128)S(1)} %get-tuple-element.57, f32[8,1024]{1,0:T(8,128)S(1)} %collective-permute-done.10), kind=kLoop, calls=%fused_computation | loop fusion | flops 32768 | bytes 147456 | tf_op jit(solution)/shard_map/convert_element_type | solution.py:563
  (3 shorter events, 0.1 us)
Async XLA Ops:
  2.7 9.5 %collective-permute-start.2 = (bf16[8,3200]{1,0:T(8,128)(2,1)S(1)}, bf16[8,3200]{1,0:T(8,128)(2,1)S(1)}, u32[]{:S(2)}, u32[]{:S(2)}) collective-permute-start(bf16[8,3200]{1,0:T(8,128)(2,1)S(1)} %get-tuple-element.34.refs_0_.b0), channel_id=1, source_target_pairs={{0,12},{4,8},{8,4},{12,0},{1,13},{5,9},{9,5},{13,1},{2,14},{6,10},... | collective-permute-start | bytes 153608 | tf_op jit(solution)/shard_map/ppermute | solution.py:30
  7.8 5.0 %collective-permute-start.1 = (bf16[8,3200]{1,0:T(8,128)(2,1)S(1)}, bf16[8,3200]{1,0:T(8,128)(2,1)S(1)}, u32[]{:S(2)}, u32[]{:S(2)}) collective-permute-start(bf16[8,3200]{1,0:T(8,128)(2,1)S(1)} %get-tuple-element.34.refs_0_.b0), channel_id=1, source_target_pairs={{0,8},{4,12},{8,0},{12,4},{1,9},{5,13},{9,1},{13,5},{2,10},{6,14},... | collective-permute-start | bytes 153608 | tf_op jit(solution)/shard_map/ppermute | solution.py:30
  7.8 5.0 %collective-permute-start = (bf16[8,3200]{1,0:T(8,128)(2,1)S(1)}, bf16[8,3200]{1,0:T(8,128)(2,1)S(1)}, u32[]{:S(2)}, u32[]{:S(2)}) collective-permute-start(bf16[8,3200]{1,0:T(8,128)(2,1)S(1)} %get-tuple-element.34.refs_0_.b0), channel_id=1, source_target_pairs={{0,4},{4,0},{8,12},{12,8},{1,5},{5,1},{9,13},{13,9},{2,6},{6,2},{1... | collective-permute-start | bytes 153608 | tf_op jit(solution)/shard_map/ppermute | solution.py:30
  13.7 1.4 %collective-permute-start.3 = (f32[32,1024]{1,0:T(8,128)S(1)}, f32[32,1024]{1,0:T(8,128)S(1)}, u32[]{:S(2)}, u32[]{:S(2)}) collective-permute-start(f32[32,1024]{1,0:T(8,128)S(1)} %get-tuple-element.37.a), channel_id=1, source_target_pairs={{0,1},{1,0},{2,3},{3,2},{4,5},{5,4},{6,7},{7,6},{8,9},{9,8},{10,11... | collective-permute-start | bytes 393224 | tf_op jit(solution)/shard_map/ppermute | solution.py:30
  15.1 5.8 %collective-permute-start.4 = (f32[32,1024]{1,0:T(8,128)S(1)}, f32[32,1024]{1,0:T(8,128)S(1)}, u32[]{:S(2)}, u32[]{:S(2)}) collective-permute-start(f32[32,1024]{1,0:T(8,128)S(1)} %add.16.refs_0_.a), channel_id=1, source_target_pairs={{0,2},{1,3},{2,0},{3,1},{4,6},{5,7},{6,4},{7,5},{8,10},{9,11},{10,... | collective-permute-start | bytes 393224 | tf_op jit(solution)/shard_map/ppermute | solution.py:30
  21.0 9.0 %collective-permute-start.7 = (bf16[32,1152]{1,0:T(8,128)(2,1)S(1)}, bf16[32,1152]{1,0:T(8,128)(2,1)S(1)}, u32[]{:S(2)}, u32[]{:S(2)}) collective-permute-start(bf16[32,1152]{1,0:T(8,128)(2,1)S(1)} %get-tuple-element.39.refs_0_), channel_id=1, source_target_pairs={{0,12},{4,8},{8,4},{12,0},{1,13},{5,9},{9,5},{13,1},{2,14},{6,10},... | collective-permute-start | bytes 221192 | tf_op jit(solution)/shard_map/ppermute | solution.py:30
  24.2 6.2 %collective-permute-start.6 = (bf16[32,1152]{1,0:T(8,128)(2,1)S(1)}, bf16[32,1152]{1,0:T(8,128)(2,1)S(1)}, u32[]{:S(2)}, u32[]{:S(2)}) collective-permute-start(bf16[32,1152]{1,0:T(8,128)(2,1)S(1)} %get-tuple-element.39.refs_0_), channel_id=1, source_target_pairs={{0,8},{4,12},{8,0},{12,4},{1,9},{5,13},{9,1},{13,5},{2,10},{6,14},... | collective-permute-start | bytes 221192 | tf_op jit(solution)/shard_map/ppermute | solution.py:30
  24.2 6.2 %collective-permute-start.5 = (bf16[32,1152]{1,0:T(8,128)(2,1)S(1)}, bf16[32,1152]{1,0:T(8,128)(2,1)S(1)}, u32[]{:S(2)}, u32[]{:S(2)}) collective-permute-start(bf16[32,1152]{1,0:T(8,128)(2,1)S(1)} %get-tuple-element.39.refs_0_), channel_id=1, source_target_pairs={{0,4},{4,0},{8,12},{12,8},{1,5},{5,1},{9,13},{13,9},{2,6},{6,2},{1... | collective-permute-start | bytes 221192 | tf_op jit(solution)/shard_map/ppermute | solution.py:30
  39.3 5.5 %collective-permute-start.8 = (bf16[32,2048]{1,0:T(8,128)(2,1)S(1)}, bf16[32,2048]{1,0:T(8,128)(2,1)S(1)}, u32[]{:S(2)}, u32[]{:S(2)}) collective-permute-start(bf16[32,2048]{1,0:T(8,128)(2,1)S(1)} %get-tuple-element.53.refs_5_), channel_id=1, source_target_pairs={{0,2},{1,3},{2,0},{3,1},{4,6},{5,7},{6,4},{7,5},{8,10},{9,11},{10,... | collective-permute-start | bytes 393224 | tf_op jit(solution)/shard_map/ppermute | solution.py:30
  44.8 1.4 %collective-permute-start.9 = (f32[32,1024]{1,0:T(8,128)S(1)}, f32[32,1024]{1,0:T(8,128)S(1)}, u32[]{:S(2)}, u32[]{:S(2)}) collective-permute-start(f32[32,1024]{1,0:T(8,128)S(1)} %get-tuple-element.55), channel_id=1, source_target_pairs={{0,1},{1,0},{2,3},{3,2},{4,5},{5,4},{6,7},{7,6},{8,9},{9,8},{10,11... | collective-permute-start | bytes 393224 | tf_op jit(solution)/shard_map/ppermute | solution.py:30
  46.2 5.8 %collective-permute-start.10 = (f32[8,1024]{1,0:T(8,128)S(1)}, f32[8,1024]{1,0:T(8,128)S(1)}, u32[]{:S(2)}, u32[]{:S(2)}) collective-permute-start(f32[8,1024]{1,0:T(8,128)S(1)} %get-tuple-element.58), channel_id=1, source_target_pairs={{0,12},{4,8},{8,4},{12,0},{1,13},{5,9},{9,5},{13,1},{2,14},{6,10},... | collective-permute-start | bytes 98312 | tf_op jit(solution)/shard_map/ppermute | solution.py:30
  48.7 4.8 %collective-permute-start.11 = (f32[8,1024]{1,0:T(8,128)S(1)}, f32[8,1024]{1,0:T(8,128)S(1)}, u32[]{:S(2)}, u32[]{:S(2)}) collective-permute-start(f32[8,1024]{1,0:T(8,128)S(1)} %get-tuple-element.59), channel_id=1, source_target_pairs={{0,8},{4,12},{8,0},{12,4},{1,9},{5,13},{9,1},{13,5},{2,10},{6,14},... | collective-permute-start | bytes 98312 | tf_op jit(solution)/shard_map/ppermute | solution.py:30
  48.7 4.8 %collective-permute-start.12 = (f32[8,1024]{1,0:T(8,128)S(1)}, f32[8,1024]{1,0:T(8,128)S(1)}, u32[]{:S(2)}, u32[]{:S(2)}) collective-permute-start(f32[8,1024]{1,0:T(8,128)S(1)} %get-tuple-element.60), channel_id=1, source_target_pairs={{0,4},{4,0},{8,12},{12,8},{1,5},{5,1},{9,13},{13,9},{2,6},{6,2},{1... | collective-permute-start | bytes 98312 | tf_op jit(solution)/shard_map/ppermute | solution.py:30

commit v7 on v6

--- a/solution.py
+++ b/solution.py
@@ -333,7 +333,7 @@
     near, out = refs[:-1], refs[-1]
     width = packed.shape[1] - 128
     start = pl.multiple_of(lax.axis_index("ep") * width, width)
-    turned = packed[:, :width].astype(F32).T.astype(BF16)
+    turned = packed[:, :width].T
     at = 0
     for array in near:
         for first in range(0, array.shape[0], hidden):
@@ -369,7 +369,7 @@
     if first:
         out, turned = rest
         for k, packed in enumerate(packs):
-            turned[k * width : (k + 1) * width, :] = packed[:, :width].astype(F32).T.astype(BF16)
+            turned[k * width : (k + 1) * width, :] = packed[:, :width].T
     else:
         turned, out = rest
     squares = jnp.zeros((rows, 128), F32)
@@ -406,7 +406,7 @@
             if len(pair) == 2:
                 end = number * hidden
                 both = jnp.concatenate(pair, axis=0)
-                out[:, end - 2 * hidden : end] = both.T.astype(BF16)
+                out[:, end - 2 * hidden : end] = both.astype(BF16).T
                 pair = []
 
 
@@ -509,8 +509,8 @@
     "fetch1": [("entry", 6, 2), ("entry", 8, 5)],
     "own": [("leave", 0, 8)],
     "entry0": [("entry", 13, 3), ("leave", 8, 1)],
-    "entry8": [("away", 9, 7)],
-    "leave1": [("here", 9, 7)],
+    "entry8": [("leave", 9, 2), ("away", 11, 5)],
+    "leave1": [("here", 11, 5)],
 }
 
 

time: 54.4 us -> 53.9 us (level)
  transfers between devices with their start and end apart: 13 -> 13, of which waited for: 7 -> 7; matrix products, arithmetic and copies ran while one was open for 0% -> 0% of each run, Pallas kernels for 27% -> 28%
where the time goes in v7:
time: 53.9 us; the launch traced here: 53.7 us
  Pallas kernels  27 us (50%)
  starting transfers between devices  17.7 us (33%)
  waiting for transfers between devices  8.28 us (15%)
  other arithmetic  0.62 us (1%)
    pallas_call x13, Pallas kernels, kernel_call(): pl.pallas_call(hosted(body, len(args), len(outs), loads) if loads or body...  27 us
    ppermute x13, starting transfers between devices, swap(): return lax.ppermute(block, axis, [(i, i ^ k) for i in range(SIDE)])  17.7 us
    ppermute x13, waiting for transfers between devices, swap(): return lax.ppermute(block, axis, [(i, i ^ k) for i in range(SIDE)])  8.28 us
  transfers between devices with their start and end apart: 13, of which 7 were waited for; matrix products, arithmetic and copies ran while one was open for 0% of the time, Pallas kernels for 28%

profile of v7, /device:TPU:0, one launch (start us, length us, event | category | flops | bytes accessed | tf_op | source)
XLA Modules:
  0.0 53.7 jit_solution(202675817839898199)
XLA Ops:
  0.0 2.7 %attention.1 = (bf16[8,3200]{1,0:T(8,128)(2,1)S(1)}, bf16[2048,1024]{1,0:T(8,128)(2,1)S(1)}, bf16[32,32]{1,0:T(8,128)(2,1)S(1)}) custom-call(s32[8]{0:T(128)} %refs_0_.1, bf16[8,2048]{1,0:T(8,128)(2,1)} %refs_1_.1, bf16[8,512,128]{2,1,0:T(8,128)(2,1)} %bitcast.14, s32[8,8]{1,0:T(8,128)} %refs_3_.1, f32[8,8]{1,0:T(8,128)} %refs_4_.1, ...), custom_call_target="tpu_custom_call" | custom-call | flops 140000000 | bytes 12000000 | tf_op jit(solution)/shard_map/attention/pallas_call | solution.py:89
  2.7 5.1 %collective-permute-start.2 = (bf16[8,3200]{1,0:T(8,128)(2,1)S(1)}, bf16[8,3200]{1,0:T(8,128)(2,1)S(1)}, u32[]{:S(2)}, u32[]{:S(2)}) collective-permute-start(bf16[8,3200]{1,0:T(8,128)(2,1)S(1)} %get-tuple-element.35.refs_0_.b0), channel_id=1, source_target_pairs={{0,12},{4,8},{8,4},{12,0},{1,13},{5,9},{9,5},{13,1},{2,14},{6,10},... | collective-permute-start | bytes 153608 | tf_op jit(solution)/shard_map/ppermute | solution.py:30
  7.8 0.0 collective-permute-start.1
  7.8 0.6 %collective-permute-start = (bf16[8,3200]{1,0:T(8,128)(2,1)S(1)}, bf16[8,3200]{1,0:T(8,128)(2,1)S(1)}, u32[]{:S(2)}, u32[]{:S(2)}) collective-permute-start(bf16[8,3200]{1,0:T(8,128)(2,1)S(1)} %get-tuple-element.35.refs_0_.b0), channel_id=1, source_target_pairs={{0,4},{4,0},{8,12},{12,8},{1,5},{5,1},{9,13},{13,9},{2,6},{6,2},{1... | collective-permute-start | bytes 153608 | tf_op jit(solution)/shard_map/ppermute | solution.py:30
  8.4 3.7 %fetch0.1 = (f32[8,128]{1,0:T(8,128)S(1)}, bf16[1152,4096]{1,0:T(8,128)(2,1)S(1)}) custom-call(bf16[8,3200]{1,0:T(8,128)(2,1)S(1)} %get-tuple-element.35.refs_0_.b0, bf16[3072,4096]{1,0:T(8,128)(2,1)} %bitcast.10), custom_call_target="tpu_custom_call" | custom-call | bytes 9437184 | tf_op jit(solution)/shard_map/fetch0/pallas_call | solution.py:89
  12.1 0.0 collective-permute-done.2.b3
  12.1 0.7 %collective-permute-done.1.b2 = bf16[8,3200]{1,0:T(8,128)(2,1)S(1)} collective-permute-done((bf16[8,3200]{1,0:T(8,128)(2,1)S(1)}, bf16[8,3200]{1,0:T(8,128)(2,1)S(1)}, u32[]{:S(2)}, u32[]{:S(2)}) %collective-permute-start.1) | collective-permute-done | bytes 51232 | tf_op jit(solution)/shard_map/ppermute | solution.py:30
  12.8 0.0 collective-permute-done.b1
  12.8 0.9 %projection.1 = (f32[32,1024]{1,0:T(8,128)S(1)}, f32[32,128]{1,0:T(8,128)S(1)}) custom-call(bf16[32,32]{1,0:T(8,128)(2,1)S(1)} %get-tuple-element.34.order, bf16[8,3200]{1,0:T(8,128)(2,1)S(1)} %get-tuple-element.35.refs_0_.b0, bf16[8,3200]{1,0:T(8,128)(2,1)S(1)} %collective-permute-done.b1, bf16[8,3200]{1,0:T(8,128)(2,1)S(1)} %collective-permute-done.1.b2, ...), custom_call_target="tpu_custom_call" | custom-call | flops 140000000 | bytes 4500000 | tf_op jit(solution)/shard_map/projection/pallas_call | solution.py:89
  13.7 0.0 collective-permute-start.3
  13.8 1.3 %collective-permute-done.3.b = f32[32,1024]{1,0:T(8,128)S(1)} collective-permute-done((f32[32,1024]{1,0:T(8,128)S(1)}, f32[32,1024]{1,0:T(8,128)S(1)}, u32[]{:S(2)}, u32[]{:S(2)}) %collective-permute-start.3) | collective-permute-done | bytes 131104 | tf_op jit(solution)/shard_map/ppermute | solution.py:30
  15.1 1.6 %collective-permute-start.4 = (f32[32,1024]{1,0:T(8,128)S(1)}, f32[32,1024]{1,0:T(8,128)S(1)}, u32[]{:S(2)}, u32[]{:S(2)}) collective-permute-start(f32[32,1024]{1,0:T(8,128)S(1)} %add.16.refs_0_.a), channel_id=1, source_target_pairs={{0,2},{1,3},{2,0},{3,1},{4,6},{5,7},{6,4},{7,5},{8,10},{9,11},{10,... | collective-permute-start | bytes 393224 | tf_op jit(solution)/shard_map/ppermute | solution.py:30
  16.7 4.2 %fetch1.1 = (f32[8,128]{1,0:T(8,128)S(1)}, bf16[384,4096]{1,0:T(8,128)(2,1)S(1)}, bf16[960,4096]{1,0:T(8,128)(2,1)S(1)}) custom-call(f32[32,1024]{1,0:T(8,128)S(1)} %add.16.refs_0_.a, bf16[3072,4096]{1,0:T(8,128)(2,1)} %bitcast.11, bf16[3072,4096]{1,0:T(8,128)(2,1)} %bitcast.12), custom_call_target="tpu_custom_call" | custom-call | bytes 11010048 | tf_op jit(solution)/shard_map/fetch1/pallas_call | solution.py:89
  20.9 0.0 collective-permute-done.4.b
  20.9 0.1 stream.1
  21.0 3.2 %collective-permute-start.7 = (bf16[32,1152]{1,0:T(8,128)(2,1)S(1)}, bf16[32,1152]{1,0:T(8,128)(2,1)S(1)}, u32[]{:S(2)}, u32[]{:S(2)}) collective-permute-start(bf16[32,1152]{1,0:T(8,128)(2,1)S(1)} %get-tuple-element.40.refs_0_), channel_id=1, source_target_pairs={{0,12},{4,8},{8,4},{12,0},{1,13},{5,9},{9,5},{13,1},{2,14},{6,10},... | collective-permute-start | bytes 221192 | tf_op jit(solution)/shard_map/ppermute | solution.py:30
  24.2 0.0 collective-permute-start.6
  24.2 1.3 %collective-permute-start.5 = (bf16[32,1152]{1,0:T(8,128)(2,1)S(1)}, bf16[32,1152]{1,0:T(8,128)(2,1)S(1)}, u32[]{:S(2)}, u32[]{:S(2)}) collective-permute-start(bf16[32,1152]{1,0:T(8,128)(2,1)S(1)} %get-tuple-element.40.refs_0_), channel_id=1, source_target_pairs={{0,4},{4,0},{8,12},{12,8},{1,5},{5,1},{9,13},{13,9},{2,6},{6,2},{1... | collective-permute-start | bytes 221192 | tf_op jit(solution)/shard_map/ppermute | solution.py:30
  25.5 4.6 %entry_own.1 = (f32[2496,32]{1,0:T(8,128)S(1)}, bf16[1536,4096]{1,0:T(8,128)(2,1)S(1)}) custom-call(bf16[32,1152]{1,0:T(8,128)(2,1)S(1)} %get-tuple-element.40.refs_0_, bf16[1152,4096]{1,0:T(8,128)(2,1)S(1)} %get-tuple-element.42.refs_1_.refs_6_, bf16[384,4096]{1,0:T(8,128)(2,1)S(1)} %get-tuple-element.43.refs_2_.refs_7_, ...), custom_call_target="tpu_custom_call" | custom-call | flops 163577856 | bytes 17694720 | tf_op jit(solution)/shard_map/entry_own/pallas_call | solution.py:89
  30.0 0.0 collective-permute-done.7.refs_3_
  30.1 0.3 collective-permute-done.6.refs_2_
  30.4 0.0 collective-permute-done.5.refs_1_
  30.4 3.0 %entry0.1 = (bf16[64,1536]{1,0:T(8,128)(2,1)S(1)}, bf16[4096,32]{1,0:T(8,128)(2,1)S(1)}, bf16[576,4096]{1,0:T(8,128)(2,1)S(1)}, bf16[192,4096]{1,0:T(8,128)(2,1)S(1)}) custom-call(bf16[32,1152]{1,0:T(8,128)(2,1)S(1)} %get-tuple-element.40.refs_0_, bf16[32,1152]{1,0:T(8,128)(2,1)S(1)} %collective-permute-done.5.refs_1_, ...), custom_call_target="tpu_custom_call" | custom-call | flops 402653184 | bytes 18874368 | tf_op jit(solution)/shard_map/entry0/pallas_call | solution.py:89
  33.3 3.2 %entry8.1 = (bf16[64,1536]{1,0:T(8,128)(2,1)S(1)}, bf16[384,4096]{1,0:T(8,128)(2,1)S(1)}, bf16[960,2048]{1,0:T(8,128)(2,1)S(1)}) custom-call(bf16[32,1152]{1,0:T(8,128)(2,1)S(1)} %get-tuple-element.40.refs_0_, bf16[32,1152]{1,0:T(8,128)(2,1)S(1)} %collective-permute-done.5.refs_1_, bf16[32,1152]{1,0:T(8,128)(2,1)S(1)} %collective-permute-done.6.refs_2_, ...), custom_call_target="tpu_custom_call" | custom-call | flops 402653184 | bytes 19660800 | tf_op jit(solution)/shard_map/entry8/pallas_call | solution.py:89
  36.5 2.3 %leave1.1 = (bf16[32,2048]{1,0:T(8,128)(2,1)S(1)}, bf16[960,2048]{1,0:T(8,128)(2,1)S(1)}) custom-call(bf16[64,1536]{1,0:T(8,128)(2,1)S(1)} %get-tuple-element.46.refs_0_, bf16[64,1536]{1,0:T(8,128)(2,1)S(1)} %get-tuple-element.49.refs_1_.refs_6_, bf16[1536,4096]{1,0:T(8,128)(2,1)S(1)} %get-tuple-element.50.refs_2_, ...), custom_call_target="tpu_custom_call" | custom-call | flops 805306368 | bytes 16515072 | tf_op jit(solution)/shard_map/leave1/pallas_call | solution.py:89
  38.8 1.3 %collective-permute-start.8 = (bf16[32,2048]{1,0:T(8,128)(2,1)S(1)}, bf16[32,2048]{1,0:T(8,128)(2,1)S(1)}, u32[]{:S(2)}, u32[]{:S(2)}) collective-permute-start(bf16[32,2048]{1,0:T(8,128)(2,1)S(1)} %get-tuple-element.55.refs_6_), channel_id=1, source_target_pairs={{0,2},{1,3},{2,0},{3,1},{4,6},{5,7},{6,4},{7,5},{8,10},{9,11},{10,... | collective-permute-start | bytes 393224 | tf_op jit(solution)/shard_map/ppermute | solution.py:30
  40.2 2.3 %leave0.1.mine = f32[32,2048]{1,0:T(8,128)S(1)} custom-call(bf16[64,1536]{1,0:T(8,128)(2,1)S(1)} %get-tuple-element.46.refs_0_, bf16[64,1536]{1,0:T(8,128)(2,1)S(1)} %get-tuple-element.49.refs_1_.refs_6_, bf16[1536,4096]{1,0:T(8,128)(2,1)S(1)} %get-tuple-element.50.refs_2_, bf16[192,4096]{1,0:T(8,128)(2,1)S(1)} %get-tuple-element.51.refs_3_, ...), custom_call_target="tpu_custom_call" | custom-call | flops 805306368 | bytes 12582912 | tf_op jit(solution)/shard_map/leave0/pallas_call | solution.py:89
  42.5 1.8 %collective-permute-done.8.received = bf16[32,2048]{1,0:T(8,128)(2,1)S(1)} collective-permute-done((bf16[32,2048]{1,0:T(8,128)(2,1)S(1)}, bf16[32,2048]{1,0:T(8,128)(2,1)S(1)}, u32[]{:S(2)}, u32[]{:S(2)}) %collective-permute-start.8) | collective-permute-done | bytes 131104 | tf_op jit(solution)/shard_map/ppermute | solution.py:30
  44.3 0.1 collective-permute-start.9
  44.4 1.3 %collective-permute-done.9.received = f32[32,1024]{1,0:T(8,128)S(1)} collective-permute-done((f32[32,1024]{1,0:T(8,128)S(1)}, f32[32,1024]{1,0:T(8,128)S(1)}, u32[]{:S(2)}, u32[]{:S(2)}) %collective-permute-start.9) | collective-permute-done | bytes 131104 | tf_op jit(solution)/shard_map/ppermute | solution.py:30
  45.8 2.5 %collective-permute-start.10 = (f32[8,1024]{1,0:T(8,128)S(1)}, f32[8,1024]{1,0:T(8,128)S(1)}, u32[]{:S(2)}, u32[]{:S(2)}) collective-permute-start(f32[8,1024]{1,0:T(8,128)S(1)} %get-tuple-element.60), channel_id=1, source_target_pairs={{0,12},{4,8},{8,4},{12,0},{1,13},{5,9},{9,5},{13,1},{2,14},{6,10},... | collective-permute-start | bytes 98312 | tf_op jit(solution)/shard_map/ppermute | solution.py:30
  48.2 0.0 collective-permute-start.11
  48.2 2.0 %collective-permute-start.12 = (f32[8,1024]{1,0:T(8,128)S(1)}, f32[8,1024]{1,0:T(8,128)S(1)}, u32[]{:S(2)}, u32[]{:S(2)}) collective-permute-start(f32[8,1024]{1,0:T(8,128)S(1)} %get-tuple-element.62), channel_id=1, source_target_pairs={{0,4},{4,0},{8,12},{12,8},{1,5},{5,1},{9,13},{13,9},{2,6},{6,2},{1... | collective-permute-start | bytes 98312 | tf_op jit(solution)/shard_map/ppermute | solution.py:30
  50.2 1.3 %collective-permute-done.10 = f32[8,1024]{1,0:T(8,128)S(1)} collective-permute-done((f32[8,1024]{1,0:T(8,128)S(1)}, f32[8,1024]{1,0:T(8,128)S(1)}, u32[]{:S(2)}, u32[]{:S(2)}) %collective-permute-start.10) | collective-permute-done | bytes 32800 | tf_op jit(solution)/shard_map/ppermute | solution.py:30
  51.6 1.5 %collective-permute-done.11 = f32[8,1024]{1,0:T(8,128)S(1)} collective-permute-done((f32[8,1024]{1,0:T(8,128)S(1)}, f32[8,1024]{1,0:T(8,128)S(1)}, u32[]{:S(2)}, u32[]{:S(2)}) %collective-permute-start.11) | collective-permute-done | bytes 32800 | tf_op jit(solution)/shard_map/ppermute | solution.py:30
  53.1 0.0 collective-permute-done.12
  53.1 0.6 %add_convert_fusion = bf16[8,1024]{1,0:T(8,128)(2,1)} fusion(f32[8,1024]{1,0:T(8,128)S(1)} %collective-permute-done.12, f32[8,1024]{1,0:T(8,128)S(1)} %collective-permute-done.11, f32[8,1024]{1,0:T(8,128)S(1)} %get-tuple-element.59, f32[8,1024]{1,0:T(8,128)S(1)} %collective-permute-done.10), kind=kLoop, calls=%fused_computation | loop fusion | flops 32768 | bytes 147456 | tf_op jit(solution)/shard_map/convert_element_type | solution.py:563
  (3 shorter events, 0.1 us)
Async XLA Ops:
  2.7 9.5 %collective-permute-start.2 = (bf16[8,3200]{1,0:T(8,128)(2,1)S(1)}, bf16[8,3200]{1,0:T(8,128)(2,1)S(1)}, u32[]{:S(2)}, u32[]{:S(2)}) collective-permute-start(bf16[8,3200]{1,0:T(8,128)(2,1)S(1)} %get-tuple-element.35.refs_0_.b0), channel_id=1, source_target_pairs={{0,12},{4,8},{8,4},{12,0},{1,13},{5,9},{9,5},{13,1},{2,14},{6,10},... | collective-permute-start | bytes 153608 | tf_op jit(solution)/shard_map/ppermute | solution.py:30
  7.8 5.0 %collective-permute-start.1 = (bf16[8,3200]{1,0:T(8,128)(2,1)S(1)}, bf16[8,3200]{1,0:T(8,128)(2,1)S(1)}, u32[]{:S(2)}, u32[]{:S(2)}) collective-permute-start(bf16[8,3200]{1,0:T(8,128)(2,1)S(1)} %get-tuple-element.35.refs_0_.b0), channel_id=1, source_target_pairs={{0,8},{4,12},{8,0},{12,4},{1,9},{5,13},{9,1},{13,5},{2,10},{6,14},... | collective-permute-start | bytes 153608 | tf_op jit(solution)/shard_map/ppermute | solution.py:30
  7.8 5.0 %collective-permute-start = (bf16[8,3200]{1,0:T(8,128)(2,1)S(1)}, bf16[8,3200]{1,0:T(8,128)(2,1)S(1)}, u32[]{:S(2)}, u32[]{:S(2)}) collective-permute-start(bf16[8,3200]{1,0:T(8,128)(2,1)S(1)} %get-tuple-element.35.refs_0_.b0), channel_id=1, source_target_pairs={{0,4},{4,0},{8,12},{12,8},{1,5},{5,1},{9,13},{13,9},{2,6},{6,2},{1... | collective-permute-start | bytes 153608 | tf_op jit(solution)/shard_map/ppermute | solution.py:30
  13.7 1.4 %collective-permute-start.3 = (f32[32,1024]{1,0:T(8,128)S(1)}, f32[32,1024]{1,0:T(8,128)S(1)}, u32[]{:S(2)}, u32[]{:S(2)}) collective-permute-start(f32[32,1024]{1,0:T(8,128)S(1)} %get-tuple-element.38.a), channel_id=1, source_target_pairs={{0,1},{1,0},{2,3},{3,2},{4,5},{5,4},{6,7},{7,6},{8,9},{9,8},{10,11... | collective-permute-start | bytes 393224 | tf_op jit(solution)/shard_map/ppermute | solution.py:30
  15.1 5.8 %collective-permute-start.4 = (f32[32,1024]{1,0:T(8,128)S(1)}, f32[32,1024]{1,0:T(8,128)S(1)}, u32[]{:S(2)}, u32[]{:S(2)}) collective-permute-start(f32[32,1024]{1,0:T(8,128)S(1)} %add.16.refs_0_.a), channel_id=1, source_target_pairs={{0,2},{1,3},{2,0},{3,1},{4,6},{5,7},{6,4},{7,5},{8,10},{9,11},{10,... | collective-permute-start | bytes 393224 | tf_op jit(solution)/shard_map/ppermute | solution.py:30
  21.0 9.0 %collective-permute-start.7 = (bf16[32,1152]{1,0:T(8,128)(2,1)S(1)}, bf16[32,1152]{1,0:T(8,128)(2,1)S(1)}, u32[]{:S(2)}, u32[]{:S(2)}) collective-permute-start(bf16[32,1152]{1,0:T(8,128)(2,1)S(1)} %get-tuple-element.40.refs_0_), channel_id=1, source_target_pairs={{0,12},{4,8},{8,4},{12,0},{1,13},{5,9},{9,5},{13,1},{2,14},{6,10},... | collective-permute-start | bytes 221192 | tf_op jit(solution)/shard_map/ppermute | solution.py:30
  24.2 6.2 %collective-permute-start.6 = (bf16[32,1152]{1,0:T(8,128)(2,1)S(1)}, bf16[32,1152]{1,0:T(8,128)(2,1)S(1)}, u32[]{:S(2)}, u32[]{:S(2)}) collective-permute-start(bf16[32,1152]{1,0:T(8,128)(2,1)S(1)} %get-tuple-element.40.refs_0_), channel_id=1, source_target_pairs={{0,8},{4,12},{8,0},{12,4},{1,9},{5,13},{9,1},{13,5},{2,10},{6,14},... | collective-permute-start | bytes 221192 | tf_op jit(solution)/shard_map/ppermute | solution.py:30
  24.2 6.2 %collective-permute-start.5 = (bf16[32,1152]{1,0:T(8,128)(2,1)S(1)}, bf16[32,1152]{1,0:T(8,128)(2,1)S(1)}, u32[]{:S(2)}, u32[]{:S(2)}) collective-permute-start(bf16[32,1152]{1,0:T(8,128)(2,1)S(1)} %get-tuple-element.40.refs_0_), channel_id=1, source_target_pairs={{0,4},{4,0},{8,12},{12,8},{1,5},{5,1},{9,13},{13,9},{2,6},{6,2},{1... | collective-permute-start | bytes 221192 | tf_op jit(solution)/shard_map/ppermute | solution.py:30
  38.8 5.5 %collective-permute-start.8 = (bf16[32,2048]{1,0:T(8,128)(2,1)S(1)}, bf16[32,2048]{1,0:T(8,128)(2,1)S(1)}, u32[]{:S(2)}, u32[]{:S(2)}) collective-permute-start(bf16[32,2048]{1,0:T(8,128)(2,1)S(1)} %get-tuple-element.55.refs_6_), channel_id=1, source_target_pairs={{0,2},{1,3},{2,0},{3,1},{4,6},{5,7},{6,4},{7,5},{8,10},{9,11},{10,... | collective-permute-start | bytes 393224 | tf_op jit(solution)/shard_map/ppermute | solution.py:30
  44.3 1.4 %collective-permute-start.9 = (f32[32,1024]{1,0:T(8,128)S(1)}, f32[32,1024]{1,0:T(8,128)S(1)}, u32[]{:S(2)}, u32[]{:S(2)}) collective-permute-start(f32[32,1024]{1,0:T(8,128)S(1)} %get-tuple-element.57), channel_id=1, source_target_pairs={{0,1},{1,0},{2,3},{3,2},{4,5},{5,4},{6,7},{7,6},{8,9},{9,8},{10,11... | collective-permute-start | bytes 393224 | tf_op jit(solution)/shard_map/ppermute | solution.py:30
  45.8 5.8 %collective-permute-start.10 = (f32[8,1024]{1,0:T(8,128)S(1)}, f32[8,1024]{1,0:T(8,128)S(1)}, u32[]{:S(2)}, u32[]{:S(2)}) collective-permute-start(f32[8,1024]{1,0:T(8,128)S(1)} %get-tuple-element.60), channel_id=1, source_target_pairs={{0,12},{4,8},{8,4},{12,0},{1,13},{5,9},{9,5},{13,1},{2,14},{6,10},... | collective-permute-start | bytes 98312 | tf_op jit(solution)/shard_map/ppermute | solution.py:30
  48.2 4.8 %collective-permute-start.11 = (f32[8,1024]{1,0:T(8,128)S(1)}, f32[8,1024]{1,0:T(8,128)S(1)}, u32[]{:S(2)}, u32[]{:S(2)}) collective-permute-start(f32[8,1024]{1,0:T(8,128)S(1)} %get-tuple-element.61), channel_id=1, source_target_pairs={{0,8},{4,12},{8,0},{12,4},{1,9},{5,13},{9,1},{13,5},{2,10},{6,14},... | collective-permute-start | bytes 98312 | tf_op jit(solution)/shard_map/ppermute | solution.py:30
  48.2 4.8 %collective-permute-start.12 = (f32[8,1024]{1,0:T(8,128)S(1)}, f32[8,1024]{1,0:T(8,128)S(1)}, u32[]{:S(2)}, u32[]{:S(2)}) collective-permute-start(f32[8,1024]{1,0:T(8,128)S(1)} %get-tuple-element.62), channel_id=1, source_target_pairs={{0,4},{4,0},{8,12},{12,8},{1,5},{5,1},{9,13},{13,9},{2,6},{6,2},{1... | collective-permute-start | bytes 98312 | tf_op jit(solution)/shard_map/ppermute | solution.py:30

commit v8 on v7

--- a/solution.py
+++ b/solution.py
@@ -509,8 +509,8 @@
     "fetch1": [("entry", 6, 2), ("entry", 8, 5)],
     "own": [("leave", 0, 8)],
     "entry0": [("entry", 13, 3), ("leave", 8, 1)],
-    "entry8": [("leave", 9, 2), ("away", 11, 5)],
-    "leave1": [("here", 11, 5)],
+    "entry8": [("leave", 9, 3), ("away", 12, 4)],
+    "leave1": [("here", 12, 4)],
 }
 
 

time: 53.9 us -> 54.1 us (level)
  transfers between devices with their start and end apart: 13 -> 13, of which waited for: 7 -> 7; matrix products, arithmetic and copies ran while one was open for 0% -> 0% of each run, Pallas kernels for 28% -> 27%
where the time goes in v8:
time: 54.1 us; the launch traced here: 53.9 us
  Pallas kernels  27.2 us (50%)
  starting transfers between devices  17.7 us (33%)
  waiting for transfers between devices  8.27 us (15%)
  other arithmetic  0.62 us (1%)
    pallas_call x13, Pallas kernels, kernel_call(): pl.pallas_call(hosted(body, len(args), len(outs), loads) if loads or body...  27.2 us
    ppermute x13, starting transfers between devices, swap(): return lax.ppermute(block, axis, [(i, i ^ k) for i in range(SIDE)])  17.7 us
    ppermute x13, waiting for transfers between devices, swap(): return lax.ppermute(block, axis, [(i, i ^ k) for i in range(SIDE)])  8.27 us
  transfers between devices with their start and end apart: 13, of which 7 were waited for; matrix products, arithmetic and copies ran while one was open for 0% of the time, Pallas kernels for 27%

profile of v8, /device:TPU:0, one launch (start us, length us, event | category | flops | bytes accessed | tf_op | source)
XLA Modules:
  0.0 53.9 jit_solution(11334147215934640254)
XLA Ops:
  0.0 2.7 %attention.1 = (bf16[8,3200]{1,0:T(8,128)(2,1)S(1)}, bf16[2048,1024]{1,0:T(8,128)(2,1)S(1)}, bf16[32,32]{1,0:T(8,128)(2,1)S(1)}) custom-call(s32[8]{0:T(128)} %refs_0_.1, bf16[8,2048]{1,0:T(8,128)(2,1)} %refs_1_.1, bf16[8,512,128]{2,1,0:T(8,128)(2,1)} %bitcast.14, s32[8,8]{1,0:T(8,128)} %refs_3_.1, f32[8,8]{1,0:T(8,128)} %refs_4_.1, ...), custom_call_target="tpu_custom_call" | custom-call | flops 140000000 | bytes 12000000 | tf_op jit(solution)/shard_map/attention/pallas_call | solution.py:89
  2.7 5.1 %collective-permute-start.2 = (bf16[8,3200]{1,0:T(8,128)(2,1)S(1)}, bf16[8,3200]{1,0:T(8,128)(2,1)S(1)}, u32[]{:S(2)}, u32[]{:S(2)}) collective-permute-start(bf16[8,3200]{1,0:T(8,128)(2,1)S(1)} %get-tuple-element.35.refs_0_.b0), channel_id=1, source_target_pairs={{0,12},{4,8},{8,4},{12,0},{1,13},{5,9},{9,5},{13,1},{2,14},{6,10},... | collective-permute-start | bytes 153608 | tf_op jit(solution)/shard_map/ppermute | solution.py:30
  7.8 0.0 collective-permute-start.1
  7.8 0.6 %collective-permute-start = (bf16[8,3200]{1,0:T(8,128)(2,1)S(1)}, bf16[8,3200]{1,0:T(8,128)(2,1)S(1)}, u32[]{:S(2)}, u32[]{:S(2)}) collective-permute-start(bf16[8,3200]{1,0:T(8,128)(2,1)S(1)} %get-tuple-element.35.refs_0_.b0), channel_id=1, source_target_pairs={{0,4},{4,0},{8,12},{12,8},{1,5},{5,1},{9,13},{13,9},{2,6},{6,2},{1... | collective-permute-start | bytes 153608 | tf_op jit(solution)/shard_map/ppermute | solution.py:30
  8.4 3.7 %fetch0.1 = (f32[8,128]{1,0:T(8,128)S(1)}, bf16[1152,4096]{1,0:T(8,128)(2,1)S(1)}) custom-call(bf16[8,3200]{1,0:T(8,128)(2,1)S(1)} %get-tuple-element.35.refs_0_.b0, bf16[3072,4096]{1,0:T(8,128)(2,1)} %bitcast.10), custom_call_target="tpu_custom_call" | custom-call | bytes 9437184 | tf_op jit(solution)/shard_map/fetch0/pallas_call | solution.py:89
  12.1 0.0 collective-permute-done.2.b3
  12.1 0.7 %collective-permute-done.1.b2 = bf16[8,3200]{1,0:T(8,128)(2,1)S(1)} collective-permute-done((bf16[8,3200]{1,0:T(8,128)(2,1)S(1)}, bf16[8,3200]{1,0:T(8,128)(2,1)S(1)}, u32[]{:S(2)}, u32[]{:S(2)}) %collective-permute-start.1) | collective-permute-done | bytes 51232 | tf_op jit(solution)/shard_map/ppermute | solution.py:30
  12.8 0.0 collective-permute-done.b1
  12.8 0.9 %projection.1 = (f32[32,1024]{1,0:T(8,128)S(1)}, f32[32,128]{1,0:T(8,128)S(1)}) custom-call(bf16[32,32]{1,0:T(8,128)(2,1)S(1)} %get-tuple-element.34.order, bf16[8,3200]{1,0:T(8,128)(2,1)S(1)} %get-tuple-element.35.refs_0_.b0, bf16[8,3200]{1,0:T(8,128)(2,1)S(1)} %collective-permute-done.b1, bf16[8,3200]{1,0:T(8,128)(2,1)S(1)} %collective-permute-done.1.b2, ...), custom_call_target="tpu_custom_call" | custom-call | flops 140000000 | bytes 4500000 | tf_op jit(solution)/shard_map/projection/pallas_call | solution.py:89
  13.7 0.0 collective-permute-start.3
  13.8 1.3 %collective-permute-done.3.b = f32[32,1024]{1,0:T(8,128)S(1)} collective-permute-done((f32[32,1024]{1,0:T(8,128)S(1)}, f32[32,1024]{1,0:T(8,128)S(1)}, u32[]{:S(2)}, u32[]{:S(2)}) %collective-permute-start.3) | collective-permute-done | bytes 131104 | tf_op jit(solution)/shard_map/ppermute | solution.py:30
  15.1 1.6 %collective-permute-start.4 = (f32[32,1024]{1,0:T(8,128)S(1)}, f32[32,1024]{1,0:T(8,128)S(1)}, u32[]{:S(2)}, u32[]{:S(2)}) collective-permute-start(f32[32,1024]{1,0:T(8,128)S(1)} %add.16.refs_0_.a), channel_id=1, source_target_pairs={{0,2},{1,3},{2,0},{3,1},{4,6},{5,7},{6,4},{7,5},{8,10},{9,11},{10,... | collective-permute-start | bytes 393224 | tf_op jit(solution)/shard_map/ppermute | solution.py:30
  16.7 4.2 %fetch1.1 = (f32[8,128]{1,0:T(8,128)S(1)}, bf16[384,4096]{1,0:T(8,128)(2,1)S(1)}, bf16[960,4096]{1,0:T(8,128)(2,1)S(1)}) custom-call(f32[32,1024]{1,0:T(8,128)S(1)} %add.16.refs_0_.a, bf16[3072,4096]{1,0:T(8,128)(2,1)} %bitcast.11, bf16[3072,4096]{1,0:T(8,128)(2,1)} %bitcast.12), custom_call_target="tpu_custom_call" | custom-call | bytes 11010048 | tf_op jit(solution)/shard_map/fetch1/pallas_call | solution.py:89
  20.9 0.0 collective-permute-done.4.b
  20.9 0.1 stream.1
  21.0 3.2 %collective-permute-start.7 = (bf16[32,1152]{1,0:T(8,128)(2,1)S(1)}, bf16[32,1152]{1,0:T(8,128)(2,1)S(1)}, u32[]{:S(2)}, u32[]{:S(2)}) collective-permute-start(bf16[32,1152]{1,0:T(8,128)(2,1)S(1)} %get-tuple-element.40.refs_0_), channel_id=1, source_target_pairs={{0,12},{4,8},{8,4},{12,0},{1,13},{5,9},{9,5},{13,1},{2,14},{6,10},... | collective-permute-start | bytes 221192 | tf_op jit(solution)/shard_map/ppermute | solution.py:30
  24.2 0.0 collective-permute-start.6
  24.2 1.3 %collective-permute-start.5 = (bf16[32,1152]{1,0:T(8,128)(2,1)S(1)}, bf16[32,1152]{1,0:T(8,128)(2,1)S(1)}, u32[]{:S(2)}, u32[]{:S(2)}) collective-permute-start(bf16[32,1152]{1,0:T(8,128)(2,1)S(1)} %get-tuple-element.40.refs_0_), channel_id=1, source_target_pairs={{0,4},{4,0},{8,12},{12,8},{1,5},{5,1},{9,13},{13,9},{2,6},{6,2},{1... | collective-permute-start | bytes 221192 | tf_op jit(solution)/shard_map/ppermute | solution.py:30
  25.5 4.6 %entry_own.1 = (f32[2496,32]{1,0:T(8,128)S(1)}, bf16[1536,4096]{1,0:T(8,128)(2,1)S(1)}) custom-call(bf16[32,1152]{1,0:T(8,128)(2,1)S(1)} %get-tuple-element.40.refs_0_, bf16[1152,4096]{1,0:T(8,128)(2,1)S(1)} %get-tuple-element.42.refs_1_.refs_6_, bf16[384,4096]{1,0:T(8,128)(2,1)S(1)} %get-tuple-element.43.refs_2_.refs_7_, ...), custom_call_target="tpu_custom_call" | custom-call | flops 163577856 | bytes 17694720 | tf_op jit(solution)/shard_map/entry_own/pallas_call | solution.py:89
  30.0 0.0 collective-permute-done.7.refs_3_
  30.1 0.3 collective-permute-done.6.refs_2_
  30.4 0.0 collective-permute-done.5.refs_1_
  30.4 3.0 %entry0.1 = (bf16[64,1536]{1,0:T(8,128)(2,1)S(1)}, bf16[4096,32]{1,0:T(8,128)(2,1)S(1)}, bf16[576,4096]{1,0:T(8,128)(2,1)S(1)}, bf16[192,4096]{1,0:T(8,128)(2,1)S(1)}) custom-call(bf16[32,1152]{1,0:T(8,128)(2,1)S(1)} %get-tuple-element.40.refs_0_, bf16[32,1152]{1,0:T(8,128)(2,1)S(1)} %collective-permute-done.5.refs_1_, ...), custom_call_target="tpu_custom_call" | custom-call | flops 402653184 | bytes 18874368 | tf_op jit(solution)/shard_map/entry0/pallas_call | solution.py:89
  33.3 3.4 %entry8.1 = (bf16[64,1536]{1,0:T(8,128)(2,1)S(1)}, bf16[576,4096]{1,0:T(8,128)(2,1)S(1)}, bf16[768,2048]{1,0:T(8,128)(2,1)S(1)}) custom-call(bf16[32,1152]{1,0:T(8,128)(2,1)S(1)} %get-tuple-element.40.refs_0_, bf16[32,1152]{1,0:T(8,128)(2,1)S(1)} %collective-permute-done.5.refs_1_, bf16[32,1152]{1,0:T(8,128)(2,1)S(1)} %collective-permute-done.6.refs_2_, ...), custom_call_target="tpu_custom_call" | custom-call | flops 402653184 | bytes 20447232 | tf_op jit(solution)/shard_map/entry8/pallas_call | solution.py:89
  36.7 2.4 %leave1.1 = (bf16[32,2048]{1,0:T(8,128)(2,1)S(1)}, bf16[768,2048]{1,0:T(8,128)(2,1)S(1)}) custom-call(bf16[64,1536]{1,0:T(8,128)(2,1)S(1)} %get-tuple-element.46.refs_0_, bf16[64,1536]{1,0:T(8,128)(2,1)S(1)} %get-tuple-element.49.refs_1_.refs_6_, bf16[1536,4096]{1,0:T(8,128)(2,1)S(1)} %get-tuple-element.50.refs_2_, ...), custom_call_target="tpu_custom_call" | custom-call | flops 805306368 | bytes 15728640 | tf_op jit(solution)/shard_map/leave1/pallas_call | solution.py:89
  39.1 1.4 %collective-permute-start.8 = (bf16[32,2048]{1,0:T(8,128)(2,1)S(1)}, bf16[32,2048]{1,0:T(8,128)(2,1)S(1)}, u32[]{:S(2)}, u32[]{:S(2)}) collective-permute-start(bf16[32,2048]{1,0:T(8,128)(2,1)S(1)} %get-tuple-element.55.refs_6_), channel_id=1, source_target_pairs={{0,2},{1,3},{2,0},{3,1},{4,6},{5,7},{6,4},{7,5},{8,10},{9,11},{10,... | collective-permute-start | bytes 393224 | tf_op jit(solution)/shard_map/ppermute | solution.py:30
  40.4 2.3 %leave0.1.mine = f32[32,2048]{1,0:T(8,128)S(1)} custom-call(bf16[64,1536]{1,0:T(8,128)(2,1)S(1)} %get-tuple-element.46.refs_0_, bf16[64,1536]{1,0:T(8,128)(2,1)S(1)} %get-tuple-element.49.refs_1_.refs_6_, bf16[1536,4096]{1,0:T(8,128)(2,1)S(1)} %get-tuple-element.50.refs_2_, bf16[192,4096]{1,0:T(8,128)(2,1)S(1)} %get-tuple-element.51.refs_3_, ...), custom_call_target="tpu_custom_call" | custom-call | flops 805306368 | bytes 12582912 | tf_op jit(solution)/shard_map/leave0/pallas_call | solution.py:89
  42.7 1.8 %collective-permute-done.8.received = bf16[32,2048]{1,0:T(8,128)(2,1)S(1)} collective-permute-done((bf16[32,2048]{1,0:T(8,128)(2,1)S(1)}, bf16[32,2048]{1,0:T(8,128)(2,1)S(1)}, u32[]{:S(2)}, u32[]{:S(2)}) %collective-permute-start.8) | collective-permute-done | bytes 131104 | tf_op jit(solution)/shard_map/ppermute | solution.py:30
  44.6 0.1 collective-permute-start.9
  44.6 1.3 %collective-permute-done.9.received = f32[32,1024]{1,0:T(8,128)S(1)} collective-permute-done((f32[32,1024]{1,0:T(8,128)S(1)}, f32[32,1024]{1,0:T(8,128)S(1)}, u32[]{:S(2)}, u32[]{:S(2)}) %collective-permute-start.9) | collective-permute-done | bytes 131104 | tf_op jit(solution)/shard_map/ppermute | solution.py:30
  46.0 2.5 %collective-permute-start.10 = (f32[8,1024]{1,0:T(8,128)S(1)}, f32[8,1024]{1,0:T(8,128)S(1)}, u32[]{:S(2)}, u32[]{:S(2)}) collective-permute-start(f32[8,1024]{1,0:T(8,128)S(1)} %get-tuple-element.60), channel_id=1, source_target_pairs={{0,12},{4,8},{8,4},{12,0},{1,13},{5,9},{9,5},{13,1},{2,14},{6,10},... | collective-permute-start | bytes 98312 | tf_op jit(solution)/shard_map/ppermute | solution.py:30
  48.5 0.0 collective-permute-start.11
  48.5 2.0 %collective-permute-start.12 = (f32[8,1024]{1,0:T(8,128)S(1)}, f32[8,1024]{1,0:T(8,128)S(1)}, u32[]{:S(2)}, u32[]{:S(2)}) collective-permute-start(f32[8,1024]{1,0:T(8,128)S(1)} %get-tuple-element.62), channel_id=1, source_target_pairs={{0,4},{4,0},{8,12},{12,8},{1,5},{5,1},{9,13},{13,9},{2,6},{6,2},{1... | collective-permute-start | bytes 98312 | tf_op jit(solution)/shard_map/ppermute | solution.py:30
  50.5 1.3 %collective-permute-done.10 = f32[8,1024]{1,0:T(8,128)S(1)} collective-permute-done((f32[8,1024]{1,0:T(8,128)S(1)}, f32[8,1024]{1,0:T(8,128)S(1)}, u32[]{:S(2)}, u32[]{:S(2)}) %collective-permute-start.10) | collective-permute-done | bytes 32800 | tf_op jit(solution)/shard_map/ppermute | solution.py:30
  51.8 1.5 %collective-permute-done.11 = f32[8,1024]{1,0:T(8,128)S(1)} collective-permute-done((f32[8,1024]{1,0:T(8,128)S(1)}, f32[8,1024]{1,0:T(8,128)S(1)}, u32[]{:S(2)}, u32[]{:S(2)}) %collective-permute-start.11) | collective-permute-done | bytes 32800 | tf_op jit(solution)/shard_map/ppermute | solution.py:30
  53.3 0.0 collective-permute-done.12
  53.3 0.6 %add_convert_fusion = bf16[8,1024]{1,0:T(8,128)(2,1)} fusion(f32[8,1024]{1,0:T(8,128)S(1)} %collective-permute-done.12, f32[8,1024]{1,0:T(8,128)S(1)} %collective-permute-done.11, f32[8,1024]{1,0:T(8,128)S(1)} %get-tuple-element.59, f32[8,1024]{1,0:T(8,128)S(1)} %collective-permute-done.10), kind=kLoop, calls=%fused_computation | loop fusion | flops 32768 | bytes 147456 | tf_op jit(solution)/shard_map/convert_element_type | solution.py:563
  (3 shorter events, 0.1 us)
Async XLA Ops:
  2.7 9.5 %collective-permute-start.2 = (bf16[8,3200]{1,0:T(8,128)(2,1)S(1)}, bf16[8,3200]{1,0:T(8,128)(2,1)S(1)}, u32[]{:S(2)}, u32[]{:S(2)}) collective-permute-start(bf16[8,3200]{1,0:T(8,128)(2,1)S(1)} %get-tuple-element.35.refs_0_.b0), channel_id=1, source_target_pairs={{0,12},{4,8},{8,4},{12,0},{1,13},{5,9},{9,5},{13,1},{2,14},{6,10},... | collective-permute-start | bytes 153608 | tf_op jit(solution)/shard_map/ppermute | solution.py:30
  7.8 5.0 %collective-permute-start.1 = (bf16[8,3200]{1,0:T(8,128)(2,1)S(1)}, bf16[8,3200]{1,0:T(8,128)(2,1)S(1)}, u32[]{:S(2)}, u32[]{:S(2)}) collective-permute-start(bf16[8,3200]{1,0:T(8,128)(2,1)S(1)} %get-tuple-element.35.refs_0_.b0), channel_id=1, source_target_pairs={{0,8},{4,12},{8,0},{12,4},{1,9},{5,13},{9,1},{13,5},{2,10},{6,14},... | collective-permute-start | bytes 153608 | tf_op jit(solution)/shard_map/ppermute | solution.py:30
  7.8 5.0 %collective-permute-start = (bf16[8,3200]{1,0:T(8,128)(2,1)S(1)}, bf16[8,3200]{1,0:T(8,128)(2,1)S(1)}, u32[]{:S(2)}, u32[]{:S(2)}) collective-permute-start(bf16[8,3200]{1,0:T(8,128)(2,1)S(1)} %get-tuple-element.35.refs_0_.b0), channel_id=1, source_target_pairs={{0,4},{4,0},{8,12},{12,8},{1,5},{5,1},{9,13},{13,9},{2,6},{6,2},{1... | collective-permute-start | bytes 153608 | tf_op jit(solution)/shard_map/ppermute | solution.py:30
  13.7 1.4 %collective-permute-start.3 = (f32[32,1024]{1,0:T(8,128)S(1)}, f32[32,1024]{1,0:T(8,128)S(1)}, u32[]{:S(2)}, u32[]{:S(2)}) collective-permute-start(f32[32,1024]{1,0:T(8,128)S(1)} %get-tuple-element.38.a), channel_id=1, source_target_pairs={{0,1},{1,0},{2,3},{3,2},{4,5},{5,4},{6,7},{7,6},{8,9},{9,8},{10,11... | collective-permute-start | bytes 393224 | tf_op jit(solution)/shard_map/ppermute | solution.py:30
  15.1 5.8 %collective-permute-start.4 = (f32[32,1024]{1,0:T(8,128)S(1)}, f32[32,1024]{1,0:T(8,128)S(1)}, u32[]{:S(2)}, u32[]{:S(2)}) collective-permute-start(f32[32,1024]{1,0:T(8,128)S(1)} %add.16.refs_0_.a), channel_id=1, source_target_pairs={{0,2},{1,3},{2,0},{3,1},{4,6},{5,7},{6,4},{7,5},{8,10},{9,11},{10,... | collective-permute-start | bytes 393224 | tf_op jit(solution)/shard_map/ppermute | solution.py:30
  21.0 9.0 %collective-permute-start.7 = (bf16[32,1152]{1,0:T(8,128)(2,1)S(1)}, bf16[32,1152]{1,0:T(8,128)(2,1)S(1)}, u32[]{:S(2)}, u32[]{:S(2)}) collective-permute-start(bf16[32,1152]{1,0:T(8,128)(2,1)S(1)} %get-tuple-element.40.refs_0_), channel_id=1, source_target_pairs={{0,12},{4,8},{8,4},{12,0},{1,13},{5,9},{9,5},{13,1},{2,14},{6,10},... | collective-permute-start | bytes 221192 | tf_op jit(solution)/shard_map/ppermute | solution.py:30
  24.2 6.2 %collective-permute-start.6 = (bf16[32,1152]{1,0:T(8,128)(2,1)S(1)}, bf16[32,1152]{1,0:T(8,128)(2,1)S(1)}, u32[]{:S(2)}, u32[]{:S(2)}) collective-permute-start(bf16[32,1152]{1,0:T(8,128)(2,1)S(1)} %get-tuple-element.40.refs_0_), channel_id=1, source_target_pairs={{0,8},{4,12},{8,0},{12,4},{1,9},{5,13},{9,1},{13,5},{2,10},{6,14},... | collective-permute-start | bytes 221192 | tf_op jit(solution)/shard_map/ppermute | solution.py:30
  24.2 6.2 %collective-permute-start.5 = (bf16[32,1152]{1,0:T(8,128)(2,1)S(1)}, bf16[32,1152]{1,0:T(8,128)(2,1)S(1)}, u32[]{:S(2)}, u32[]{:S(2)}) collective-permute-start(bf16[32,1152]{1,0:T(8,128)(2,1)S(1)} %get-tuple-element.40.refs_0_), channel_id=1, source_target_pairs={{0,4},{4,0},{8,12},{12,8},{1,5},{5,1},{9,13},{13,9},{2,6},{6,2},{1... | collective-permute-start | bytes 221192 | tf_op jit(solution)/shard_map/ppermute | solution.py:30
  39.1 5.5 %collective-permute-start.8 = (bf16[32,2048]{1,0:T(8,128)(2,1)S(1)}, bf16[32,2048]{1,0:T(8,128)(2,1)S(1)}, u32[]{:S(2)}, u32[]{:S(2)}) collective-permute-start(bf16[32,2048]{1,0:T(8,128)(2,1)S(1)} %get-tuple-element.55.refs_6_), channel_id=1, source_target_pairs={{0,2},{1,3},{2,0},{3,1},{4,6},{5,7},{6,4},{7,5},{8,10},{9,11},{10,... | collective-permute-start | bytes 393224 | tf_op jit(solution)/shard_map/ppermute | solution.py:30
  44.6 1.4 %collective-permute-start.9 = (f32[32,1024]{1,0:T(8,128)S(1)}, f32[32,1024]{1,0:T(8,128)S(1)}, u32[]{:S(2)}, u32[]{:S(2)}) collective-permute-start(f32[32,1024]{1,0:T(8,128)S(1)} %get-tuple-element.57), channel_id=1, source_target_pairs={{0,1},{1,0},{2,3},{3,2},{4,5},{5,4},{6,7},{7,6},{8,9},{9,8},{10,11... | collective-permute-start | bytes 393224 | tf_op jit(solution)/shard_map/ppermute | solution.py:30
  46.0 5.8 %collective-permute-start.10 = (f32[8,1024]{1,0:T(8,128)S(1)}, f32[8,1024]{1,0:T(8,128)S(1)}, u32[]{:S(2)}, u32[]{:S(2)}) collective-permute-start(f32[8,1024]{1,0:T(8,128)S(1)} %get-tuple-element.60), channel_id=1, source_target_pairs={{0,12},{4,8},{8,4},{12,0},{1,13},{5,9},{9,5},{13,1},{2,14},{6,10},... | collective-permute-start | bytes 98312 | tf_op jit(solution)/shard_map/ppermute | solution.py:30
  48.5 4.8 %collective-permute-start.11 = (f32[8,1024]{1,0:T(8,128)S(1)}, f32[8,1024]{1,0:T(8,128)S(1)}, u32[]{:S(2)}, u32[]{:S(2)}) collective-permute-start(f32[8,1024]{1,0:T(8,128)S(1)} %get-tuple-element.61), channel_id=1, source_target_pairs={{0,8},{4,12},{8,0},{12,4},{1,9},{5,13},{9,1},{13,5},{2,10},{6,14},... | collective-permute-start | bytes 98312 | tf_op jit(solution)/shard_map/ppermute | solution.py:30
  48.5 4.8 %collective-permute-start.12 = (f32[8,1024]{1,0:T(8,128)S(1)}, f32[8,1024]{1,0:T(8,128)S(1)}, u32[]{:S(2)}, u32[]{:S(2)}) collective-permute-start(f32[8,1024]{1,0:T(8,128)S(1)} %get-tuple-element.62), channel_id=1, source_target_pairs={{0,4},{4,0},{8,12},{12,8},{1,5},{5,1},{9,13},{13,9},{2,6},{6,2},{1... | collective-permute-start | bytes 98312 | tf_op jit(solution)/shard_map/ppermute | solution.py:30
